TPU v7x, 512 devices: a whole 4x8x8 slice. The times are simulated.
512 devices in a mesh: dp: 32 (over y, z_hi, core), image: 16 (over z_lo, x).
Axes of the slice: x: 4, y: 8, z: 8 (z_hi: 2, z_lo: 4; z = z_hi * 4 + z_lo), core: 2. Of those that a mesh axis runs over, the one named last changes fastest.
Arguments:
- queries: bfloat16 [64, 1024, 4096], P('dp', 'image'), may hold values from -6 to 6
- vision: bfloat16 [64, 16, 8, 8192], P('dp', 'image'), may hold values from -40 to 40
- cotangent: bfloat16 [64, 1024, 4096], P('dp', 'image'), may hold values from -16 to 16
- assignment: int32 [32, 2], P('dp'), may hold values from 0 to 1, each once within a row
- frame_counts: int32 [64], P('dp'), may hold values from 4 to 16, as said below
- lambdas: float32 [4, 16, 128], replicated, may hold values from -2.5 to 2.5
- norm_gain: float32 [256], replicated, may hold values from 0.1 to 1.9
- gate_logit: float32 [1], replicated, may hold values from 0.3 to 1.5
Outputs:
- grad_queries: bfloat16 [64, 1024, 4096], P('dp', 'image')
- grad_vision: bfloat16 [64, 16, 8, 8192], P('dp', 'image')
- grad_lambdas: float32 [4, 16, 128], replicated
- grad_gain: float32 [256], replicated
- grad_gate: float32 [1], replicated
Inputs may be any that keep to these rules, and one draw needn't show every extreme that they name: `assignment`: for each index of dp, its 2 sequences attend to its 2 videos, each video to exactly one sequence. A video's first frame_counts frames are used; some video uses all 16.
All inputs are finite; a program needn't handle non-finite values.
Results may differ from a plain program's by a relative error of at most 0.017.
Values may be sent and summed in bfloat16 or wider, within the bound.
No kernel may reach another device: no remote copies, remote signals or barrier semaphores. Data moves between devices by JAX's collectives and lax.ppermute only.
A program may use at most 64 MiB of HBM per device.

v0:
```python
import jax
import jax.numpy as jnp
from jax import lax
from jax.sharding import PartitionSpec as P

rate_offset = 0.8
epsilon = 1e-05


def rates_of(lambdas):
    first_exp = jnp.exp(jnp.sum(lambdas[0] * lambdas[1], axis=-1))
    second_exp = jnp.exp(jnp.sum(lambdas[2] * lambdas[3], axis=-1))
    return (first_exp - second_exp + rate_offset, first_exp, second_exp)


def forward(head_queries, key_rows, value_rows, counts, head_rates, patch_count):
    score_scale = head_queries.shape[-1] ** (-0.5)
    usable = (
        jnp.arange(key_rows.shape[1], dtype=jnp.int32)[None, :] // patch_count < counts[:, None]
    )
    scores = (
        jnp.einsum("slmhd,skmhd->smhlk", head_queries, key_rows, preferred_element_type=jnp.float32)
        * score_scale
    )
    scores = jnp.where(usable[:, None, None, None, :], scores, -jnp.inf)
    shifted = jnp.exp(scores - jnp.max(scores, axis=-1, keepdims=True))
    probability = shifted / jnp.sum(shifted, axis=-1, keepdims=True)
    mixed = (probability[:, 0] - head_rates[None, :, None, None] * probability[:, 1]).astype(
        jnp.bfloat16
    )
    attended = jnp.einsum("shlk,skhe->slhe", mixed, value_rows, preferred_element_type=jnp.float32)
    return (probability, mixed, attended)


def backward(
    grad_out,
    head_queries,
    key_rows,
    value_rows,
    probability,
    mixed,
    attended,
    head_rates,
    norm_gain,
    gate_tanh,
):
    score_scale = head_queries.shape[-1] ** (-0.5)
    inverse_rms = lax.rsqrt(jnp.mean(attended * attended, axis=-1, keepdims=True) + epsilon)
    normed = attended * inverse_rms
    output_scale = gate_tanh * (1.0 - rate_offset)
    grad_wide = grad_out.astype(jnp.float32)
    grad_gate = (
        jnp.sum(grad_wide * normed * norm_gain)
        * (1.0 - rate_offset)
        * (1.0 - gate_tanh * gate_tanh)
    )
    grad_gain = jnp.sum(grad_wide * normed, axis=(0, 1, 2)) * output_scale
    scaled_grad = grad_wide * output_scale * norm_gain
    grad_attended = inverse_rms * (
        scaled_grad - normed * jnp.mean(scaled_grad * normed, axis=-1, keepdims=True)
    )
    grad_attended = grad_attended.astype(jnp.bfloat16)
    grad_mixed = jnp.einsum(
        "slhe,skhe->shlk", grad_attended, value_rows, preferred_element_type=jnp.float32
    )
    grad_values = jnp.einsum(
        "shlk,slhe->skhe", mixed, grad_attended, preferred_element_type=jnp.float32
    )
    grad_rate = -jnp.sum(grad_mixed * probability[:, 1], axis=(0, 2, 3))
    grad_probs = jnp.stack([grad_mixed, -head_rates[None, :, None, None] * grad_mixed], axis=1)
    grad_scores = (
        probability
        * (grad_probs - jnp.sum(grad_probs * probability, axis=-1, keepdims=True))
        * score_scale
    )
    grad_scores = grad_scores.astype(jnp.bfloat16)
    grad_query = jnp.einsum(
        "smhlk,skmhd->slmhd", grad_scores, key_rows, preferred_element_type=jnp.float32
    )
    grad_key = jnp.einsum(
        "smhlk,slmhd->skmhd", grad_scores, head_queries, preferred_element_type=jnp.float32
    )
    return (grad_query, grad_key, grad_values, grad_rate, grad_gain, grad_gate)


def shards(queries, vision, cotangent, assignment, frame_counts, lambdas, norm_gain, gate_logit):
    image_count = lax.axis_size("image")
    seq_count, tok_count = (queries.shape[0], queries.shape[1])
    head_count, head_size = (lambdas.shape[1], lambdas.shape[2])
    local_heads = head_count // image_count
    frames_dev, patch_count = (vision.shape[1], vision.shape[2])
    query_split = queries.reshape(seq_count, tok_count, 2, head_count, head_size)
    grad_split = cotangent.reshape(seq_count, tok_count, 1, head_count, 2 * head_size)
    head_queries, head_grads = (
        lax.all_to_all(query_split, "image", split_axis=3, concat_axis=1, tiled=True),
        lax.all_to_all(grad_split, "image", split_axis=3, concat_axis=1, tiled=True),
    )
    key_maps = vision[..., : 2 * head_count * head_size].reshape(
        seq_count, frames_dev, patch_count, 2, head_count, head_size
    )
    value_maps = vision[..., 2 * head_count * head_size :].reshape(
        seq_count, frames_dev, patch_count, 1, head_count, 2 * head_size
    )
    head_keys, head_values = (
        lax.all_to_all(key_maps, "image", split_axis=4, concat_axis=1, tiled=True),
        lax.all_to_all(value_maps, "image", split_axis=4, concat_axis=1, tiled=True),
    )
    frames = head_keys.shape[1]
    video_order = assignment[0]
    key_rows = jnp.take(head_keys, video_order, axis=0).reshape(
        seq_count, frames * patch_count, 2, local_heads, head_size
    )
    value_rows = jnp.take(head_values, video_order, axis=0).reshape(
        seq_count, frames * patch_count, local_heads, 2 * head_size
    )
    counts = jnp.take(frame_counts, video_order)
    all_rates, first_exp, second_exp = rates_of(lambdas)
    head_start = lax.axis_index("image") * local_heads
    head_rates = lax.dynamic_slice_in_dim(all_rates, head_start, local_heads)
    gate_tanh = jnp.tanh(gate_logit[0])
    probability, mixed, attended = forward(
        head_queries, key_rows, value_rows, counts, head_rates, patch_count
    )
    full_length = head_grads.shape[1]
    grad_out = head_grads.reshape(seq_count, full_length, local_heads, 2 * head_size)
    grad_query, grad_key, grad_values, grad_rate, grad_gain, grad_gate = backward(
        grad_out,
        head_queries,
        key_rows,
        value_rows,
        probability,
        mixed,
        attended,
        head_rates,
        norm_gain,
        gate_tanh,
    )
    text_grads = lax.all_to_all(
        grad_query.astype(jnp.bfloat16), "image", split_axis=1, concat_axis=3, tiled=True
    )
    grad_queries = text_grads.reshape(seq_count, tok_count, 2 * head_count * head_size)
    matches = video_order[:, None] == jnp.arange(seq_count, dtype=jnp.int32)[None, :]
    inverse = jnp.sum(
        jnp.where(matches, jnp.arange(seq_count, dtype=jnp.int32)[:, None], 0), axis=0
    )
    key_back = jnp.take(grad_key.astype(jnp.bfloat16), inverse, axis=0).reshape(
        seq_count, frames, patch_count, 2, local_heads, head_size
    )
    value_back = jnp.take(grad_values.astype(jnp.bfloat16), inverse, axis=0).reshape(
        seq_count, frames, patch_count, 1, local_heads, 2 * head_size
    )
    frame_keys, frame_values = (
        lax.all_to_all(key_back, "image", split_axis=1, concat_axis=4, tiled=True),
        lax.all_to_all(value_back, "image", split_axis=1, concat_axis=4, tiled=True),
    )
    grad_vision = jnp.concatenate(
        [
            frame_keys.reshape(seq_count, frames_dev, patch_count, -1),
            frame_values.reshape(seq_count, frames_dev, patch_count, -1),
        ],
        axis=-1,
    )
    head_onehot = (
        jnp.arange(head_count, dtype=jnp.int32)[None, :]
        == head_start + jnp.arange(local_heads, dtype=jnp.int32)[:, None]
    )
    rate_full = jnp.sum(jnp.where(head_onehot, grad_rate[:, None], 0.0), axis=0)
    weight_one = (rate_full * first_exp)[:, None]
    weight_two = (rate_full * second_exp)[:, None]
    param_terms = jnp.stack(
        [
            weight_one * lambdas[1],
            weight_one * lambdas[0],
            -weight_two * lambdas[3],
            -weight_two * lambdas[2],
        ]
    )
    grad_lambdas, total_gain, total_gate = lax.psum(
        (param_terms, grad_gain, grad_gate), ("dp", "image")
    )
    return (grad_queries, grad_vision, grad_lambdas, total_gain, total_gate.reshape(1))


def solution(mesh):
    placed = (
        P("dp", "image", None),
        P("dp", "image", None, None),
        P("dp", "image", None),
        P("dp", None),
        P("dp"),
        P(),
        P(),
        P(),
    )
    return jax.shard_map(
        shards,
        mesh=mesh,
        in_specs=placed,
        out_specs=(P("dp", "image", None), P("dp", "image", None, None), P(), P(), P()),
        check_vma=False,
    )
```

profile of v0, /device:TPU:1, one launch (start us, length us, event | category | flops | bytes accessed | tf_op | source)
XLA Modules:
  0.0 255.0 jit_solution(10271723405887589601)
XLA Ops:
  2.5 10.4 %all-to-all-start.2 = ((bf16[2,1,8,1,16,256]{5,2,0,3,1,4:T(8,128)(2,1)}), bf16[2,1,8,1,16,256]{5,2,0,3,1,4:T(8,128)(2,1)S(1)}, u32[]{:S(2)}, u32[]{:S(2)}) async-start(bf16[2,1,8,1,16,256]{5,2,0,3,1,4:T(8,128)(2,1)} %copy.100), calls=%async_computation.2 | async-start | bytes 262144 | tf_op jit(solution)/shard_map/all_to_all | solution.py:106
  13.6 7.1 %all-to-all-done.2 = bf16[2,1,8,1,16,256]{5,2,0,3,1,4:T(8,128)(2,1)S(1)} async-done(((bf16[2,1,8,1,16,256]{5,2,0,3,1,4:T(8,128)(2,1)}), bf16[2,1,8,1,16,256]{5,2,0,3,1,4:T(8,128)(2,1)S(1)}, u32[]{:S(2)}, u32[]{:S(2)}) %all-to-all-start.2) | async-done | bytes 131104 | tf_op jit(solution)/shard_map/all_to_all | solution.py:106
  20.7 3.5 %all-to-all-start = ((bf16[2,1,8,2,16,128]{5,2,3,0,1,4:T(8,128)(2,1)}), bf16[2,1,8,2,16,128]{5,2,3,0,1,4:T(8,128)(2,1)S(1)}, u32[]{:S(2)}, u32[]{:S(2)}) async-start(bf16[2,1,8,2,16,128]{5,2,3,0,1,4:T(8,128)(2,1)} %copy.95), calls=%async_computation | async-start | bytes 262144 | tf_op jit(solution)/shard_map/all_to_all | solution.py:105
  24.5 1.4 copy.98
  25.9 6.1 %all-to-all-done = bf16[2,1,8,2,16,128]{5,2,3,0,1,4:T(8,128)(2,1)S(1)} async-done(((bf16[2,1,8,2,16,128]{5,2,3,0,1,4:T(8,128)(2,1)}), bf16[2,1,8,2,16,128]{5,2,3,0,1,4:T(8,128)(2,1)S(1)}, u32[]{:S(2)}, u32[]{:S(2)}) %all-to-all-start) | async-done | bytes 131104 | tf_op jit(solution)/shard_map/all_to_all | solution.py:105
  32.0 3.7 %all-to-all-start.1 = ((bf16[2,64,2,16,128]{4,1,2,0,3:T(8,128)(2,1)}), bf16[2,64,2,16,128]{4,1,2,0,3:T(8,128)(2,1)S(1)}, u32[]{:S(2)}, u32[]{:S(2)}) async-start(bf16[2,64,2,16,128]{4,1,2,0,3:T(8,128)(2,1)} %copy.98), calls=%async_computation.1 | async-start | bytes 2097152 | tf_op jit(solution)/shard_map/all_to_all | solution.py:95
  37.3 19.9 %all-to-all-done.1 = bf16[2,64,2,16,128]{4,1,2,0,3:T(8,128)(2,1)S(1)} async-done(((bf16[2,64,2,16,128]{4,1,2,0,3:T(8,128)(2,1)}), bf16[2,64,2,16,128]{4,1,2,0,3:T(8,128)(2,1)S(1)}, u32[]{:S(2)}, u32[]{:S(2)}) %all-to-all-start.1) | async-done | bytes 1048608 | tf_op jit(solution)/shard_map/all_to_all | solution.py:95
  57.2 7.7 %all-to-all-start.3 = ((bf16[2,64,1,16,256]{4,1,0,2,3:T(8,128)(2,1)}), bf16[2,64,1,16,256]{4,1,0,2,3:T(8,128)(2,1)S(1)}, u32[]{:S(2)}, u32[]{:S(2)}) async-start(bf16[2,64,1,16,256]{4,1,0,2,3:T(8,128)(2,1)} %copy.104), calls=%async_computation.3 | async-start | bytes 2097152 | tf_op jit(solution)/shard_map/all_to_all | solution.py:96
  69.1 17.8 %all-to-all-done.3 = bf16[2,64,1,16,256]{4,1,0,2,3:T(8,128)(2,1)S(1)} async-done(((bf16[2,64,1,16,256]{4,1,0,2,3:T(8,128)(2,1)}), bf16[2,64,1,16,256]{4,1,0,2,3:T(8,128)(2,1)S(1)}, u32[]{:S(2)}, u32[]{:S(2)}) %all-to-all-start.3) | async-done | bytes 1048608 | tf_op jit(solution)/shard_map/all_to_all | solution.py:96
  86.9 1.6 bitcast_convert_fusion
  88.5 1.9 copy.106
  90.5 2.4 fusion.15
  92.8 2.4 fusion.37
  95.9 1.9 multiply_reduce_fusion
  100.7 7.8 %all-to-all-start.6 = ((bf16[2,16,8,1,1,256]{5,2,0,4,3,1:T(8,128)(2,1)}), bf16[2,16,8,1,1,256]{5,2,0,4,3,1:T(8,128)(2,1)S(1)}, u32[]{:S(2)}, u32[]{:S(2)}) async-start(bf16[2,16,8,1,1,256]{5,2,0,4,3,1:T(8,128)(2,1)} %copy.117), calls=%async_computation.6 | async-start | bytes 262144 | tf_op jit(solution)/shard_map/all_to_all | solution.py:154
  108.5 2.2 multiply_reduce_fusion.2
  110.7 3.2 %fusion.31 = bf16[2,128,2,128]{3,1,2,0:T(8,128)(2,1)S(1)} fusion(bf16[2,1024,2,128]{3,1,2,0:T(8,128)(2,1)S(1)} %bitcast.210, f32[2,2,1024,128]{2,3,1,0:T(8,128)} %fusion.15, f32[2,1,1024,128]{2,3,1,0:T(8,128)S(1)} %get-tuple-element.26, f32[2,1,1024,128]{2,3,1,0:T(8,128)S(1)} %bitcast.200), kind=kOutput, calls=%fused_computation.36 | convolution fusion | flops 137957504 | bytes 5373952 | tf_op jit(solution)/shard_map/smhlk,slmhd->skmhd/dot_general | solution.py:80
  114.4 1.4 copy_select_fusion
  116.3 6.5 %all-to-all-start.5 = ((bf16[2,16,8,2,1,128]{5,2,3,0,4,1:T(8,128)(2,1)}), bf16[2,16,8,2,1,128]{5,2,3,0,4,1:T(8,128)(2,1)S(1)}, u32[]{:S(2)}, u32[]{:S(2)}) async-start(bf16[2,16,8,2,1,128]{5,2,3,0,4,1:T(8,128)(2,1)} %copy_select_fusion), calls=%async_computation.5 | async-start | bytes 262144 | tf_op jit(solution)/shard_map/all_to_all | solution.py:153
  122.8 3.2 %fusion.25 = bf16[2,1024,2,1,128]{1,4,2,0,3:T(8,128)(2,1)S(1)} fusion(f32[2,2,1024,128]{2,3,1,0:T(8,128)} %fusion.15, f32[2,1,1024,128]{2,3,1,0:T(8,128)S(1)} %get-tuple-element.26, f32[2,1,1024,128]{2,3,1,0:T(8,128)S(1)} %bitcast.201, bf16[2,16,8,2,128]{4,2,3,1,0:T(8,128)(2,1)S(1)} %gather_fusion, pred[2]{0:T(512)(128)(4,1)S(1)} %get-tuple-element.24), kind=kOutput, calls=%fused_computation.33 | convolution fusion | flops 138481792 | bytes 5373954 | tf_op jit(solution)/shard_map/smhlk,skmhd->slmhd/dot_general | solution.py:77
  126.0 2.0 copy.110
  128.0 2.5 all-to-all-done.5
  130.6 4.4 %all-to-all-start.4 = ((bf16[2,1024,2,1,128]{4,2,0,3,1:T(2,128)(2,1)}), bf16[2,1024,2,1,128]{4,2,0,3,1:T(2,128)(2,1)S(1)}, u32[]{:S(2)}, u32[]{:S(2)}) async-start(bf16[2,1024,2,1,128]{4,2,0,3,1:T(2,128)(2,1)} %copy.110), calls=%async_computation.4 | async-start | bytes 2097152 | tf_op jit(solution)/shard_map/all_to_all | solution.py:138
  136.4 115.6 %all-reduce = (f32[4,16,128]{2,1,0:T(8,128)}, f32[256]{0:T(256)}, f32[1]{0:T(128)}) all-reduce(f32[4,16,128]{2,1,0:T(8,128)S(1)} %pad_maximum_fusion.2, f32[256]{0:T(256)S(1)} %broadcast_multiply_fusion.1, f32[1]{0:T(128)} %bitcast.52), channel_id=1, replica_groups=mesh['dp'=32,'image'=16] {'dp','image'}, use_global_device_ids=true, to_apply=%region_9.10 | all-reduce | flops 8449 | bytes 67592 | tf_op jit(solution)/shard_map/psum | solution.py:178
  (74 shorter events, 14.8 us)
Async XLA Ops:
  0.6 66.4 %copy-start = (s32[2]{0:T(128)S(1)}, s32[2]{0:T(128)}, u32[]{:S(2)}) copy-start(s32[2]{0:T(128)} %param.12) | copy-start | bytes 28
  0.6 23.6 %copy-start.1 = (bf16[2,64,4096]{2,1,0:T(8,128)(2,1)S(1)}, bf16[2,64,4096]{2,1,0:T(8,128)(2,1)}, u32[]{:S(2)}) copy-start(bf16[2,64,4096]{2,1,0:T(8,128)(2,1)} %param.8) | copy-start | bytes 3145732
  2.5 18.2 %all-to-all-start.2 = ((bf16[2,1,8,1,16,256]{5,2,0,3,1,4:T(8,128)(2,1)}), bf16[2,1,8,1,16,256]{5,2,0,3,1,4:T(8,128)(2,1)S(1)}, u32[]{:S(2)}, u32[]{:S(2)}) async-start(bf16[2,1,8,1,16,256]{5,2,0,3,1,4:T(8,128)(2,1)} %copy.100), calls=%async_computation.2 | async-start | bytes 262144 | tf_op jit(solution)/shard_map/all_to_all | solution.py:106
  20.7 11.3 %all-to-all-start = ((bf16[2,1,8,2,16,128]{5,2,3,0,1,4:T(8,128)(2,1)}), bf16[2,1,8,2,16,128]{5,2,3,0,1,4:T(8,128)(2,1)S(1)}, u32[]{:S(2)}, u32[]{:S(2)}) async-start(bf16[2,1,8,2,16,128]{5,2,3,0,1,4:T(8,128)(2,1)} %copy.95), calls=%async_computation | async-start | bytes 262144 | tf_op jit(solution)/shard_map/all_to_all | solution.py:105
  24.5 11.2 %copy-start.2 = (bf16[2,64,4096]{2,1,0:T(8,128)(2,1)S(1)}, bf16[2,64,4096]{2,1,0:T(8,128)(2,1)}, u32[]{:S(2)}) copy-start(bf16[2,64,4096]{2,1,0:T(8,128)(2,1)} %param.10) | copy-start | bytes 3145732
  32.0 25.2 %all-to-all-start.1 = ((bf16[2,64,2,16,128]{4,1,2,0,3:T(8,128)(2,1)}), bf16[2,64,2,16,128]{4,1,2,0,3:T(8,128)(2,1)S(1)}, u32[]{:S(2)}, u32[]{:S(2)}) async-start(bf16[2,64,2,16,128]{4,1,2,0,3:T(8,128)(2,1)} %copy.98), calls=%async_computation.1 | async-start | bytes 2097152 | tf_op jit(solution)/shard_map/all_to_all | solution.py:95
  35.9 29.6 %copy-start.3 = (f32[4,16,128]{2,1,0:T(8,128)S(1)}, f32[4,16,128]{2,1,0:T(8,128)}, u32[]{:S(2)}) copy-start(f32[4,16,128]{2,1,0:T(8,128)} %param.13) | copy-start | bytes 98308
  35.9 31.1 %copy-start.11 = (s32[1,2]{1,0:T(1,128)S(1)}, s32[1,2]{1,0:T(1,128)}, u32[]{:S(2)}) copy-start(s32[1,2]{1,0:T(1,128)} %param.11) | copy-start | bytes 28
  57.2 29.7 %all-to-all-start.3 = ((bf16[2,64,1,16,256]{4,1,0,2,3:T(8,128)(2,1)}), bf16[2,64,1,16,256]{4,1,0,2,3:T(8,128)(2,1)S(1)}, u32[]{:S(2)}, u32[]{:S(2)}) async-start(bf16[2,64,1,16,256]{4,1,0,2,3:T(8,128)(2,1)} %copy.104), calls=%async_computation.3 | async-start | bytes 2097152 | tf_op jit(solution)/shard_map/all_to_all | solution.py:96
  65.7 1.3 copy-start.7
  65.7 1.3 copy-start.9
  67.8 32.1 %copy-start.6 = (pred[2]{0:T(512)(128)(4,1)}, pred[2]{0:T(512)(128)(4,1)S(1)}, u32[]{:S(2)}) copy-start(pred[2]{0:T(512)(128)(4,1)S(1)} %compare_and_fusion) | copy-start | bytes 10
  92.8 3.0 %copy-start.5 = (f32[256]{0:T(256)S(1)}, f32[256]{0:T(256)}, u32[]{:S(2)}) copy-start(f32[256]{0:T(256)} %param.14) | copy-start | bytes 3076
  100.7 15.6 %all-to-all-start.6 = ((bf16[2,16,8,1,1,256]{5,2,0,4,3,1:T(8,128)(2,1)}), bf16[2,16,8,1,1,256]{5,2,0,4,3,1:T(8,128)(2,1)S(1)}, u32[]{:S(2)}, u32[]{:S(2)}) async-start(bf16[2,16,8,1,1,256]{5,2,0,4,3,1:T(8,128)(2,1)} %copy.117), calls=%async_computation.6 | async-start | bytes 262144 | tf_op jit(solution)/shard_map/all_to_all | solution.py:154
  116.3 14.3 %all-to-all-start.5 = ((bf16[2,16,8,2,1,128]{5,2,3,0,4,1:T(8,128)(2,1)}), bf16[2,16,8,2,1,128]{5,2,3,0,4,1:T(8,128)(2,1)S(1)}, u32[]{:S(2)}, u32[]{:S(2)}) async-start(bf16[2,16,8,2,1,128]{5,2,3,0,4,1:T(8,128)(2,1)} %copy_select_fusion), calls=%async_computation.5 | async-start | bytes 262144 | tf_op jit(solution)/shard_map/all_to_all | solution.py:153
  126.0 10.3 %copy-start.8 = (f32[16]{0:T(128)S(1)}, f32[16]{0:T(128)}, u32[]{:S(2)}) copy-start(f32[16]{0:T(128)} %copy-done.7) | copy-start | bytes 196
  126.0 10.3 %copy-start.10 = (f32[16]{0:T(128)S(1)}, f32[16]{0:T(128)}, u32[]{:S(2)}) copy-start(f32[16]{0:T(128)} %copy-done.9) | copy-start | bytes 196
  126.0 10.3 %copy-start.4 = (f32[4,16,128]{2,1,0:T(8,128)S(1)}, f32[4,16,128]{2,1,0:T(8,128)}, u32[]{:S(2)}) copy-start(f32[4,16,128]{2,1,0:T(8,128)} %param.13) | copy-start | bytes 98308
  130.6 122.4 %all-to-all-start.4 = ((bf16[2,1024,2,1,128]{4,2,0,3,1:T(2,128)(2,1)}), bf16[2,1024,2,1,128]{4,2,0,3,1:T(2,128)(2,1)S(1)}, u32[]{:S(2)}, u32[]{:S(2)}) async-start(bf16[2,1024,2,1,128]{4,2,0,3,1:T(2,128)(2,1)} %copy.110), calls=%async_computation.4 | async-start | bytes 2097152 | tf_op jit(solution)/shard_map/all_to_all | solution.py:138
where the time goes:
time: 256 us; the launch traced here: 255 us
  blocking collectives  116 us (45%)
  waiting for transfers between devices  53.9 us (21%)
  starting transfers between devices  43.9 us (17%)
  local copies, waits for them, and re-layouts  16.5 us (6%)
  other arithmetic  11.4 us (4%)
  matrix products  10.1 us (4%)
  between operations  3.73 us (1%)
    psum x1, blocking collectives, shards(): lax.psum((param_terms, grad_gain, grad_gate), ('dp', 'image'))  116 us
    all_to_all x1, waiting for transfers between devices, shards(): lax.all_to_all(query_split, 'image', split_axis=3, concat_axis=1, tiled=T...  19.9 us
    all_to_all x1, waiting for transfers between devices, shards(): lax.all_to_all(grad_split, 'image', split_axis=3, concat_axis=1, tiled=True)  17.8 us
    all_to_all x1, starting transfers between devices, shards(): lax.all_to_all(value_maps, 'image', split_axis=4, concat_axis=1, tiled=True)  10.4 us
    all_to_all x1, starting transfers between devices, shards(): lax.all_to_all(value_back, 'image', split_axis=1, concat_axis=4, tiled=True)  7.77 us
    all_to_all x1, starting transfers between devices, shards(): lax.all_to_all(grad_split, 'image', split_axis=3, concat_axis=1, tiled=True)  7.67 us
    all_to_all x1, waiting for transfers between devices, shards(): lax.all_to_all(value_maps, 'image', split_axis=4, concat_axis=1, tiled=True)  7.1 us
    all_to_all x1, starting transfers between devices, shards(): lax.all_to_all(key_back, 'image', split_axis=1, concat_axis=4, tiled=True)  6.48 us
  transfers between devices with their start and end apart: 7, of which 6 were waited for; matrix products, arithmetic and copies ran while one was open for 8% of the time, Pallas kernels for 0%

commit v1 on v0

v1 whole, which is shorter than its diff:
```python
import functools

import jax
import jax.numpy as jnp
from jax import lax
from jax.experimental import pallas as pl
from jax.experimental.pallas import tpu as pltpu
from jax.sharding import Mesh, PartitionSpec as P

rate_offset = 0.8
epsilon = 1e-05
DP = ("y", "zh", "core")
IMAGE = ("zl", "x")
FIRST, SECOND = 32, 16
PARTS = 4
VMEM = pl.BlockSpec(memory_space=pltpu.VMEM)
SMEM = pl.BlockSpec(memory_space=pltpu.SMEM)
ANY = pl.BlockSpec(memory_space=pl.ANY)
LIMIT = pltpu.CompilerParams(vmem_limit_bytes=32 * 2**20)
f32, bf16 = jnp.float32, jnp.bfloat16


def dot(a, b, contract):
    return lax.dot_general(
        a, b, ((contract[:1], contract[1:]), ((), ())), preferred_element_type=f32
    )


def wrap(index):
    return lax.rem(index + PARTS, PARTS)


def pack_vision_body(vision, out):
    half = vision.shape[1] // 4
    width = half // PARTS
    for g in range(PARTS):
        out[g, :, :width] = vision[:, g * width : (g + 1) * width]
        out[g, :, width : 2 * width] = vision[:, half + g * width : half + (g + 1) * width]
        out[g, :, 2 * width :] = vision[
            :, 2 * half + 2 * g * width : 2 * half + 2 * (g + 1) * width
        ]


def pack_text_body(place, queries, cotangent, *refs):
    outs, sems = refs[:PARTS], refs[PARTS]
    half = queries.shape[2] // 2
    width = half // PARTS
    copies = []
    for shift in range(PARTS):
        g = wrap(place[1] + shift)
        first = pl.multiple_of(g * width, width)
        second = pl.multiple_of(half + g * width, width)
        wide = pl.multiple_of(g * 2 * width, 2 * width)
        pieces = (
            (queries.at[:, :, pl.ds(first, width)], pl.ds(0, width)),
            (queries.at[:, :, pl.ds(second, width)], pl.ds(width, width)),
            (cotangent.at[:, :, pl.ds(wide, 2 * width)], pl.ds(2 * width, 2 * width)),
        )
        for i, (source, columns) in enumerate(pieces):
            copies.append(
                pltpu.make_async_copy(source, outs[shift].at[:, :, columns], sems.at[shift, i])
            )
    for copy in copies:
        copy.start()
    for copy in copies:
        copy.wait()


def attend_body(
    place, assignment, counts, lambdas, norm_gain, gate, *refs, heads, head_size, patch
):
    text, vision, grad_text, grad_vision = (refs[i * PARTS : (i + 1) * PARTS] for i in range(4))
    stats = refs[4 * PARTS]
    zl, x = place[0], place[1]
    seqs, toks = text[0].shape[0], text[0].shape[1]
    frames = PARTS * PARTS
    keys = frames * patch
    width = heads * head_size
    scale = head_size ** (-0.5)
    output_scale = jnp.tanh(gate[...]) * (1.0 - rate_offset)
    gain_row = norm_gain[...] * output_scale
    first_exp = jnp.exp(jnp.sum(lambdas[0] * lambdas[1], axis=-1, keepdims=True))
    second_exp = jnp.exp(jnp.sum(lambdas[2] * lambdas[3], axis=-1, keepdims=True))
    all_rates = first_exp - second_exp + rate_offset
    head_index = lax.broadcasted_iota(jnp.int32, all_rates.shape, 0)
    spot = lax.broadcasted_iota(jnp.int32, (1, keys), 1) // patch
    part = spot // PARTS
    frame = wrap(zl - part) * PARTS + spot - part * PARTS
    raw_gain = jnp.zeros((1, 2 * head_size), f32)
    lane = lax.broadcasted_iota(jnp.int32, (1, head_size), 1)
    rate_row = jnp.zeros((1, head_size), f32)

    def block(columns):
        wide = jnp.concatenate([part[:, :, columns] for part in vision], axis=0)
        return wide.astype(f32).reshape(frames, seqs, patch, -1)

    def of_video(wide, v):
        return wide[:, v].reshape(keys, -1).astype(bf16)

    for h in range(heads):
        rate = jnp.sum(
            jnp.where(head_index == x * heads + h, all_rates, 0.0), axis=0, keepdims=True
        )
        map_columns = [pl.ds(m * width + h * head_size, head_size) for m in range(2)]
        value_columns = pl.ds(2 * width + 2 * h * head_size, 2 * head_size)
        wide_keys = [block(c) for c in map_columns]
        wide_values = block(value_columns)
        grad_keys, grad_values = ([[], []], [])
        total_rate = jnp.zeros((1, 1), f32)
        for v in range(seqs):
            s = jnp.where(assignment[0, 0] == v, 0, 1)
            usable = frame < counts[v]
            value_rows = of_video(wide_values, v)
            key_rows, query_rows, probs = [], [], []
            for m in range(2):
                k = of_video(wide_keys[m], v)
                q = jnp.concatenate([t[s, :, map_columns[m]] for t in text], axis=0)
                scores = dot(q, k, (1, 1)) * scale
                scores = jnp.where(usable, scores, -jnp.inf)
                shifted = jnp.exp(scores - jnp.max(scores, axis=-1, keepdims=True))
                probs.append(shifted / jnp.sum(shifted, axis=-1, keepdims=True))
                key_rows.append(k)
                query_rows.append(q)
            mixed = (probs[0] - rate * probs[1]).astype(bf16)
            attended = dot(mixed, value_rows, (1, 0))
            inverse_rms = lax.rsqrt(
                jnp.mean(attended * attended, axis=-1, keepdims=True) + epsilon
            )
            normed = attended * inverse_rms
            grad_out = jnp.concatenate([t[s, :, value_columns] for t in text], axis=0).astype(f32)
            raw_gain = raw_gain + jnp.sum(grad_out * normed, axis=0, keepdims=True)
            scaled = grad_out * gain_row
            grad_attended = (
                inverse_rms
                * (scaled - normed * jnp.mean(scaled * normed, axis=-1, keepdims=True))
            ).astype(bf16)
            grad_mixed = dot(grad_attended, value_rows, (1, 1))
            grad_values.append(dot(mixed, grad_attended, (0, 0)).reshape(frames, patch, -1))
            sums = [jnp.sum(grad_mixed * p, axis=-1, keepdims=True) for p in probs]
            total_rate = total_rate - jnp.sum(sums[1], axis=0, keepdims=True)
            factors = (scale, -rate * scale)
            for m in range(2):
                grad_scores = (probs[m] * (grad_mixed - sums[m]) * factors[m]).astype(bf16)
                grad_query = dot(grad_scores, key_rows[m], (1, 0)).astype(bf16)
                for i in range(PARTS):
                    grad_text[i][s, :, map_columns[m]] = grad_query[i * toks : (i + 1) * toks]
                grad_key = dot(grad_scores, query_rows[m], (0, 0))
                grad_keys[m].append(grad_key.reshape(frames, patch, -1))
        for columns, parts in (
            (map_columns[0], grad_keys[0]),
            (map_columns[1], grad_keys[1]),
            (value_columns, grad_values),
        ):
            joined = jnp.concatenate(parts, axis=1).astype(bf16)
            for j in range(PARTS):
                grad_vision[j][:, :, columns] = joined[j * PARTS : (j + 1) * PARTS]
        rate_row = jnp.where(lane == x * heads + h, total_rate, rate_row)
    row = lax.broadcasted_iota(jnp.int32, stats.shape[1:], 0)
    tile = jnp.where(row == 0, raw_gain[:, :head_size], 0.0)
    tile = jnp.where(row == 1, raw_gain[:, head_size:], tile)
    tile = jnp.where(row == 2, rate_row, tile)
    for i in range(stats.shape[0]):
        stats[i] = tile


def sum_parts(refs):
    total = refs[0][...].astype(f32)
    for part in refs[1:]:
        total = total + part[...].astype(f32)
    return total


def sum_vision_body(*refs):
    refs[PARTS][...] = sum_parts(refs[:PARTS]).astype(bf16)


def spread_sum_body(tiles, out):
    total = jnp.sum(tiles[...], axis=0)
    for i in range(out.shape[0]):
        out[i] = total


def finish_body(tiles, lambdas, norm_gain, gate, grad_lambdas, grad_gain, grad_gate):
    total = jnp.sum(tiles[...], axis=0)
    head_count, head_size = lambdas.shape[1:]
    gate_tanh = jnp.tanh(gate[...])
    grad_gain[...] = total[:2] * (gate_tanh * (1.0 - rate_offset))
    weighed = jnp.sum(total[:2] * norm_gain[...], axis=-1, keepdims=True)
    grad_gate[...] = (
        jnp.sum(weighed, axis=0, keepdims=True)
        * (1.0 - rate_offset)
        * (1.0 - gate_tanh * gate_tanh)
    )
    shape = (head_count, head_size)
    own = lax.broadcasted_iota(jnp.int32, shape, 0) == lax.broadcasted_iota(jnp.int32, shape, 1)
    grad_rate = jnp.sum(jnp.where(own, total[2:3], 0.0), axis=-1, keepdims=True)
    first_exp = jnp.exp(jnp.sum(lambdas[0] * lambdas[1], axis=-1, keepdims=True))
    second_exp = jnp.exp(jnp.sum(lambdas[2] * lambdas[3], axis=-1, keepdims=True))
    weight_one, weight_two = grad_rate * first_exp, grad_rate * second_exp
    grad_lambdas[0] = weight_one * lambdas[1]
    grad_lambdas[1] = weight_one * lambdas[0]
    grad_lambdas[2] = -weight_two * lambdas[3]
    grad_lambdas[3] = -weight_two * lambdas[2]


def unpack_vision_body(received, out):
    half = out.shape[1] // 4
    width = half // PARTS
    for g in range(PARTS):
        out[:, g * width : (g + 1) * width] = received[g, :, :width]
        out[:, half + g * width : half + (g + 1) * width] = received[g, :, width : 2 * width]
        out[:, 2 * half + 2 * g * width : 2 * half + 2 * (g + 1) * width] = received[
            g, :, 2 * width :
        ]


def unpack_text_body(place, *refs):
    parts, out, sems = refs[:PARTS], refs[PARTS], refs[PARTS + 1]
    half = out.shape[2] // 2
    width = half // PARTS
    copies = []
    for shift in range(PARTS):
        g = wrap(place[1] + shift)
        for m in range(2):
            columns = pl.ds(pl.multiple_of(m * half + g * width, width), width)
            copies.append(
                pltpu.make_async_copy(
                    parts[shift].at[:, :, pl.ds(m * width, width)],
                    out.at[:, :, columns],
                    sems.at[shift, m],
                )
            )
    for copy in copies:
        copy.start()
    for copy in copies:
        copy.wait()


def along(shift):
    return [(i, (i + shift) % PARTS) for i in range(PARTS)]


def kernel(body, out_shape, in_specs, out_specs, **more):
    return pl.pallas_call(
        body,
        out_shape=out_shape,
        in_specs=in_specs,
        out_specs=out_specs,
        compiler_params=LIMIT,
        **more,
    )


def shaped(shape, dtype=bf16):
    return jax.ShapeDtypeStruct(shape, dtype)


def exchange(value, axes):
    return lax.all_to_all(value, axes, 0, 0, tiled=True)


def shards(queries, vision, cotangent, assignment, frame_counts, lambdas, norm_gain, gate_logit):
    seqs, toks, text_columns = queries.shape
    frames_dev, patch, vision_columns = vision.shape[1:]
    head_count, head_size = lambdas.shape[1:]
    heads = head_count // PARTS
    rows = seqs * frames_dev * patch
    place = jnp.stack([lax.axis_index("zl"), lax.axis_index("x")]).astype(jnp.int32)
    slab = shaped((PARTS, rows, vision_columns // PARTS))
    gain_rows = norm_gain.reshape(-1, head_size)
    gate = gate_logit.reshape(1, 1)

    sent_vision = kernel(pack_vision_body, slab, [VMEM], VMEM)(
        vision.reshape(rows, vision_columns)
    )
    row_vision = exchange(sent_vision, "x")
    sent_text = kernel(
        pack_text_body,
        [shaped((seqs, toks, 2 * text_columns // PARTS))] * PARTS,
        [SMEM, ANY, ANY],
        [ANY] * PARTS,
        scratch_shapes=[pltpu.SemaphoreType.DMA((PARTS, 3))],
    )(place, queries, cotangent)
    held_text = [sent_text[0]] + [
        lax.ppermute(sent_text[k], "x", along(k)) for k in range(1, PARTS)
    ]
    held_vision = [row_vision] + [
        lax.ppermute(row_vision, "zl", along(k)) for k in range(1, PARTS)
    ]

    grads = kernel(
        functools.partial(attend_body, heads=heads, head_size=head_size, patch=patch),
        [shaped((seqs, toks, text_columns // PARTS))] * PARTS
        + [slab] * PARTS
        + [shaped((FIRST, 4, head_size), f32)],
        [SMEM] * 3 + [VMEM] * (3 + 2 * PARTS),
        [VMEM] * (2 * PARTS + 1),
    )(
        place,
        assignment,
        frame_counts,
        lambdas,
        norm_gain.reshape(1, -1),
        gate,
        *held_text,
        *held_vision,
    )
    grad_text, grad_vision, stats = grads[:PARTS], grads[PARTS : 2 * PARTS], grads[2 * PARTS]

    stats = exchange(stats, ("y", "x"))
    back_vision = [grad_vision[0]] + [
        lax.ppermute(grad_vision[k], "zl", along(-k)) for k in range(1, PARTS)
    ]
    stats = kernel(spread_sum_body, shaped((SECOND, 4, head_size), f32), [VMEM], VMEM)(stats)
    stats = exchange(stats, ("zh", "core", "zl"))
    back_text = [grad_text[0]] + [
        lax.ppermute(grad_text[k], "x", along(-k)) for k in range(1, PARTS)
    ]
    row_vision = kernel(sum_vision_body, slab, [VMEM] * PARTS, VMEM)(*back_vision)
    row_vision = exchange(row_vision, "x")

    grad_queries = kernel(
        unpack_text_body,
        shaped(queries.shape),
        [SMEM] + [ANY] * PARTS,
        ANY,
        scratch_shapes=[pltpu.SemaphoreType.DMA((PARTS, 2))],
    )(place, *back_text)
    grad_lambdas, grad_gain, grad_gate = kernel(
        finish_body,
        [shaped(lambdas.shape, f32), shaped(gain_rows.shape, f32), shaped((1, 1), f32)],
        [VMEM] * 4,
        [VMEM] * 3,
    )(stats, lambdas, gain_rows, gate)
    grad_vision = kernel(unpack_vision_body, shaped((rows, vision_columns)), [VMEM], VMEM)(
        row_vision
    )
    return (
        grad_queries,
        grad_vision.reshape(vision.shape),
        grad_lambdas,
        grad_gain.reshape(norm_gain.shape),
        grad_gate.reshape(gate_logit.shape),
    )


def solution(mesh):
    fine = Mesh(mesh.devices.reshape(8, 2, 2, PARTS, PARTS), DP + IMAGE)
    placed = (
        P(DP, IMAGE, None),
        P(DP, IMAGE, None, None),
        P(DP, IMAGE, None),
        P(DP, None),
        P(DP),
        P(),
        P(),
        P(),
    )
    return jax.shard_map(
        shards,
        mesh=fine,
        in_specs=placed,
        out_specs=(P(DP, IMAGE, None), P(DP, IMAGE, None, None), P(), P(), P()),
        check_vma=False,
    )
```

time: 256 us -> 114 us (0.45)
  blocking collectives: 116 us -> 0 us
  waiting for transfers between devices: 53.9 us -> 24.1 us
  starting transfers between devices: 43.9 us -> 68.8 us
  Pallas kernels: 0 us -> 15.6 us
  local copies, waits for them, and re-layouts: 16.5 us -> 2.94 us
  other arithmetic: 11.4 us -> 0.07 us
  matrix products: 10.1 us -> 0 us
    psum x1 -> x0, blocking collectives: 116 us -> none  [shards(): lax.psum((param_terms, grad_gain, grad_gate), ('dp', 'image'))]
    all_to_all x7 -> x4, waiting for transfers between devices: 53.9 us -> 9.95 us  [exchange(): return lax.all_to_all(value, axes, 0, 0, tiled=True)]
    ppermute x0 -> x12, starting transfers between devices: none -> 40.6 us  [the longest x3 11.7 us: shards(): lax.ppermute(row_vision, 'zl', along(k))]
    all_to_all x7 -> x4, starting transfers between devices: 43.9 us -> 28.2 us  [exchange(): return lax.all_to_all(value, axes, 0, 0, tiled=True)]
    pallas_call x0 -> x8, Pallas kernels: none -> 15.6 us  [the longest x1 9.44 us: shards(): kernel(functools.partial(attend_body, heads=heads, head_size=head_size, p...]
    ppermute x0 -> x12, waiting for transfers between devices: none -> 14.1 us  [the longest x3 12.8 us: shards(): lax.ppermute(row_vision, 'zl', along(k))]
    dot_general x5 -> x0, matrix products: 7.69 us -> none  [the longest x1 3.19 us: backward(): jnp.einsum('smhlk,skmhd->slmhd', grad_scores, key_rows, preferred_element...]
    reshape x7 -> x0, local copies, waits for them, and re-layouts: 5.53 us -> none  [the longest x1 1.38 us: shards(): queries.reshape(seq_count, tok_count, 2, head_count, head_size)]
  transfers between devices with their start and end apart: 7 -> 16, of which waited for: 6 -> 4; matrix products, arithmetic and copies ran while one was open for 8% -> 0% of each run, Pallas kernels for 0% -> 4%
where the time goes in v1:
time: 114 us; the launch traced here: 113 us
  starting transfers between devices  68.8 us (60%)
  waiting for transfers between devices  24.1 us (21%)
  Pallas kernels  15.6 us (14%)
  local copies, waits for them, and re-layouts  2.94 us (3%)
  between operations  1.49 us (1%)
    all_to_all x4, starting transfers between devices, exchange(): return lax.all_to_all(value, axes, 0, 0, tiled=True)  28.2 us
    ppermute x3, waiting for transfers between devices, shards(): lax.ppermute(row_vision, 'zl', along(k))  12.8 us
    ppermute x3, starting transfers between devices, shards(): lax.ppermute(row_vision, 'zl', along(k))  11.7 us
    ppermute x3, starting transfers between devices, shards(): lax.ppermute(sent_text[k], 'x', along(k))  10.8 us
    all_to_all x4, waiting for transfers between devices, exchange(): return lax.all_to_all(value, axes, 0, 0, tiled=True)  9.95 us
    pallas_call x1, Pallas kernels, shards(): kernel(functools.partial(attend_body, heads=heads, head_size=head_size, p...  9.44 us
    ppermute x3, starting transfers between devices, shards(): lax.ppermute(grad_text[k], 'x', along(-k))  9.32 us
    ppermute x3, starting transfers between devices, shards(): lax.ppermute(grad_vision[k], 'zl', along(-k))  8.76 us
  transfers between devices with their start and end apart: 16, of which 4 were waited for; matrix products, arithmetic and copies ran while one was open for 0% of the time, Pallas kernels for 4%

profile of v1, /device:TPU:1, one launch (start us, length us, event | category | flops | bytes accessed | tf_op | source)
XLA Modules:
  0.0 113.0 jit_solution(2844070162515527371)
XLA Ops:
  0.7 1.0 copy-done.2
  2.4 4.8 %all-to-all-start = ((bf16[4,16,2048]{2,1,0:T(8,128)(2,1)}), bf16[4,16,2048]{2,1,0:T(8,128)(2,1)S(1)}, u32[]{:S(2)}, u32[]{:S(2)}) async-start(bf16[4,16,2048]{2,1,0:T(8,128)(2,1)} %shard_map.120), calls=%async_computation | async-start | bytes 524288 | tf_op jit(solution)/shard_map/all_to_all | solution.py:259
  7.3 1.2 %copy-done.1 = bf16[2,64,4096]{2,1,0:T(8,128)(2,1)S(1)} copy-done((bf16[2,64,4096]{2,1,0:T(8,128)(2,1)S(1)}, bf16[2,64,4096]{2,1,0:T(8,128)(2,1)}, u32[]{:S(2)}) %copy-start.1) | copy-done | bytes 1048600
  9.5 3.4 %collective-permute-start = (bf16[2,64,2048]{2,1,0:T(8,128)(2,1)S(1)}, bf16[2,64,2048]{2,1,0:T(8,128)(2,1)S(1)}, u32[]{:S(2)}, u32[]{:S(2)}) collective-permute-start(bf16[2,64,2048]{2,1,0:T(8,128)(2,1)S(1)} %get-tuple-element.22), channel_id=1, source_target_pairs={{0,1},{1,2},{2,3},{3,0},{4,5},{5,6},{6,7},{7,4},{8,9},{9,10},{10,1... | collective-permute-start | bytes 1572872 | tf_op jit(solution)/shard_map/ppermute | solution.py:285
  12.9 7.6 %collective-permute-start.5 = (bf16[4,16,2048]{2,1,0:T(8,128)(2,1)S(1)}, bf16[4,16,2048]{2,1,0:T(8,128)(2,1)S(1)}, u32[]{:S(2)}, u32[]{:S(2)}) collective-permute-start(bf16[4,16,2048]{2,1,0:T(8,128)(2,1)S(1)} %all-to-all-done.refs_4_), channel_id=1, source_target_pairs={{0,12},{4,0},{8,4},{12,8},{1,13},{5,1},{9,5},{13,9},{2,14},{6,2},{... | collective-permute-start | bytes 786440 | tf_op jit(solution)/shard_map/ppermute | solution.py:288
  20.5 4.3 %collective-permute-start.1 = (bf16[2,64,2048]{2,1,0:T(8,128)(2,1)S(1)}, bf16[2,64,2048]{2,1,0:T(8,128)(2,1)S(1)}, u32[]{:S(2)}, u32[]{:S(2)}) collective-permute-start(bf16[2,64,2048]{2,1,0:T(8,128)(2,1)S(1)} %get-tuple-element.23), channel_id=1, source_target_pairs={{0,2},{1,3},{2,0},{3,1},{4,6},{5,7},{6,4},{7,5},{8,10},{9,11},{10,... | collective-permute-start | bytes 1572872 | tf_op jit(solution)/shard_map/ppermute | solution.py:285
  24.8 3.1 %collective-permute-start.2 = (bf16[2,64,2048]{2,1,0:T(8,128)(2,1)S(1)}, bf16[2,64,2048]{2,1,0:T(8,128)(2,1)S(1)}, u32[]{:S(2)}, u32[]{:S(2)}) collective-permute-start(bf16[2,64,2048]{2,1,0:T(8,128)(2,1)S(1)} %get-tuple-element.24), channel_id=1, source_target_pairs={{0,3},{1,0},{2,1},{3,2},{4,7},{5,4},{6,5},{7,6},{8,11},{9,8},{10,9... | collective-permute-start | bytes 1572872 | tf_op jit(solution)/shard_map/ppermute | solution.py:285
  27.9 1.9 %collective-permute-start.4 = (bf16[4,16,2048]{2,1,0:T(8,128)(2,1)S(1)}, bf16[4,16,2048]{2,1,0:T(8,128)(2,1)S(1)}, u32[]{:S(2)}, u32[]{:S(2)}) collective-permute-start(bf16[4,16,2048]{2,1,0:T(8,128)(2,1)S(1)} %all-to-all-done.refs_4_), channel_id=1, source_target_pairs={{0,8},{4,12},{8,0},{12,4},{1,9},{5,13},{9,1},{13,5},{2,10},{6,14},... | collective-permute-start | bytes 786440 | tf_op jit(solution)/shard_map/ppermute | solution.py:288
  29.8 2.2 %collective-permute-start.3 = (bf16[4,16,2048]{2,1,0:T(8,128)(2,1)S(1)}, bf16[4,16,2048]{2,1,0:T(8,128)(2,1)S(1)}, u32[]{:S(2)}, u32[]{:S(2)}) collective-permute-start(bf16[4,16,2048]{2,1,0:T(8,128)(2,1)S(1)} %all-to-all-done.refs_4_), channel_id=1, source_target_pairs={{0,4},{4,8},{8,12},{12,0},{1,5},{5,9},{9,13},{13,1},{2,6},{6,10},{... | collective-permute-start | bytes 786440 | tf_op jit(solution)/shard_map/ppermute | solution.py:288
  32.7 12.8 %collective-permute-done.4.refs_6_ = bf16[4,16,2048]{2,1,0:T(8,128)(2,1)S(1)} collective-permute-done((bf16[4,16,2048]{2,1,0:T(8,128)(2,1)S(1)}, bf16[4,16,2048]{2,1,0:T(8,128)(2,1)S(1)}, u32[]{:S(2)}, u32[]{:S(2)}) %collective-permute-start.4) | collective-permute-done | bytes 262176 | tf_op jit(solution)/shard_map/ppermute | solution.py:288
  45.5 1.3 %collective-permute-done.2.refs_3_ = bf16[2,64,2048]{2,1,0:T(8,128)(2,1)S(1)} collective-permute-done((bf16[2,64,2048]{2,1,0:T(8,128)(2,1)S(1)}, bf16[2,64,2048]{2,1,0:T(8,128)(2,1)S(1)}, u32[]{:S(2)}, u32[]{:S(2)}) %collective-permute-start.2) | collective-permute-done | bytes 524320 | tf_op jit(solution)/shard_map/ppermute | solution.py:285
  47.5 9.4 %shard_map.121 = (bf16[2,64,1024]{2,1,0:T(8,128)(2,1)S(1)}, bf16[2,64,1024]{2,1,0:T(8,128)(2,1)S(1)}, bf16[2,64,1024]{2,1,0:T(8,128)(2,1)S(1)}, bf16[2,64,1024]{...) custom-call(s32[2]{0:T(128)S(1)} %pad_add_fusion.place, ...), custom_call_target="tpu_custom_call" | custom-call | tf_op jit(solution)/shard_map/pallas_call | solution.py:291
  56.9 1.9 %collective-permute-start.9 = (bf16[4,16,2048]{2,1,0:T(8,128)(2,1)}, bf16[4,16,2048]{2,1,0:T(8,128)(2,1)S(1)}, u32[]{:S(2)}, u32[]{:S(2)}) collective-permute-start(bf16[4,16,2048]{2,1,0:T(8,128)(2,1)} %get-tuple-element.30), channel_id=1, source_target_pairs={{0,12},{4,0},{8,4},{12,8},{1,13},{5,1},{9,5},{13,9},{2,14},{6,2},{... | collective-permute-start | bytes 786440 | tf_op jit(solution)/shard_map/ppermute | solution.py:312
  58.8 3.5 %collective-permute-start.10 = (bf16[4,16,2048]{2,1,0:T(8,128)(2,1)}, bf16[4,16,2048]{2,1,0:T(8,128)(2,1)S(1)}, u32[]{:S(2)}, u32[]{:S(2)}) collective-permute-start(bf16[4,16,2048]{2,1,0:T(8,128)(2,1)} %get-tuple-element.31), channel_id=1, source_target_pairs={{0,8},{4,12},{8,0},{12,4},{1,9},{5,13},{9,1},{13,5},{2,10},{6,14},... | collective-permute-start | bytes 786440 | tf_op jit(solution)/shard_map/ppermute | solution.py:312
  62.3 3.4 %collective-permute-start.11 = (bf16[4,16,2048]{2,1,0:T(8,128)(2,1)S(1)}, bf16[4,16,2048]{2,1,0:T(8,128)(2,1)S(1)}, u32[]{:S(2)}, u32[]{:S(2)}) collective-permute-start(bf16[4,16,2048]{2,1,0:T(8,128)(2,1)S(1)} %get-tuple-element.32), channel_id=1, source_target_pairs={{0,4},{4,8},{8,12},{12,0},{1,5},{5,9},{9,13},{13,1},{2,6},{6,10},{... | collective-permute-start | bytes 786440 | tf_op jit(solution)/shard_map/ppermute | solution.py:312
  65.7 8.8 %all-to-all-start.2 = ((f32[32,4,128]{2,1,0:T(4,128)}), f32[32,4,128]{2,1,0:T(4,128)S(1)}, u32[]{:S(2)}, u32[]{:S(2)}) async-start(f32[32,4,128]{2,1,0:T(4,128)} %get-tuple-element.33), calls=%async_computation.2 | async-start | bytes 131072 | tf_op jit(solution)/shard_map/all_to_all | solution.py:259
  74.5 4.3 %collective-permute-start.6 = (bf16[2,64,1024]{2,1,0:T(8,128)(2,1)S(1)}, bf16[2,64,1024]{2,1,0:T(8,128)(2,1)S(1)}, u32[]{:S(2)}, u32[]{:S(2)}) collective-permute-start(bf16[2,64,1024]{2,1,0:T(8,128)(2,1)S(1)} %get-tuple-element.26), channel_id=1, source_target_pairs={{0,3},{1,0},{2,1},{3,2},{4,7},{5,4},{6,5},{7,6},{8,11},{9,8},{10,9... | collective-permute-start | bytes 786440 | tf_op jit(solution)/shard_map/ppermute | solution.py:317
  78.8 2.5 %collective-permute-start.7 = (bf16[2,64,1024]{2,1,0:T(8,128)(2,1)S(1)}, bf16[2,64,1024]{2,1,0:T(8,128)(2,1)S(1)}, u32[]{:S(2)}, u32[]{:S(2)}) collective-permute-start(bf16[2,64,1024]{2,1,0:T(8,128)(2,1)S(1)} %get-tuple-element.27), channel_id=1, source_target_pairs={{0,2},{1,3},{2,0},{3,1},{4,6},{5,7},{6,4},{7,5},{8,10},{9,11},{10,... | collective-permute-start | bytes 786440 | tf_op jit(solution)/shard_map/ppermute | solution.py:317
  81.3 2.5 %collective-permute-start.8 = (bf16[2,64,1024]{2,1,0:T(8,128)(2,1)S(1)}, bf16[2,64,1024]{2,1,0:T(8,128)(2,1)S(1)}, u32[]{:S(2)}, u32[]{:S(2)}) collective-permute-start(bf16[2,64,1024]{2,1,0:T(8,128)(2,1)S(1)} %get-tuple-element.28), channel_id=1, source_target_pairs={{0,1},{1,2},{2,3},{3,0},{4,5},{5,6},{6,7},{7,4},{8,9},{9,10},{10,1... | collective-permute-start | bytes 786440 | tf_op jit(solution)/shard_map/ppermute | solution.py:317
  84.5 11.2 %all-to-all-start.3 = ((f32[16,4,128]{2,1,0:T(4,128)}), f32[16,4,128]{2,1,0:T(4,128)S(1)}, u32[]{:S(2)}, u32[]{:S(2)}) async-start(f32[16,4,128]{2,1,0:T(4,128)} %shard_map.125), calls=%async_computation.3 | async-start | bytes 65536 | tf_op jit(solution)/shard_map/all_to_all | solution.py:259
  96.6 6.5 %all-to-all-done.3.tiles = f32[16,4,128]{2,1,0:T(4,128)S(1)} async-done(((f32[16,4,128]{2,1,0:T(4,128)}), f32[16,4,128]{2,1,0:T(4,128)S(1)}, u32[]{:S(2)}, u32[]{:S(2)}) %all-to-all-start.3) | async-done | bytes 32800 | tf_op jit(solution)/shard_map/all_to_all | solution.py:259
  103.1 3.4 %all-to-all-start.1 = ((bf16[4,16,2048]{2,1,0:T(8,128)(2,1)}), bf16[4,16,2048]{2,1,0:T(8,128)(2,1)S(1)}, u32[]{:S(2)}, u32[]{:S(2)}) async-start(bf16[4,16,2048]{2,1,0:T(8,128)(2,1)} %shard_map.123), calls=%async_computation.1 | async-start | bytes 524288 | tf_op jit(solution)/shard_map/all_to_all | solution.py:259
  107.3 1.6 %shard_map.122 = bf16[2,64,4096]{2,1,0:T(8,128)(2,1)} custom-call(s32[2]{0:T(128)S(1)} %pad_add_fusion.place, bf16[2,64,1024]{2,1,0:T(8,128)(2,1)S(1)} %get-tuple-element.25.refs_0_, bf16[2,64,1024]{2,1,0:T(8,128)(2,1)S(1)} %collective-permute-done.6.refs_1_, bf16[2,64,1024]{2,1,0:T(8,128)(2,1)S(1)} %collective-permute-done.7.refs_2_, ...), custom_call_target="tpu_custom_call" | custom-call | tf_op jit(solution)/shard_map/pallas_call | solution.py:322
  108.8 3.4 %all-to-all-done.1.received = bf16[4,16,2048]{2,1,0:T(8,128)(2,1)S(1)} async-done(((bf16[4,16,2048]{2,1,0:T(8,128)(2,1)}), bf16[4,16,2048]{2,1,0:T(8,128)(2,1)S(1)}, u32[]{:S(2)}, u32[]{:S(2)}) %all-to-all-start.1) | async-done | bytes 262176 | tf_op jit(solution)/shard_map/all_to_all | solution.py:259
  (31 shorter events, 5.4 us)
Async XLA Ops:
  0.6 6.7 %copy-start = (bf16[2,64,4096]{2,1,0:T(8,128)(2,1)S(1)}, bf16[2,64,4096]{2,1,0:T(8,128)(2,1)}, u32[]{:S(2)}) copy-start(bf16[2,64,4096]{2,1,0:T(8,128)(2,1)} %queries.1) | copy-start | bytes 3145732
  0.6 1.0 copy-start.2
  2.4 10.5 %all-to-all-start = ((bf16[4,16,2048]{2,1,0:T(8,128)(2,1)}), bf16[4,16,2048]{2,1,0:T(8,128)(2,1)S(1)}, u32[]{:S(2)}, u32[]{:S(2)}) async-start(bf16[4,16,2048]{2,1,0:T(8,128)(2,1)} %shard_map.120), calls=%async_computation | async-start | bytes 524288 | tf_op jit(solution)/shard_map/all_to_all | solution.py:259
  7.3 1.2 %copy-start.1 = (bf16[2,64,4096]{2,1,0:T(8,128)(2,1)S(1)}, bf16[2,64,4096]{2,1,0:T(8,128)(2,1)}, u32[]{:S(2)}) copy-start(bf16[2,64,4096]{2,1,0:T(8,128)(2,1)} %cotangent.1) | copy-start | bytes 3145732
  8.5 38.2 %copy-start.3 = (f32[4,16,128]{2,1,0:T(8,128)S(1)}, f32[4,16,128]{2,1,0:T(8,128)}, u32[]{:S(2)}) copy-start(f32[4,16,128]{2,1,0:T(8,128)} %lambdas.3) | copy-start | bytes 98308
  8.5 38.2 %copy-start.6 = (s32[2]{0:T(128)S(1)}, s32[2]{0:T(128)}, u32[]{:S(2)}) copy-start(s32[2]{0:T(128)} %counts.1) | copy-start | bytes 28
  9.5 36.0 %collective-permute-start = (bf16[2,64,2048]{2,1,0:T(8,128)(2,1)S(1)}, bf16[2,64,2048]{2,1,0:T(8,128)(2,1)S(1)}, u32[]{:S(2)}, u32[]{:S(2)}) collective-permute-start(bf16[2,64,2048]{2,1,0:T(8,128)(2,1)S(1)} %get-tuple-element.22), channel_id=1, source_target_pairs={{0,1},{1,2},{2,3},{3,0},{4,5},{5,6},{6,7},{7,4},{8,9},{9,10},{10,1... | collective-permute-start | bytes 1572872 | tf_op jit(solution)/shard_map/ppermute | solution.py:285
  12.9 17.0 %collective-permute-start.5 = (bf16[4,16,2048]{2,1,0:T(8,128)(2,1)S(1)}, bf16[4,16,2048]{2,1,0:T(8,128)(2,1)S(1)}, u32[]{:S(2)}, u32[]{:S(2)}) collective-permute-start(bf16[4,16,2048]{2,1,0:T(8,128)(2,1)S(1)} %all-to-all-done.refs_4_), channel_id=1, source_target_pairs={{0,12},{4,0},{8,4},{12,8},{1,13},{5,1},{9,5},{13,9},{2,14},{6,2},{... | collective-permute-start | bytes 786440 | tf_op jit(solution)/shard_map/ppermute | solution.py:288
  20.5 25.0 %collective-permute-start.1 = (bf16[2,64,2048]{2,1,0:T(8,128)(2,1)S(1)}, bf16[2,64,2048]{2,1,0:T(8,128)(2,1)S(1)}, u32[]{:S(2)}, u32[]{:S(2)}) collective-permute-start(bf16[2,64,2048]{2,1,0:T(8,128)(2,1)S(1)} %get-tuple-element.23), channel_id=1, source_target_pairs={{0,2},{1,3},{2,0},{3,1},{4,6},{5,7},{6,4},{7,5},{8,10},{9,11},{10,... | collective-permute-start | bytes 1572872 | tf_op jit(solution)/shard_map/ppermute | solution.py:285
  24.8 22.0 %collective-permute-start.2 = (bf16[2,64,2048]{2,1,0:T(8,128)(2,1)S(1)}, bf16[2,64,2048]{2,1,0:T(8,128)(2,1)S(1)}, u32[]{:S(2)}, u32[]{:S(2)}) collective-permute-start(bf16[2,64,2048]{2,1,0:T(8,128)(2,1)S(1)} %get-tuple-element.24), channel_id=1, source_target_pairs={{0,3},{1,0},{2,1},{3,2},{4,7},{5,4},{6,5},{7,6},{8,11},{9,8},{10,9... | collective-permute-start | bytes 1572872 | tf_op jit(solution)/shard_map/ppermute | solution.py:285
  27.9 17.6 %collective-permute-start.4 = (bf16[4,16,2048]{2,1,0:T(8,128)(2,1)S(1)}, bf16[4,16,2048]{2,1,0:T(8,128)(2,1)S(1)}, u32[]{:S(2)}, u32[]{:S(2)}) collective-permute-start(bf16[4,16,2048]{2,1,0:T(8,128)(2,1)S(1)} %all-to-all-done.refs_4_), channel_id=1, source_target_pairs={{0,8},{4,12},{8,0},{12,4},{1,9},{5,13},{9,1},{13,5},{2,10},{6,14},... | collective-permute-start | bytes 786440 | tf_op jit(solution)/shard_map/ppermute | solution.py:288
  29.8 15.7 %collective-permute-start.3 = (bf16[4,16,2048]{2,1,0:T(8,128)(2,1)S(1)}, bf16[4,16,2048]{2,1,0:T(8,128)(2,1)S(1)}, u32[]{:S(2)}, u32[]{:S(2)}) collective-permute-start(bf16[4,16,2048]{2,1,0:T(8,128)(2,1)S(1)} %all-to-all-done.refs_4_), channel_id=1, source_target_pairs={{0,4},{4,8},{8,12},{12,0},{1,5},{5,9},{9,13},{13,1},{2,6},{6,10},{... | collective-permute-start | bytes 786440 | tf_op jit(solution)/shard_map/ppermute | solution.py:288
  46.8 0.7 copy-start.4
  46.8 0.7 copy-start.5
  56.9 24.4 %collective-permute-start.9 = (bf16[4,16,2048]{2,1,0:T(8,128)(2,1)}, bf16[4,16,2048]{2,1,0:T(8,128)(2,1)S(1)}, u32[]{:S(2)}, u32[]{:S(2)}) collective-permute-start(bf16[4,16,2048]{2,1,0:T(8,128)(2,1)} %get-tuple-element.30), channel_id=1, source_target_pairs={{0,12},{4,0},{8,4},{12,8},{1,13},{5,1},{9,5},{13,9},{2,14},{6,2},{... | collective-permute-start | bytes 786440 | tf_op jit(solution)/shard_map/ppermute | solution.py:312
  58.8 36.9 %collective-permute-start.10 = (bf16[4,16,2048]{2,1,0:T(8,128)(2,1)}, bf16[4,16,2048]{2,1,0:T(8,128)(2,1)S(1)}, u32[]{:S(2)}, u32[]{:S(2)}) collective-permute-start(bf16[4,16,2048]{2,1,0:T(8,128)(2,1)} %get-tuple-element.31), channel_id=1, source_target_pairs={{0,8},{4,12},{8,0},{12,4},{1,9},{5,13},{9,1},{13,5},{2,10},{6,14},... | collective-permute-start | bytes 786440 | tf_op jit(solution)/shard_map/ppermute | solution.py:312
  62.3 33.4 %collective-permute-start.11 = (bf16[4,16,2048]{2,1,0:T(8,128)(2,1)S(1)}, bf16[4,16,2048]{2,1,0:T(8,128)(2,1)S(1)}, u32[]{:S(2)}, u32[]{:S(2)}) collective-permute-start(bf16[4,16,2048]{2,1,0:T(8,128)(2,1)S(1)} %get-tuple-element.32), channel_id=1, source_target_pairs={{0,4},{4,8},{8,12},{12,0},{1,5},{5,9},{9,13},{13,1},{2,6},{6,10},{... | collective-permute-start | bytes 786440 | tf_op jit(solution)/shard_map/ppermute | solution.py:312
  65.7 18.1 %all-to-all-start.2 = ((f32[32,4,128]{2,1,0:T(4,128)}), f32[32,4,128]{2,1,0:T(4,128)S(1)}, u32[]{:S(2)}, u32[]{:S(2)}) async-start(f32[32,4,128]{2,1,0:T(4,128)} %get-tuple-element.33), calls=%async_computation.2 | async-start | bytes 131072 | tf_op jit(solution)/shard_map/all_to_all | solution.py:259
  74.5 32.8 %collective-permute-start.6 = (bf16[2,64,1024]{2,1,0:T(8,128)(2,1)S(1)}, bf16[2,64,1024]{2,1,0:T(8,128)(2,1)S(1)}, u32[]{:S(2)}, u32[]{:S(2)}) collective-permute-start(bf16[2,64,1024]{2,1,0:T(8,128)(2,1)S(1)} %get-tuple-element.26), channel_id=1, source_target_pairs={{0,3},{1,0},{2,1},{3,2},{4,7},{5,4},{6,5},{7,6},{8,11},{9,8},{10,9... | collective-permute-start | bytes 786440 | tf_op jit(solution)/shard_map/ppermute | solution.py:317
  78.8 28.4 %collective-permute-start.7 = (bf16[2,64,1024]{2,1,0:T(8,128)(2,1)S(1)}, bf16[2,64,1024]{2,1,0:T(8,128)(2,1)S(1)}, u32[]{:S(2)}, u32[]{:S(2)}) collective-permute-start(bf16[2,64,1024]{2,1,0:T(8,128)(2,1)S(1)} %get-tuple-element.27), channel_id=1, source_target_pairs={{0,2},{1,3},{2,0},{3,1},{4,6},{5,7},{6,4},{7,5},{8,10},{9,11},{10,... | collective-permute-start | bytes 786440 | tf_op jit(solution)/shard_map/ppermute | solution.py:317
  81.3 25.9 %collective-permute-start.8 = (bf16[2,64,1024]{2,1,0:T(8,128)(2,1)S(1)}, bf16[2,64,1024]{2,1,0:T(8,128)(2,1)S(1)}, u32[]{:S(2)}, u32[]{:S(2)}) collective-permute-start(bf16[2,64,1024]{2,1,0:T(8,128)(2,1)S(1)} %get-tuple-element.28), channel_id=1, source_target_pairs={{0,1},{1,2},{2,3},{3,0},{4,5},{5,6},{6,7},{7,4},{8,9},{9,10},{10,1... | collective-permute-start | bytes 786440 | tf_op jit(solution)/shard_map/ppermute | solution.py:317
  84.5 18.6 %all-to-all-start.3 = ((f32[16,4,128]{2,1,0:T(4,128)}), f32[16,4,128]{2,1,0:T(4,128)S(1)}, u32[]{:S(2)}, u32[]{:S(2)}) async-start(f32[16,4,128]{2,1,0:T(4,128)} %shard_map.125), calls=%async_computation.3 | async-start | bytes 65536 | tf_op jit(solution)/shard_map/all_to_all | solution.py:259
  103.1 9.2 %all-to-all-start.1 = ((bf16[4,16,2048]{2,1,0:T(8,128)(2,1)}), bf16[4,16,2048]{2,1,0:T(8,128)(2,1)S(1)}, u32[]{:S(2)}, u32[]{:S(2)}) async-start(bf16[4,16,2048]{2,1,0:T(8,128)(2,1)} %shard_map.123), calls=%async_computation.1 | async-start | bytes 524288 | tf_op jit(solution)/shard_map/all_to_all | solution.py:259

commit v2 on v1

--- a/solution.py
+++ b/solution.py
@@ -13,6 +13,7 @@
 IMAGE = ("zl", "x")
 FIRST, SECOND = 32, 16
 PARTS = 4
+ORDER, LATE = (0, 2, 1, 3), (0, 3, 1, 2)
 VMEM = pl.BlockSpec(memory_space=pltpu.VMEM)
 SMEM = pl.BlockSpec(memory_space=pltpu.SMEM)
 ANY = pl.BlockSpec(memory_space=pl.ANY)
@@ -42,11 +43,11 @@
 
 
 def pack_text_body(place, queries, cotangent, *refs):
-    outs, sems = refs[:PARTS], refs[PARTS]
+    outs, sems = refs[:-1], refs[-1]
     half = queries.shape[2] // 2
     width = half // PARTS
     copies = []
-    for shift in range(PARTS):
+    for n, shift in enumerate(ORDER):
         g = wrap(place[1] + shift)
         first = pl.multiple_of(g * width, width)
         second = pl.multiple_of(half + g * width, width)
@@ -58,7 +59,7 @@
         )
         for i, (source, columns) in enumerate(pieces):
             copies.append(
-                pltpu.make_async_copy(source, outs[shift].at[:, :, columns], sems.at[shift, i])
+                pltpu.make_async_copy(source, outs[n].at[:, :, columns], sems.at[n, i])
             )
     for copy in copies:
         copy.start()
@@ -69,7 +70,8 @@
 def attend_body(
     place, assignment, counts, lambdas, norm_gain, gate, *refs, heads, head_size, patch
 ):
-    text, vision, grad_text, grad_vision = (refs[i * PARTS : (i + 1) * PARTS] for i in range(4))
+    text, vision, payload, grad_vision = (refs[i * PARTS : (i + 1) * PARTS] for i in range(4))
+    vision = [vision[LATE.index(k)] for k in range(PARTS)]
     stats = refs[4 * PARTS]
     zl, x = place[0], place[1]
     seqs, toks = text[0].shape[0], text[0].shape[1]
@@ -142,8 +144,9 @@
             for m in range(2):
                 grad_scores = (probs[m] * (grad_mixed - sums[m]) * factors[m]).astype(bf16)
                 grad_query = dot(grad_scores, key_rows[m], (1, 0)).astype(bf16)
+                own_rows = pl.ds(pl.multiple_of(s * toks, toks), toks)
                 for i in range(PARTS):
-                    grad_text[i][s, :, map_columns[m]] = grad_query[i * toks : (i + 1) * toks]
+                    payload[i][own_rows, map_columns[m]] = grad_query[i * toks : (i + 1) * toks]
                 grad_key = dot(grad_scores, query_rows[m], (0, 0))
                 grad_keys[m].append(grad_key.reshape(frames, patch, -1))
         for columns, parts in (
@@ -163,18 +166,35 @@
         stats[i] = tile
 
 
-def sum_parts(refs):
-    total = refs[0][...].astype(f32)
-    for part in refs[1:]:
-        total = total + part[...].astype(f32)
-    return total
-
-
-def sum_vision_body(*refs):
-    refs[PARTS][...] = sum_parts(refs[:PARTS]).astype(bf16)
-
-
-def spread_sum_body(tiles, out):
+def sum_vision_body(place, after, *refs):
+    del after
+    parts, outs, total, sems = (
+        refs[:PARTS],
+        refs[2 * PARTS : 3 * PARTS],
+        refs[3 * PARTS],
+        refs[3 * PARTS + 1],
+    )
+    rows, columns = total.shape[1] // 2, total.shape[2]
+    copies = []
+    for k in range(PARTS):
+        x = wrap(place[1] - ORDER[k])
+        value = parts[0][x].astype(f32)
+        for part in parts[1:]:
+            value = value + part[x].astype(f32)
+        value = value.astype(bf16)
+        total[k, :rows] = value[:, :columns]
+        total[k, rows:] = value[:, columns:]
+        base = outs[k].shape[0] - 2 * rows
+        copies.append(
+            pltpu.make_async_copy(total.at[k], outs[k].at[pl.ds(base, 2 * rows)], sems.at[k])
+        )
+        copies[k].start()
+    for copy in copies:
+        copy.wait()
+
+
+def spread_sum_body(tiles, after, out):
+    del after
     total = jnp.sum(tiles[...], axis=0)
     for i in range(out.shape[0]):
         out[i] = total
@@ -203,31 +223,31 @@
     grad_lambdas[3] = -weight_two * lambdas[2]
 
 
-def unpack_vision_body(received, out):
-    half = out.shape[1] // 4
-    width = half // PARTS
-    for g in range(PARTS):
-        out[:, g * width : (g + 1) * width] = received[g, :, :width]
-        out[:, half + g * width : half + (g + 1) * width] = received[g, :, width : 2 * width]
-        out[:, 2 * half + 2 * g * width : 2 * half + 2 * (g + 1) * width] = received[
-            g, :, 2 * width :
-        ]
-
-
-def unpack_text_body(place, *refs):
-    parts, out, sems = refs[:PARTS], refs[PARTS], refs[PARTS + 1]
-    half = out.shape[2] // 2
+def unpack_body(place, *refs):
+    parts, grad_queries, grad_vision, sems = refs[:PARTS], refs[PARTS], refs[PARTS + 1], refs[-1]
+    text_rows, rows = grad_queries.shape[0], grad_vision.shape[0]
+    half = grad_queries.shape[1] // 2
     width = half // PARTS
     copies = []
-    for shift in range(PARTS):
-        g = wrap(place[1] + shift)
-        for m in range(2):
-            columns = pl.ds(pl.multiple_of(m * half + g * width, width), width)
+    for k in range(PARTS):
+        g = wrap(place[1] + ORDER[k])
+        first = pl.multiple_of(g * width, width)
+        second = pl.multiple_of(half + g * width, width)
+        wide = pl.multiple_of(2 * half + 2 * g * width, 2 * width)
+        text, keys = pl.ds(0, text_rows), pl.ds(text_rows, rows)
+        values = pl.ds(text_rows + rows, rows)
+        left, right, both = pl.ds(0, width), pl.ds(width, width), pl.ds(0, 2 * width)
+        pieces = (
+            (text, left, grad_queries, pl.ds(first, width)),
+            (text, right, grad_queries, pl.ds(second, width)),
+            (keys, left, grad_vision, pl.ds(first, width)),
+            (keys, right, grad_vision, pl.ds(second, width)),
+            (values, both, grad_vision, pl.ds(wide, 2 * width)),
+        )
+        for i, (own_rows, columns, out, to) in enumerate(pieces):
             copies.append(
                 pltpu.make_async_copy(
-                    parts[shift].at[:, :, pl.ds(m * width, width)],
-                    out.at[:, :, columns],
-                    sems.at[shift, m],
+                    parts[k].at[own_rows, columns], out.at[:, to], sems.at[k, i]
                 )
             )
     for copy in copies:
@@ -236,8 +256,11 @@
         copy.wait()
 
 
-def along(shift):
-    return [(i, (i + shift) % PARTS) for i in range(PARTS)]
+def shift_all(parts, axis, order, way):
+    return [
+        lax.ppermute(part, axis, [(i, (i + way * k) % PARTS) for i in range(PARTS)]) if k else part
+        for part, k in zip(parts, order)
+    ]
 
 
 def kernel(body, out_shape, in_specs, out_specs, **more):
@@ -281,16 +304,12 @@
         [ANY] * PARTS,
         scratch_shapes=[pltpu.SemaphoreType.DMA((PARTS, 3))],
     )(place, queries, cotangent)
-    held_text = [sent_text[0]] + [
-        lax.ppermute(sent_text[k], "x", along(k)) for k in range(1, PARTS)
-    ]
-    held_vision = [row_vision] + [
-        lax.ppermute(row_vision, "zl", along(k)) for k in range(1, PARTS)
-    ]
+    held_text = shift_all(sent_text, "x", ORDER, 1)
+    held_vision = shift_all([row_vision] * PARTS, "zl", LATE, 1)
 
     grads = kernel(
         functools.partial(attend_body, heads=heads, head_size=head_size, patch=patch),
-        [shaped((seqs, toks, text_columns // PARTS))] * PARTS
+        [shaped((seqs * toks + 2 * rows, text_columns // PARTS))] * PARTS
         + [slab] * PARTS
         + [shaped((FIRST, 4, head_size), f32)],
         [SMEM] * 3 + [VMEM] * (3 + 2 * PARTS),
@@ -305,38 +324,42 @@
         *held_text,
         *held_vision,
     )
-    grad_text, grad_vision, stats = grads[:PARTS], grads[PARTS : 2 * PARTS], grads[2 * PARTS]
-
+    payload, grad_vision, stats = grads[:PARTS], grads[PARTS : 2 * PARTS], grads[2 * PARTS]
+
+    back_vision = shift_all([grad_vision[k] for k in ORDER], "zl", ORDER, -1)
     stats = exchange(stats, ("y", "x"))
-    back_vision = [grad_vision[0]] + [
-        lax.ppermute(grad_vision[k], "zl", along(-k)) for k in range(1, PARTS)
-    ]
-    stats = kernel(spread_sum_body, shaped((SECOND, 4, head_size), f32), [VMEM], VMEM)(stats)
+    payload = kernel(
+        sum_vision_body,
+        [shaped(payload[0].shape)] * PARTS,
+        [SMEM, ANY] + [VMEM] * PARTS + [ANY] * PARTS,
+        [ANY] * PARTS,
+        scratch_shapes=[
+            pltpu.VMEM((PARTS, 2 * rows, text_columns // PARTS), bf16),
+            pltpu.SemaphoreType.DMA((PARTS,)),
+        ],
+        input_output_aliases={2 + PARTS + k: k for k in range(PARTS)},
+    )(place, stats, *back_vision, *payload)
+    back = shift_all(payload, "x", ORDER, -1)
+    stats = kernel(spread_sum_body, shaped((SECOND, 4, head_size), f32), [VMEM, ANY], VMEM)(
+        stats, payload[0]
+    )
     stats = exchange(stats, ("zh", "core", "zl"))
-    back_text = [grad_text[0]] + [
-        lax.ppermute(grad_text[k], "x", along(-k)) for k in range(1, PARTS)
-    ]
-    row_vision = kernel(sum_vision_body, slab, [VMEM] * PARTS, VMEM)(*back_vision)
-    row_vision = exchange(row_vision, "x")
-
-    grad_queries = kernel(
-        unpack_text_body,
-        shaped(queries.shape),
+    grad_queries, grad_vision = kernel(
+        unpack_body,
+        [shaped((seqs * toks, text_columns)), shaped((rows, vision_columns))],
         [SMEM] + [ANY] * PARTS,
-        ANY,
-        scratch_shapes=[pltpu.SemaphoreType.DMA((PARTS, 2))],
-    )(place, *back_text)
+        [ANY] * 2,
+        scratch_shapes=[pltpu.SemaphoreType.DMA((PARTS, 5))],
+    )(place, *back)
+
     grad_lambdas, grad_gain, grad_gate = kernel(
         finish_body,
         [shaped(lambdas.shape, f32), shaped(gain_rows.shape, f32), shaped((1, 1), f32)],
         [VMEM] * 4,
         [VMEM] * 3,
     )(stats, lambdas, gain_rows, gate)
-    grad_vision = kernel(unpack_vision_body, shaped((rows, vision_columns)), [VMEM], VMEM)(
-        row_vision
-    )
     return (
-        grad_queries,
+        grad_queries.reshape(queries.shape),
         grad_vision.reshape(vision.shape),
         grad_lambdas,
         grad_gain.reshape(norm_gain.shape),

time: 114 us -> 114 us (level)
  blocking collectives: 0 us -> 35.1 us
  starting transfers between devices: 68.8 us -> 46.3 us
  waiting for transfers between devices: 24.1 us -> 13.6 us
  Pallas kernels: 15.6 us -> 13.9 us
    all_to_all x0 -> x2, blocking collectives: none -> 35.1 us  [exchange(): return lax.all_to_all(value, axes, 0, 0, tiled=True)]
    all_to_all x4 -> x1, starting transfers between devices: 28.2 us -> 4.84 us  [exchange(): return lax.all_to_all(value, axes, 0, 0, tiled=True)]
    all_to_all x4 -> x1, waiting for transfers between devices: 9.95 us -> 3.29 us  [exchange(): return lax.all_to_all(value, axes, 0, 0, tiled=True)]
    ppermute x12, waiting for transfers between devices: 14.1 us -> 10.3 us  [shift_all(): lax.ppermute(part, axis, [(i, (i + way * k) % PARTS) for i in range(PARTS)])]
    pallas_call x4 -> x3, Pallas kernels: 3.78 us -> 2.89 us  [the longest x1 1.76 us: shards(): kernel(unpack_body, [shaped((seqs * toks, text_columns)), shaped((rows, v...]
  transfers between devices with their start and end apart: 16 -> 13, of which waited for: 4 -> 3; matrix products, arithmetic and copies ran while one was open for 0% -> 0% of each run, Pallas kernels for 4% -> 1%
where the time goes in v2:
time: 114 us; the launch traced here: 113 us
  starting transfers between devices  46.3 us (41%)
  blocking collectives  35.1 us (31%)
  Pallas kernels  13.9 us (12%)
  waiting for transfers between devices  13.6 us (12%)
  local copies, waits for them, and re-layouts  2.93 us (3%)
  between operations  1.46 us (1%)
    ppermute x12, starting transfers between devices, shift_all(): lax.ppermute(part, axis, [(i, (i + way * k) % PARTS) for i in range(PARTS)])  41.5 us
    all_to_all x2, blocking collectives, exchange(): return lax.all_to_all(value, axes, 0, 0, tiled=True)  35.1 us
    ppermute x12, waiting for transfers between devices, shift_all(): lax.ppermute(part, axis, [(i, (i + way * k) % PARTS) for i in range(PARTS)])  10.3 us
    pallas_call x1, Pallas kernels, shards(): kernel(functools.partial(attend_body, heads=heads, head_size=head_size, p...  8.67 us
    all_to_all x1, starting transfers between devices, exchange(): return lax.all_to_all(value, axes, 0, 0, tiled=True)  4.84 us
    all_to_all x1, waiting for transfers between devices, exchange(): return lax.all_to_all(value, axes, 0, 0, tiled=True)  3.29 us
    unnamed x14, local copies, waits for them, and re-layouts  2.93 us
  transfers between devices with their start and end apart: 13, of which 3 were waited for; matrix products, arithmetic and copies ran while one was open for 0% of the time, Pallas kernels for 1%

profile of v2, /device:TPU:1, one launch (start us, length us, event | category | flops | bytes accessed | tf_op | source)
XLA Modules:
  0.0 113.4 jit_solution(8517740316746673339)
XLA Ops:
  0.7 1.0 copy-done.2
  2.4 4.8 %all-to-all-start = ((bf16[4,16,2048]{2,1,0:T(8,128)(2,1)}), bf16[4,16,2048]{2,1,0:T(8,128)(2,1)S(1)}, u32[]{:S(2)}, u32[]{:S(2)}) async-start(bf16[4,16,2048]{2,1,0:T(8,128)(2,1)} %shard_map.120), calls=%async_computation | async-start | bytes 524288 | tf_op jit(solution)/shard_map/all_to_all | solution.py:282
  7.3 1.2 %copy-done.1 = bf16[2,64,4096]{2,1,0:T(8,128)(2,1)S(1)} copy-done((bf16[2,64,4096]{2,1,0:T(8,128)(2,1)S(1)}, bf16[2,64,4096]{2,1,0:T(8,128)(2,1)}, u32[]{:S(2)}) %copy-start.1) | copy-done | bytes 1048600
  8.6 0.9 shard_map.119
  9.5 3.3 %all-to-all-done.refs_4_ = bf16[4,16,2048]{2,1,0:T(8,128)(2,1)S(1)} async-done(((bf16[4,16,2048]{2,1,0:T(8,128)(2,1)}), bf16[4,16,2048]{2,1,0:T(8,128)(2,1)S(1)}, u32[]{:S(2)}, u32[]{:S(2)}) %all-to-all-start) | async-done | bytes 262176 | tf_op jit(solution)/shard_map/all_to_all | solution.py:282
  12.8 5.8 %collective-permute-start.5 = (bf16[4,16,2048]{2,1,0:T(8,128)(2,1)S(1)}, bf16[4,16,2048]{2,1,0:T(8,128)(2,1)S(1)}, u32[]{:S(2)}, u32[]{:S(2)}) collective-permute-start(bf16[4,16,2048]{2,1,0:T(8,128)(2,1)S(1)} %all-to-all-done.refs_4_), channel_id=1, source_target_pairs={{0,8},{4,12},{8,0},{12,4},{1,9},{5,13},{9,1},{13,5},{2,10},{6,14},... | collective-permute-start | bytes 786440 | tf_op jit(solution)/shard_map/ppermute | solution.py:261
  18.6 2.2 %collective-permute-start = (bf16[2,64,2048]{2,1,0:T(8,128)(2,1)S(1)}, bf16[2,64,2048]{2,1,0:T(8,128)(2,1)S(1)}, u32[]{:S(2)}, u32[]{:S(2)}) collective-permute-start(bf16[2,64,2048]{2,1,0:T(8,128)(2,1)S(1)} %get-tuple-element.28), channel_id=1, source_target_pairs={{0,2},{1,3},{2,0},{3,1},{4,6},{5,7},{6,4},{7,5},{8,10},{9,11},{10,... | collective-permute-start | bytes 1572872 | tf_op jit(solution)/shard_map/ppermute | solution.py:261
  20.8 3.1 %collective-permute-start.1 = (bf16[2,64,2048]{2,1,0:T(8,128)(2,1)S(1)}, bf16[2,64,2048]{2,1,0:T(8,128)(2,1)S(1)}, u32[]{:S(2)}, u32[]{:S(2)}) collective-permute-start(bf16[2,64,2048]{2,1,0:T(8,128)(2,1)S(1)} %get-tuple-element.29), channel_id=1, source_target_pairs={{0,1},{1,2},{2,3},{3,0},{4,5},{5,6},{6,7},{7,4},{8,9},{9,10},{10,1... | collective-permute-start | bytes 1572872 | tf_op jit(solution)/shard_map/ppermute | solution.py:261
  23.9 3.4 %collective-permute-start.2 = (bf16[2,64,2048]{2,1,0:T(8,128)(2,1)S(1)}, bf16[2,64,2048]{2,1,0:T(8,128)(2,1)S(1)}, u32[]{:S(2)}, u32[]{:S(2)}) collective-permute-start(bf16[2,64,2048]{2,1,0:T(8,128)(2,1)S(1)} %get-tuple-element.30), channel_id=1, source_target_pairs={{0,3},{1,0},{2,1},{3,2},{4,7},{5,4},{6,5},{7,6},{8,11},{9,8},{10,9... | collective-permute-start | bytes 1572872 | tf_op jit(solution)/shard_map/ppermute | solution.py:261
  27.3 4.0 %collective-permute-start.4 = (bf16[4,16,2048]{2,1,0:T(8,128)(2,1)S(1)}, bf16[4,16,2048]{2,1,0:T(8,128)(2,1)S(1)}, u32[]{:S(2)}, u32[]{:S(2)}) collective-permute-start(bf16[4,16,2048]{2,1,0:T(8,128)(2,1)S(1)} %all-to-all-done.refs_4_), channel_id=1, source_target_pairs={{0,4},{4,8},{8,12},{12,0},{1,5},{5,9},{9,13},{13,1},{2,6},{6,10},{... | collective-permute-start | bytes 786440 | tf_op jit(solution)/shard_map/ppermute | solution.py:261
  31.3 4.8 %collective-permute-start.3 = (bf16[4,16,2048]{2,1,0:T(8,128)(2,1)S(1)}, bf16[4,16,2048]{2,1,0:T(8,128)(2,1)S(1)}, u32[]{:S(2)}, u32[]{:S(2)}) collective-permute-start(bf16[4,16,2048]{2,1,0:T(8,128)(2,1)S(1)} %all-to-all-done.refs_4_), channel_id=1, source_target_pairs={{0,12},{4,0},{8,4},{12,8},{1,13},{5,1},{9,5},{13,9},{2,14},{6,2},{... | collective-permute-start | bytes 786440 | tf_op jit(solution)/shard_map/ppermute | solution.py:261
  36.8 5.5 %collective-permute-done.3.refs_5_ = bf16[4,16,2048]{2,1,0:T(8,128)(2,1)S(1)} collective-permute-done((bf16[4,16,2048]{2,1,0:T(8,128)(2,1)S(1)}, bf16[4,16,2048]{2,1,0:T(8,128)(2,1)S(1)}, u32[]{:S(2)}, u32[]{:S(2)}) %collective-permute-start.3) | collective-permute-done | bytes 262176 | tf_op jit(solution)/shard_map/ppermute | solution.py:261
  42.3 4.8 %collective-permute-done.1.refs_2_ = bf16[2,64,2048]{2,1,0:T(8,128)(2,1)S(1)} collective-permute-done((bf16[2,64,2048]{2,1,0:T(8,128)(2,1)S(1)}, bf16[2,64,2048]{2,1,0:T(8,128)(2,1)S(1)}, u32[]{:S(2)}, u32[]{:S(2)}) %collective-permute-start.1) | collective-permute-done | bytes 524320 | tf_op jit(solution)/shard_map/ppermute | solution.py:261
  47.8 8.7 %shard_map.121 = (bf16[160,1024]{1,0:T(8,128)(2,1)S(1)}, bf16[160,1024]{1,0:T(8,128)(2,1)S(1)}, bf16[160,1024]{1,0:T(8,128)(2,1)S(1)}, bf16[160,1024]{1,0:T(8,12...) custom-call(s32[2]{0:T(128)S(1)} %pad_add_fusion.place, ...), custom_call_target="tpu_custom_call" | custom-call | tf_op jit(solution)/shard_map/pallas_call | solution.py:310
  56.4 1.9 %collective-permute-start.6 = (bf16[4,16,2048]{2,1,0:T(8,128)(2,1)S(1)}, bf16[4,16,2048]{2,1,0:T(8,128)(2,1)S(1)}, u32[]{:S(2)}, u32[]{:S(2)}) collective-permute-start(bf16[4,16,2048]{2,1,0:T(8,128)(2,1)S(1)} %get-tuple-element.33), channel_id=1, source_target_pairs={{0,8},{4,12},{8,0},{12,4},{1,9},{5,13},{9,1},{13,5},{2,10},{6,14},... | collective-permute-start | bytes 786440 | tf_op jit(solution)/shard_map/ppermute | solution.py:261
  58.4 6.1 %collective-permute-start.7 = (bf16[4,16,2048]{2,1,0:T(8,128)(2,1)S(1)}, bf16[4,16,2048]{2,1,0:T(8,128)(2,1)S(1)}, u32[]{:S(2)}, u32[]{:S(2)}) collective-permute-start(bf16[4,16,2048]{2,1,0:T(8,128)(2,1)S(1)} %get-tuple-element.34), channel_id=1, source_target_pairs={{0,12},{4,0},{8,4},{12,8},{1,13},{5,1},{9,5},{13,9},{2,14},{6,2},{... | collective-permute-start | bytes 786440 | tf_op jit(solution)/shard_map/ppermute | solution.py:261
  64.5 1.9 %collective-permute-start.8 = (bf16[4,16,2048]{2,1,0:T(8,128)(2,1)S(1)}, bf16[4,16,2048]{2,1,0:T(8,128)(2,1)S(1)}, u32[]{:S(2)}, u32[]{:S(2)}) collective-permute-start(bf16[4,16,2048]{2,1,0:T(8,128)(2,1)S(1)} %get-tuple-element.35), channel_id=1, source_target_pairs={{0,4},{4,8},{8,12},{12,0},{1,5},{5,9},{9,13},{13,1},{2,6},{6,10},{... | collective-permute-start | bytes 786440 | tf_op jit(solution)/shard_map/ppermute | solution.py:261
  66.4 16.2 %all_to_all.15.after.tiles = f32[32,4,128]{2,1,0:T(4,128)S(1)} all-to-all(f32[32,4,128]{2,1,0:T(4,128)S(1)} %get-tuple-element.31), channel_id=1, replica_groups=mesh['y'=8,'zh'=2,'core'=2,'zl'=4,'x'=4] {'y','x'}, dimensions={0} | all-to-all | bytes 131072 | tf_op jit(solution)/shard_map/all_to_all | solution.py:282
  82.6 1.1 shard_map.122
  83.7 2.9 %collective-permute-start.9 = (bf16[160,1024]{1,0:T(8,128)(2,1)S(1)}, bf16[160,1024]{1,0:T(8,128)(2,1)S(1)}, u32[]{:S(2)}, u32[]{:S(2)}) collective-permute-start(bf16[160,1024]{1,0:T(8,128)(2,1)S(1)} %get-tuple-element.41), channel_id=1, source_target_pairs={{0,2},{1,3},{2,0},{3,1},{4,6},{5,7},{6,4},{7,5},{8,10},{9,11},{10,... | collective-permute-start | bytes 983048 | tf_op jit(solution)/shard_map/ppermute | solution.py:261
  86.5 3.5 %collective-permute-start.10 = (bf16[160,1024]{1,0:T(8,128)(2,1)S(1)}, bf16[160,1024]{1,0:T(8,128)(2,1)S(1)}, u32[]{:S(2)}, u32[]{:S(2)}) collective-permute-start(bf16[160,1024]{1,0:T(8,128)(2,1)S(1)} %get-tuple-element.42), channel_id=1, source_target_pairs={{0,3},{1,0},{2,1},{3,2},{4,7},{5,4},{6,5},{7,6},{8,11},{9,8},{10,9... | collective-permute-start | bytes 983048 | tf_op jit(solution)/shard_map/ppermute | solution.py:261
  90.0 1.9 %collective-permute-start.11 = (bf16[160,1024]{1,0:T(8,128)(2,1)S(1)}, bf16[160,1024]{1,0:T(8,128)(2,1)S(1)}, u32[]{:S(2)}, u32[]{:S(2)}) collective-permute-start(bf16[160,1024]{1,0:T(8,128)(2,1)S(1)} %get-tuple-element.43), channel_id=1, source_target_pairs={{0,1},{1,2},{2,3},{3,0},{4,5},{5,6},{6,7},{7,4},{8,9},{9,10},{10,1... | collective-permute-start | bytes 983048 | tf_op jit(solution)/shard_map/ppermute | solution.py:261
  92.0 18.9 %all_to_all.16.tiles = f32[16,4,128]{2,1,0:T(4,128)S(1)} all-to-all(f32[16,4,128]{2,1,0:T(4,128)S(1)} %shard_map.124), channel_id=1, replica_groups=mesh['y'=8,'zh'=2,'core'=2,'zl'=4,'x'=4] {'zh','core','zl'}, dimensions={0} | all-to-all | bytes 65536 | tf_op jit(solution)/shard_map/all_to_all | solution.py:282
  111.7 1.8 %shard_map.123 = (bf16[128,4096]{1,0:T(8,128)(2,1)}, bf16[16,8192]{1,0:T(8,128)(2,1)}) custom-call(s32[2]{0:T(128)S(1)} %pad_add_fusion.place, bf16[160,1024]{1,0:T(8,128)(2,1)S(1)} %get-tuple-element.40.refs_0_.after, bf16[160,1024]{1,0:T(8,128)(2,1)S(1)} %collective-permute-done.9.refs_1_, bf16[160,1024]{1,0:T(8,128)(2,1)S(1)} %collective-permute-done.10.refs_2_, ...), custom_call_target="tpu_custom_call" | custom-call | tf_op jit(solution)/shard_map/pallas_call | solution.py:347
  (26 shorter events, 2.3 us)
Async XLA Ops:
  0.6 6.7 %copy-start = (bf16[2,64,4096]{2,1,0:T(8,128)(2,1)S(1)}, bf16[2,64,4096]{2,1,0:T(8,128)(2,1)}, u32[]{:S(2)}) copy-start(bf16[2,64,4096]{2,1,0:T(8,128)(2,1)} %queries.1) | copy-start | bytes 3145732
  0.6 1.0 copy-start.2
  2.4 10.4 %all-to-all-start = ((bf16[4,16,2048]{2,1,0:T(8,128)(2,1)}), bf16[4,16,2048]{2,1,0:T(8,128)(2,1)S(1)}, u32[]{:S(2)}, u32[]{:S(2)}) async-start(bf16[4,16,2048]{2,1,0:T(8,128)(2,1)} %shard_map.120), calls=%async_computation | async-start | bytes 524288 | tf_op jit(solution)/shard_map/all_to_all | solution.py:282
  7.3 1.2 %copy-start.1 = (bf16[2,64,4096]{2,1,0:T(8,128)(2,1)S(1)}, bf16[2,64,4096]{2,1,0:T(8,128)(2,1)}, u32[]{:S(2)}) copy-start(bf16[2,64,4096]{2,1,0:T(8,128)(2,1)} %cotangent.1) | copy-start | bytes 3145732
  8.5 38.5 %copy-start.3 = (f32[4,16,128]{2,1,0:T(8,128)S(1)}, f32[4,16,128]{2,1,0:T(8,128)}, u32[]{:S(2)}) copy-start(f32[4,16,128]{2,1,0:T(8,128)} %lambdas.3) | copy-start | bytes 98308
  8.5 38.6 %copy-start.6 = (s32[2]{0:T(128)S(1)}, s32[2]{0:T(128)}, u32[]{:S(2)}) copy-start(s32[2]{0:T(128)} %counts.1) | copy-start | bytes 28
  12.8 18.5 %collective-permute-start.5 = (bf16[4,16,2048]{2,1,0:T(8,128)(2,1)S(1)}, bf16[4,16,2048]{2,1,0:T(8,128)(2,1)S(1)}, u32[]{:S(2)}, u32[]{:S(2)}) collective-permute-start(bf16[4,16,2048]{2,1,0:T(8,128)(2,1)S(1)} %all-to-all-done.refs_4_), channel_id=1, source_target_pairs={{0,8},{4,12},{8,0},{12,4},{1,9},{5,13},{9,1},{13,5},{2,10},{6,14},... | collective-permute-start | bytes 786440 | tf_op jit(solution)/shard_map/ppermute | solution.py:261
  18.6 23.6 %collective-permute-start = (bf16[2,64,2048]{2,1,0:T(8,128)(2,1)S(1)}, bf16[2,64,2048]{2,1,0:T(8,128)(2,1)S(1)}, u32[]{:S(2)}, u32[]{:S(2)}) collective-permute-start(bf16[2,64,2048]{2,1,0:T(8,128)(2,1)S(1)} %get-tuple-element.28), channel_id=1, source_target_pairs={{0,2},{1,3},{2,0},{3,1},{4,6},{5,7},{6,4},{7,5},{8,10},{9,11},{10,... | collective-permute-start | bytes 1572872 | tf_op jit(solution)/shard_map/ppermute | solution.py:261
  20.8 26.3 %collective-permute-start.1 = (bf16[2,64,2048]{2,1,0:T(8,128)(2,1)S(1)}, bf16[2,64,2048]{2,1,0:T(8,128)(2,1)S(1)}, u32[]{:S(2)}, u32[]{:S(2)}) collective-permute-start(bf16[2,64,2048]{2,1,0:T(8,128)(2,1)S(1)} %get-tuple-element.29), channel_id=1, source_target_pairs={{0,1},{1,2},{2,3},{3,0},{4,5},{5,6},{6,7},{7,4},{8,9},{9,10},{10,1... | collective-permute-start | bytes 1572872 | tf_op jit(solution)/shard_map/ppermute | solution.py:261
  23.9 23.2 %collective-permute-start.2 = (bf16[2,64,2048]{2,1,0:T(8,128)(2,1)S(1)}, bf16[2,64,2048]{2,1,0:T(8,128)(2,1)S(1)}, u32[]{:S(2)}, u32[]{:S(2)}) collective-permute-start(bf16[2,64,2048]{2,1,0:T(8,128)(2,1)S(1)} %get-tuple-element.30), channel_id=1, source_target_pairs={{0,3},{1,0},{2,1},{3,2},{4,7},{5,4},{6,5},{7,6},{8,11},{9,8},{10,9... | collective-permute-start | bytes 1572872 | tf_op jit(solution)/shard_map/ppermute | solution.py:261
  27.3 9.5 %collective-permute-start.4 = (bf16[4,16,2048]{2,1,0:T(8,128)(2,1)S(1)}, bf16[4,16,2048]{2,1,0:T(8,128)(2,1)S(1)}, u32[]{:S(2)}, u32[]{:S(2)}) collective-permute-start(bf16[4,16,2048]{2,1,0:T(8,128)(2,1)S(1)} %all-to-all-done.refs_4_), channel_id=1, source_target_pairs={{0,4},{4,8},{8,12},{12,0},{1,5},{5,9},{9,13},{13,1},{2,6},{6,10},{... | collective-permute-start | bytes 786440 | tf_op jit(solution)/shard_map/ppermute | solution.py:261
  31.3 10.9 %collective-permute-start.3 = (bf16[4,16,2048]{2,1,0:T(8,128)(2,1)S(1)}, bf16[4,16,2048]{2,1,0:T(8,128)(2,1)S(1)}, u32[]{:S(2)}, u32[]{:S(2)}) collective-permute-start(bf16[4,16,2048]{2,1,0:T(8,128)(2,1)S(1)} %all-to-all-done.refs_4_), channel_id=1, source_target_pairs={{0,12},{4,0},{8,4},{12,8},{1,13},{5,1},{9,5},{13,9},{2,14},{6,2},{... | collective-permute-start | bytes 786440 | tf_op jit(solution)/shard_map/ppermute | solution.py:261
  47.1 0.7 copy-start.4
  47.1 0.7 copy-start.5
  56.4 26.1 %collective-permute-start.6 = (bf16[4,16,2048]{2,1,0:T(8,128)(2,1)S(1)}, bf16[4,16,2048]{2,1,0:T(8,128)(2,1)S(1)}, u32[]{:S(2)}, u32[]{:S(2)}) collective-permute-start(bf16[4,16,2048]{2,1,0:T(8,128)(2,1)S(1)} %get-tuple-element.33), channel_id=1, source_target_pairs={{0,8},{4,12},{8,0},{12,4},{1,9},{5,13},{9,1},{13,5},{2,10},{6,14},... | collective-permute-start | bytes 786440 | tf_op jit(solution)/shard_map/ppermute | solution.py:261
  58.4 24.2 %collective-permute-start.7 = (bf16[4,16,2048]{2,1,0:T(8,128)(2,1)S(1)}, bf16[4,16,2048]{2,1,0:T(8,128)(2,1)S(1)}, u32[]{:S(2)}, u32[]{:S(2)}) collective-permute-start(bf16[4,16,2048]{2,1,0:T(8,128)(2,1)S(1)} %get-tuple-element.34), channel_id=1, source_target_pairs={{0,12},{4,0},{8,4},{12,8},{1,13},{5,1},{9,5},{13,9},{2,14},{6,2},{... | collective-permute-start | bytes 786440 | tf_op jit(solution)/shard_map/ppermute | solution.py:261
  64.5 18.1 %collective-permute-start.8 = (bf16[4,16,2048]{2,1,0:T(8,128)(2,1)S(1)}, bf16[4,16,2048]{2,1,0:T(8,128)(2,1)S(1)}, u32[]{:S(2)}, u32[]{:S(2)}) collective-permute-start(bf16[4,16,2048]{2,1,0:T(8,128)(2,1)S(1)} %get-tuple-element.35), channel_id=1, source_target_pairs={{0,4},{4,8},{8,12},{12,0},{1,5},{5,9},{9,13},{13,1},{2,6},{6,10},{... | collective-permute-start | bytes 786440 | tf_op jit(solution)/shard_map/ppermute | solution.py:261
  83.7 28.0 %collective-permute-start.9 = (bf16[160,1024]{1,0:T(8,128)(2,1)S(1)}, bf16[160,1024]{1,0:T(8,128)(2,1)S(1)}, u32[]{:S(2)}, u32[]{:S(2)}) collective-permute-start(bf16[160,1024]{1,0:T(8,128)(2,1)S(1)} %get-tuple-element.41), channel_id=1, source_target_pairs={{0,2},{1,3},{2,0},{3,1},{4,6},{5,7},{6,4},{7,5},{8,10},{9,11},{10,... | collective-permute-start | bytes 983048 | tf_op jit(solution)/shard_map/ppermute | solution.py:261
  86.5 25.2 %collective-permute-start.10 = (bf16[160,1024]{1,0:T(8,128)(2,1)S(1)}, bf16[160,1024]{1,0:T(8,128)(2,1)S(1)}, u32[]{:S(2)}, u32[]{:S(2)}) collective-permute-start(bf16[160,1024]{1,0:T(8,128)(2,1)S(1)} %get-tuple-element.42), channel_id=1, source_target_pairs={{0,3},{1,0},{2,1},{3,2},{4,7},{5,4},{6,5},{7,6},{8,11},{9,8},{10,9... | collective-permute-start | bytes 983048 | tf_op jit(solution)/shard_map/ppermute | solution.py:261
  90.0 21.6 %collective-permute-start.11 = (bf16[160,1024]{1,0:T(8,128)(2,1)S(1)}, bf16[160,1024]{1,0:T(8,128)(2,1)S(1)}, u32[]{:S(2)}, u32[]{:S(2)}) collective-permute-start(bf16[160,1024]{1,0:T(8,128)(2,1)S(1)} %get-tuple-element.43), channel_id=1, source_target_pairs={{0,1},{1,2},{2,3},{3,0},{4,5},{5,6},{6,7},{7,4},{8,9},{9,10},{10,1... | collective-permute-start | bytes 983048 | tf_op jit(solution)/shard_map/ppermute | solution.py:261

commit v3 on v2

--- a/solution.py
+++ b/solution.py
@@ -42,24 +42,23 @@
         ]
 
 
-def pack_text_body(place, queries, cotangent, *refs):
-    outs, sems = refs[:-1], refs[-1]
+def pack_text_body(queries, cotangent, out, sems):
     half = queries.shape[2] // 2
     width = half // PARTS
     copies = []
-    for n, shift in enumerate(ORDER):
-        g = wrap(place[1] + shift)
-        first = pl.multiple_of(g * width, width)
-        second = pl.multiple_of(half + g * width, width)
-        wide = pl.multiple_of(g * 2 * width, 2 * width)
+    for g in range(PARTS):
         pieces = (
-            (queries.at[:, :, pl.ds(first, width)], pl.ds(0, width)),
-            (queries.at[:, :, pl.ds(second, width)], pl.ds(width, width)),
-            (cotangent.at[:, :, pl.ds(wide, 2 * width)], pl.ds(2 * width, 2 * width)),
+            (queries, g * width, 0, width),
+            (queries, half + g * width, width, width),
+            (cotangent, 2 * g * width, 2 * width, 2 * width),
         )
-        for i, (source, columns) in enumerate(pieces):
+        for i, (source, first, to, size) in enumerate(pieces):
             copies.append(
-                pltpu.make_async_copy(source, outs[n].at[:, :, columns], sems.at[n, i])
+                pltpu.make_async_copy(
+                    source.at[:, :, pl.ds(first, size)],
+                    out.at[g, :, :, pl.ds(to, size)],
+                    sems.at[g, i],
+                )
             )
     for copy in copies:
         copy.start()
@@ -70,11 +69,13 @@
 def attend_body(
     place, assignment, counts, lambdas, norm_gain, gate, *refs, heads, head_size, patch
 ):
-    text, vision, payload, grad_vision = (refs[i * PARTS : (i + 1) * PARTS] for i in range(4))
+    text = refs[0]
+    vision, payload, grad_vision = (refs[1 + i * PARTS : 1 + (i + 1) * PARTS] for i in range(3))
     vision = [vision[LATE.index(k)] for k in range(PARTS)]
-    stats = refs[4 * PARTS]
+    stats = refs[1 + 3 * PARTS]
     zl, x = place[0], place[1]
-    seqs, toks = text[0].shape[0], text[0].shape[1]
+    seqs, toks = text.shape[1:3]
+    sources = [wrap(x - k) for k in ORDER]
     frames = PARTS * PARTS
     keys = frames * patch
     width = heads * head_size
@@ -116,7 +117,7 @@
             key_rows, query_rows, probs = [], [], []
             for m in range(2):
                 k = of_video(wide_keys[m], v)
-                q = jnp.concatenate([t[s, :, map_columns[m]] for t in text], axis=0)
+                q = jnp.concatenate([text[i, s, :, map_columns[m]] for i in sources], axis=0)
                 scores = dot(q, k, (1, 1)) * scale
                 scores = jnp.where(usable, scores, -jnp.inf)
                 shifted = jnp.exp(scores - jnp.max(scores, axis=-1, keepdims=True))
@@ -129,7 +130,9 @@
                 jnp.mean(attended * attended, axis=-1, keepdims=True) + epsilon
             )
             normed = attended * inverse_rms
-            grad_out = jnp.concatenate([t[s, :, value_columns] for t in text], axis=0).astype(f32)
+            grad_out = jnp.concatenate(
+                [text[i, s, :, value_columns] for i in sources], axis=0
+            ).astype(f32)
             raw_gain = raw_gain + jnp.sum(grad_out * normed, axis=0, keepdims=True)
             scaled = grad_out * gain_row
             grad_attended = (
@@ -200,31 +203,11 @@
         out[i] = total
 
 
-def finish_body(tiles, lambdas, norm_gain, gate, grad_lambdas, grad_gain, grad_gate):
-    total = jnp.sum(tiles[...], axis=0)
-    head_count, head_size = lambdas.shape[1:]
-    gate_tanh = jnp.tanh(gate[...])
-    grad_gain[...] = total[:2] * (gate_tanh * (1.0 - rate_offset))
-    weighed = jnp.sum(total[:2] * norm_gain[...], axis=-1, keepdims=True)
-    grad_gate[...] = (
-        jnp.sum(weighed, axis=0, keepdims=True)
-        * (1.0 - rate_offset)
-        * (1.0 - gate_tanh * gate_tanh)
-    )
-    shape = (head_count, head_size)
-    own = lax.broadcasted_iota(jnp.int32, shape, 0) == lax.broadcasted_iota(jnp.int32, shape, 1)
-    grad_rate = jnp.sum(jnp.where(own, total[2:3], 0.0), axis=-1, keepdims=True)
-    first_exp = jnp.exp(jnp.sum(lambdas[0] * lambdas[1], axis=-1, keepdims=True))
-    second_exp = jnp.exp(jnp.sum(lambdas[2] * lambdas[3], axis=-1, keepdims=True))
-    weight_one, weight_two = grad_rate * first_exp, grad_rate * second_exp
-    grad_lambdas[0] = weight_one * lambdas[1]
-    grad_lambdas[1] = weight_one * lambdas[0]
-    grad_lambdas[2] = -weight_two * lambdas[3]
-    grad_lambdas[3] = -weight_two * lambdas[2]
-
-
-def unpack_body(place, *refs):
-    parts, grad_queries, grad_vision, sems = refs[:PARTS], refs[PARTS], refs[PARTS + 1], refs[-1]
+def finish_body(place, tiles, lambdas, norm_gain, gate, *refs):
+    parts, grad_queries, grad_vision, grad_lambdas, grad_gain, grad_gate, sems = (
+        refs[:PARTS],
+        *refs[PARTS:],
+    )
     text_rows, rows = grad_queries.shape[0], grad_vision.shape[0]
     half = grad_queries.shape[1] // 2
     width = half // PARTS
@@ -252,6 +235,26 @@
             )
     for copy in copies:
         copy.start()
+    total = jnp.sum(tiles[...], axis=0)
+    head_count, head_size = lambdas.shape[1:]
+    gate_tanh = jnp.tanh(gate[...])
+    grad_gain[...] = total[:2] * (gate_tanh * (1.0 - rate_offset))
+    weighed = jnp.sum(total[:2] * norm_gain[...], axis=-1, keepdims=True)
+    grad_gate[...] = (
+        jnp.sum(weighed, axis=0, keepdims=True)
+        * (1.0 - rate_offset)
+        * (1.0 - gate_tanh * gate_tanh)
+    )
+    shape = (head_count, head_size)
+    own = lax.broadcasted_iota(jnp.int32, shape, 0) == lax.broadcasted_iota(jnp.int32, shape, 1)
+    grad_rate = jnp.sum(jnp.where(own, total[2:3], 0.0), axis=-1, keepdims=True)
+    first_exp = jnp.exp(jnp.sum(lambdas[0] * lambdas[1], axis=-1, keepdims=True))
+    second_exp = jnp.exp(jnp.sum(lambdas[2] * lambdas[3], axis=-1, keepdims=True))
+    weight_one, weight_two = grad_rate * first_exp, grad_rate * second_exp
+    grad_lambdas[0] = weight_one * lambdas[1]
+    grad_lambdas[1] = weight_one * lambdas[0]
+    grad_lambdas[2] = -weight_two * lambdas[3]
+    grad_lambdas[3] = -weight_two * lambdas[2]
     for copy in copies:
         copy.wait()
 
@@ -299,12 +302,12 @@
     row_vision = exchange(sent_vision, "x")
     sent_text = kernel(
         pack_text_body,
-        [shaped((seqs, toks, 2 * text_columns // PARTS))] * PARTS,
-        [SMEM, ANY, ANY],
-        [ANY] * PARTS,
+        shaped((PARTS, seqs, toks, 2 * text_columns // PARTS)),
+        [ANY] * 2,
+        ANY,
         scratch_shapes=[pltpu.SemaphoreType.DMA((PARTS, 3))],
-    )(place, queries, cotangent)
-    held_text = shift_all(sent_text, "x", ORDER, 1)
+    )(queries, cotangent)
+    held_text = exchange(sent_text, "x")
     held_vision = shift_all([row_vision] * PARTS, "zl", LATE, 1)
 
     grads = kernel(
@@ -312,7 +315,7 @@
         [shaped((seqs * toks + 2 * rows, text_columns // PARTS))] * PARTS
         + [slab] * PARTS
         + [shaped((FIRST, 4, head_size), f32)],
-        [SMEM] * 3 + [VMEM] * (3 + 2 * PARTS),
+        [SMEM] * 3 + [VMEM] * (4 + PARTS),
         [VMEM] * (2 * PARTS + 1),
     )(
         place,
@@ -321,12 +324,12 @@
         lambdas,
         norm_gain.reshape(1, -1),
         gate,
-        *held_text,
+        held_text,
         *held_vision,
     )
     payload, grad_vision, stats = grads[:PARTS], grads[PARTS : 2 * PARTS], grads[2 * PARTS]
 
-    back_vision = shift_all([grad_vision[k] for k in ORDER], "zl", ORDER, -1)
+    back_vision = shift_all(grad_vision, "zl", range(PARTS), -1)
     stats = exchange(stats, ("y", "x"))
     payload = kernel(
         sum_vision_body,
@@ -344,20 +347,19 @@
         stats, payload[0]
     )
     stats = exchange(stats, ("zh", "core", "zl"))
-    grad_queries, grad_vision = kernel(
-        unpack_body,
-        [shaped((seqs * toks, text_columns)), shaped((rows, vision_columns))],
-        [SMEM] + [ANY] * PARTS,
-        [ANY] * 2,
+    grad_queries, grad_vision, grad_lambdas, grad_gain, grad_gate = kernel(
+        finish_body,
+        [
+            shaped((seqs * toks, text_columns)),
+            shaped((rows, vision_columns)),
+            shaped(lambdas.shape, f32),
+            shaped(gain_rows.shape, f32),
+            shaped((1, 1), f32),
+        ],
+        [SMEM] + [VMEM] * 4 + [ANY] * PARTS,
+        [ANY] * 2 + [VMEM] * 3,
         scratch_shapes=[pltpu.SemaphoreType.DMA((PARTS, 5))],
-    )(place, *back)
-
-    grad_lambdas, grad_gain, grad_gate = kernel(
-        finish_body,
-        [shaped(lambdas.shape, f32), shaped(gain_rows.shape, f32), shaped((1, 1), f32)],
-        [VMEM] * 4,
-        [VMEM] * 3,
-    )(stats, lambdas, gain_rows, gate)
+    )(place, stats, lambdas, gain_rows, gate, *back)
     return (
         grad_queries.reshape(queries.shape),
         grad_vision.reshape(vision.shape),

time: 114 us -> 114 us (level)
  starting transfers between devices: 46.3 us -> 42.4 us
  blocking collectives: 35.1 us -> 37.1 us
  local copies, waits for them, and re-layouts: 2.93 us -> 4.72 us
    ppermute x12 -> x9, starting transfers between devices: 41.5 us -> 33.9 us  [shift_all(): lax.ppermute(part, axis, [(i, (i + way * k) % PARTS) for i in range(PARTS)])]
    all_to_all x1 -> x2, starting transfers between devices: 4.84 us -> 8.45 us  [exchange(): return lax.all_to_all(value, axes, 0, 0, tiled=True)]
    ppermute x12 -> x9, waiting for transfers between devices: 10.3 us -> 13.3 us  [shift_all(): lax.ppermute(part, axis, [(i, (i + way * k) % PARTS) for i in range(PARTS)])]
    all_to_all x2, blocking collectives: 35.1 us -> 37.1 us  [exchange(): return lax.all_to_all(value, axes, 0, 0, tiled=True)]
    all_to_all x1 -> x2, waiting for transfers between devices: 3.29 us -> 1.38 us  [exchange(): return lax.all_to_all(value, axes, 0, 0, tiled=True)]
    unnamed x14 -> x16, local copies, waits for them, and re-layouts: 2.93 us -> 4.72 us
    pallas_call x3 -> x2, Pallas kernels: 3.41 us -> 2.76 us  [the longest x1 2.4 us: shards(): kernel(finish_body, [shaped((seqs * toks, text_columns)), shaped((rows, v...]
  transfers between devices with their start and end apart: 13 -> 11, of which waited for: 3 -> 3; matrix products, arithmetic and copies ran while one was open for 0% -> 0% of each run, Pallas kernels for 1% -> 0%
where the time goes in v3:
time: 114 us
  starting transfers between devices  42.4 us (37%)
  blocking collectives  37.1 us (33%)
  waiting for transfers between devices  14.7 us (13%)
  Pallas kernels  13.3 us (12%)
  local copies, waits for them, and re-layouts  4.72 us (4%)
  between operations  1.44 us (1%)
    all_to_all x2, blocking collectives, exchange(): return lax.all_to_all(value, axes, 0, 0, tiled=True)  37.1 us
    ppermute x9, starting transfers between devices, shift_all(): lax.ppermute(part, axis, [(i, (i + way * k) % PARTS) for i in range(PARTS)])  33.9 us
    ppermute x9, waiting for transfers between devices, shift_all(): lax.ppermute(part, axis, [(i, (i + way * k) % PARTS) for i in range(PARTS)])  13.3 us
    pallas_call x1, Pallas kernels, shards(): kernel(functools.partial(attend_body, heads=heads, head_size=head_size, p...  8.68 us
    all_to_all x2, starting transfers between devices, exchange(): return lax.all_to_all(value, axes, 0, 0, tiled=True)  8.45 us
    unnamed x16, local copies, waits for them, and re-layouts  4.72 us
    pallas_call x1, Pallas kernels, shards(): kernel(finish_body, [shaped((seqs * toks, text_columns)), shaped((rows, v...  2.4 us
  transfers between devices with their start and end apart: 11, of which 3 were waited for; matrix products, arithmetic and copies ran while one was open for 0% of the time, Pallas kernels for 0%

profile of v3, /device:TPU:1, one launch (start us, length us, event | category | flops | bytes accessed | tf_op | source)
XLA Modules:
  0.0 113.7 jit_solution(12787196003231178664)
XLA Ops:
  0.6 0.9 copy-done.3
  1.6 0.7 shard_map.120
  2.3 4.8 %all-to-all-start.1 = ((bf16[4,16,2048]{2,1,0:T(8,128)(2,1)}), bf16[4,16,2048]{2,1,0:T(8,128)(2,1)S(1)}, u32[]{:S(2)}, u32[]{:S(2)}) async-start(bf16[4,16,2048]{2,1,0:T(8,128)(2,1)} %shard_map.120), calls=%async_computation.1 | async-start | bytes 524288 | tf_op jit(solution)/shard_map/all_to_all | solution.py:285
  7.1 1.2 %copy-done.1 = bf16[2,64,4096]{2,1,0:T(8,128)(2,1)S(1)} copy-done((bf16[2,64,4096]{2,1,0:T(8,128)(2,1)S(1)}, bf16[2,64,4096]{2,1,0:T(8,128)(2,1)}, u32[]{:S(2)}) %copy-start.1) | copy-done | bytes 1048600
  8.4 1.2 %copy-done.2 = bf16[2,64,4096]{2,1,0:T(8,128)(2,1)S(1)} copy-done((bf16[2,64,4096]{2,1,0:T(8,128)(2,1)S(1)}, bf16[2,64,4096]{2,1,0:T(8,128)(2,1)}, u32[]{:S(2)}) %copy-start.2) | copy-done | bytes 1048600
  10.0 1.3 %copy-done = bf16[4,2,64,2048]{3,2,1,0:T(8,128)(2,1)} copy-done((bf16[4,2,64,2048]{3,2,1,0:T(8,128)(2,1)}, bf16[4,2,64,2048]{3,2,1,0:T(8,128)(2,1)S(1)}, u32[]{:S(2)}) %copy-start) | copy-done | bytes 2097176
  11.3 1.4 %all-to-all-done.1.refs_1_ = bf16[4,16,2048]{2,1,0:T(8,128)(2,1)S(1)} async-done(((bf16[4,16,2048]{2,1,0:T(8,128)(2,1)}), bf16[4,16,2048]{2,1,0:T(8,128)(2,1)S(1)}, u32[]{:S(2)}, u32[]{:S(2)}) %all-to-all-start.1) | async-done | bytes 262176 | tf_op jit(solution)/shard_map/all_to_all | solution.py:285
  12.7 3.6 %all-to-all-start = ((bf16[4,2,64,2048]{3,2,1,0:T(8,128)(2,1)}), bf16[4,2,64,2048]{3,2,1,0:T(8,128)(2,1)S(1)}, u32[]{:S(2)}, u32[]{:S(2)}) async-start(bf16[4,2,64,2048]{3,2,1,0:T(8,128)(2,1)} %copy-done), calls=%async_computation | async-start | bytes 4194304 | tf_op jit(solution)/shard_map/all_to_all | solution.py:285
  16.3 5.8 %collective-permute-start.2 = (bf16[4,16,2048]{2,1,0:T(8,128)(2,1)S(1)}, bf16[4,16,2048]{2,1,0:T(8,128)(2,1)S(1)}, u32[]{:S(2)}, u32[]{:S(2)}) collective-permute-start(bf16[4,16,2048]{2,1,0:T(8,128)(2,1)S(1)} %all-to-all-done.1.refs_1_), channel_id=1, source_target_pairs={{0,8},{4,12},{8,0},{12,4},{1,9},{5,13},{9,1},{13,5},{2,10},{6,14},... | collective-permute-start | bytes 786440 | tf_op jit(solution)/shard_map/ppermute | solution.py:264
  22.1 4.0 %collective-permute-start.1 = (bf16[4,16,2048]{2,1,0:T(8,128)(2,1)S(1)}, bf16[4,16,2048]{2,1,0:T(8,128)(2,1)S(1)}, u32[]{:S(2)}, u32[]{:S(2)}) collective-permute-start(bf16[4,16,2048]{2,1,0:T(8,128)(2,1)S(1)} %all-to-all-done.1.refs_1_), channel_id=1, source_target_pairs={{0,4},{4,8},{8,12},{12,0},{1,5},{5,9},{9,13},{13,1},{2,6},{6,10},{... | collective-permute-start | bytes 786440 | tf_op jit(solution)/shard_map/ppermute | solution.py:264
  26.1 3.1 %collective-permute-start = (bf16[4,16,2048]{2,1,0:T(8,128)(2,1)S(1)}, bf16[4,16,2048]{2,1,0:T(8,128)(2,1)S(1)}, u32[]{:S(2)}, u32[]{:S(2)}) collective-permute-start(bf16[4,16,2048]{2,1,0:T(8,128)(2,1)S(1)} %all-to-all-done.1.refs_1_), channel_id=1, source_target_pairs={{0,12},{4,0},{8,4},{12,8},{1,13},{5,1},{9,5},{13,9},{2,14},{6,2},{... | collective-permute-start | bytes 786440 | tf_op jit(solution)/shard_map/ppermute | solution.py:264
  30.0 7.9 %collective-permute-done.2.refs_4_ = bf16[4,16,2048]{2,1,0:T(8,128)(2,1)S(1)} collective-permute-done((bf16[4,16,2048]{2,1,0:T(8,128)(2,1)S(1)}, bf16[4,16,2048]{2,1,0:T(8,128)(2,1)S(1)}, u32[]{:S(2)}, u32[]{:S(2)}) %collective-permute-start.2) | collective-permute-done | bytes 262176 | tf_op jit(solution)/shard_map/ppermute | solution.py:264
  37.8 5.4 %collective-permute-done.refs_2_ = bf16[4,16,2048]{2,1,0:T(8,128)(2,1)S(1)} collective-permute-done((bf16[4,16,2048]{2,1,0:T(8,128)(2,1)S(1)}, bf16[4,16,2048]{2,1,0:T(8,128)(2,1)S(1)}, u32[]{:S(2)}, u32[]{:S(2)}) %collective-permute-start) | collective-permute-done | bytes 262176 | tf_op jit(solution)/shard_map/ppermute | solution.py:264
  43.3 8.7 %shard_map.121 = (bf16[160,1024]{1,0:T(8,128)(2,1)S(1)}, bf16[160,1024]{1,0:T(8,128)(2,1)S(1)}, bf16[160,1024]{1,0:T(8,128)(2,1)S(1)}, bf16[160,1024]{1,0:T(8,12...) custom-call(s32[2]{0:T(128)S(1)} %pad_add_fusion.place, ...), custom_call_target="tpu_custom_call" | custom-call | tf_op jit(solution)/shard_map/pallas_call | solution.py:313
  52.0 4.9 %collective-permute-start.3 = (bf16[4,16,2048]{2,1,0:T(8,128)(2,1)S(1)}, bf16[4,16,2048]{2,1,0:T(8,128)(2,1)S(1)}, u32[]{:S(2)}, u32[]{:S(2)}) collective-permute-start(bf16[4,16,2048]{2,1,0:T(8,128)(2,1)S(1)} %get-tuple-element.25), channel_id=1, source_target_pairs={{0,12},{4,0},{8,4},{12,8},{1,13},{5,1},{9,5},{13,9},{2,14},{6,2},{... | collective-permute-start | bytes 786440 | tf_op jit(solution)/shard_map/ppermute | solution.py:264
  56.9 3.8 %collective-permute-start.4 = (bf16[4,16,2048]{2,1,0:T(8,128)(2,1)S(1)}, bf16[4,16,2048]{2,1,0:T(8,128)(2,1)S(1)}, u32[]{:S(2)}, u32[]{:S(2)}) collective-permute-start(bf16[4,16,2048]{2,1,0:T(8,128)(2,1)S(1)} %get-tuple-element.26), channel_id=1, source_target_pairs={{0,8},{4,12},{8,0},{12,4},{1,9},{5,13},{9,1},{13,5},{2,10},{6,14},... | collective-permute-start | bytes 786440 | tf_op jit(solution)/shard_map/ppermute | solution.py:264
  60.7 3.4 %collective-permute-start.5 = (bf16[4,16,2048]{2,1,0:T(8,128)(2,1)S(1)}, bf16[4,16,2048]{2,1,0:T(8,128)(2,1)S(1)}, u32[]{:S(2)}, u32[]{:S(2)}) collective-permute-start(bf16[4,16,2048]{2,1,0:T(8,128)(2,1)S(1)} %get-tuple-element.27), channel_id=1, source_target_pairs={{0,4},{4,8},{8,12},{12,0},{1,5},{5,9},{9,13},{13,1},{2,6},{6,10},{... | collective-permute-start | bytes 786440 | tf_op jit(solution)/shard_map/ppermute | solution.py:264
  64.1 18.5 %all_to_all.20.after.tiles = f32[32,4,128]{2,1,0:T(4,128)S(1)} all-to-all(f32[32,4,128]{2,1,0:T(4,128)S(1)} %get-tuple-element.23), channel_id=1, replica_groups=mesh['y'=8,'zh'=2,'core'=2,'zl'=4,'x'=4] {'y','x'}, dimensions={0} | all-to-all | bytes 131072 | tf_op jit(solution)/shard_map/all_to_all | solution.py:285
  82.6 1.1 shard_map.122
  83.7 3.6 %collective-permute-start.6 = (bf16[160,1024]{1,0:T(8,128)(2,1)S(1)}, bf16[160,1024]{1,0:T(8,128)(2,1)S(1)}, u32[]{:S(2)}, u32[]{:S(2)}) collective-permute-start(bf16[160,1024]{1,0:T(8,128)(2,1)S(1)} %get-tuple-element.33), channel_id=1, source_target_pairs={{0,2},{1,3},{2,0},{3,1},{4,6},{5,7},{6,4},{7,5},{8,10},{9,11},{10,... | collective-permute-start | bytes 983048 | tf_op jit(solution)/shard_map/ppermute | solution.py:264
  87.3 2.8 %collective-permute-start.7 = (bf16[160,1024]{1,0:T(8,128)(2,1)S(1)}, bf16[160,1024]{1,0:T(8,128)(2,1)S(1)}, u32[]{:S(2)}, u32[]{:S(2)}) collective-permute-start(bf16[160,1024]{1,0:T(8,128)(2,1)S(1)} %get-tuple-element.34), channel_id=1, source_target_pairs={{0,3},{1,0},{2,1},{3,2},{4,7},{5,4},{6,5},{7,6},{8,11},{9,8},{10,9... | collective-permute-start | bytes 983048 | tf_op jit(solution)/shard_map/ppermute | solution.py:264
  90.1 2.5 %collective-permute-start.8 = (bf16[160,1024]{1,0:T(8,128)(2,1)S(1)}, bf16[160,1024]{1,0:T(8,128)(2,1)S(1)}, u32[]{:S(2)}, u32[]{:S(2)}) collective-permute-start(bf16[160,1024]{1,0:T(8,128)(2,1)S(1)} %get-tuple-element.35), channel_id=1, source_target_pairs={{0,1},{1,2},{2,3},{3,0},{4,5},{5,6},{6,7},{7,4},{8,9},{9,10},{10,1... | collective-permute-start | bytes 983048 | tf_op jit(solution)/shard_map/ppermute | solution.py:264
  92.7 18.6 %all_to_all.21.tiles = f32[16,4,128]{2,1,0:T(4,128)S(1)} all-to-all(f32[16,4,128]{2,1,0:T(4,128)S(1)} %shard_map.123), channel_id=1, replica_groups=mesh['y'=8,'zh'=2,'core'=2,'zl'=4,'x'=4] {'zh','core','zl'}, dimensions={0} | all-to-all | bytes 65536 | tf_op jit(solution)/shard_map/all_to_all | solution.py:285
  111.3 2.4 %shard_map.124 = (bf16[128,4096]{1,0:T(8,128)(2,1)}, bf16[16,8192]{1,0:T(8,128)(2,1)}, f32[4,16,128]{2,1,0:T(8,128)}, f32[2,128]{1,0:T(2,128)}, f32[1,1]{1,0:T(1,128)}) custom-call(s32[2]{0:T(128)S(1)} %pad_add_fusion.place, f32[16,4,128]{2,1,0:T(4,128)S(1)} %all_to_all.21.tiles, f32[4,16,128]{2,1,0:T(8,128)S(1)} %copy-done.4, f32[2,128]{1,0:T(2,128)S(1)} %bitcast.16, ...), custom_call_target="tpu_custom_call" | custom-call | tf_op jit(solution)/shard_map/pallas_call | solution.py:350
  (23 shorter events, 0.5 us)
Async XLA Ops:
  0.6 1.0 copy-start.3
  2.3 10.4 %all-to-all-start.1 = ((bf16[4,16,2048]{2,1,0:T(8,128)(2,1)}), bf16[4,16,2048]{2,1,0:T(8,128)(2,1)S(1)}, u32[]{:S(2)}, u32[]{:S(2)}) async-start(bf16[4,16,2048]{2,1,0:T(8,128)(2,1)} %shard_map.120), calls=%async_computation.1 | async-start | bytes 524288 | tf_op jit(solution)/shard_map/all_to_all | solution.py:285
  7.1 1.2 %copy-start.1 = (bf16[2,64,4096]{2,1,0:T(8,128)(2,1)S(1)}, bf16[2,64,4096]{2,1,0:T(8,128)(2,1)}, u32[]{:S(2)}) copy-start(bf16[2,64,4096]{2,1,0:T(8,128)(2,1)} %queries.1) | copy-start | bytes 3145732
  8.4 1.2 %copy-start.2 = (bf16[2,64,4096]{2,1,0:T(8,128)(2,1)S(1)}, bf16[2,64,4096]{2,1,0:T(8,128)(2,1)}, u32[]{:S(2)}) copy-start(bf16[2,64,4096]{2,1,0:T(8,128)(2,1)} %cotangent.1) | copy-start | bytes 3145732
  10.0 1.3 %copy-start = (bf16[4,2,64,2048]{3,2,1,0:T(8,128)(2,1)}, bf16[4,2,64,2048]{3,2,1,0:T(8,128)(2,1)S(1)}, u32[]{:S(2)}) copy-start(bf16[4,2,64,2048]{3,2,1,0:T(8,128)(2,1)S(1)} %shard_map.119) | copy-start | bytes 6291460
  11.3 32.0 %copy-start.4 = (f32[4,16,128]{2,1,0:T(8,128)S(1)}, f32[4,16,128]{2,1,0:T(8,128)}, u32[]{:S(2)}) copy-start(f32[4,16,128]{2,1,0:T(8,128)} %lambdas.3) | copy-start | bytes 98308
  11.3 32.0 %copy-start.5 = (f32[256]{0:T(256)S(1)}, f32[256]{0:T(256)}, u32[]{:S(2)}) copy-start(f32[256]{0:T(256)} %param.14) | copy-start | bytes 3076
  11.3 32.0 %copy-start.6 = (s32[1,2]{1,0:T(1,128)S(1)}, s32[1,2]{1,0:T(1,128)}, u32[]{:S(2)}) copy-start(s32[1,2]{1,0:T(1,128)} %assignment.1) | copy-start | bytes 28
  11.3 32.0 %copy-start.7 = (s32[2]{0:T(128)S(1)}, s32[2]{0:T(128)}, u32[]{:S(2)}) copy-start(s32[2]{0:T(128)} %counts.1) | copy-start | bytes 28
  12.7 30.6 %all-to-all-start = ((bf16[4,2,64,2048]{3,2,1,0:T(8,128)(2,1)}), bf16[4,2,64,2048]{3,2,1,0:T(8,128)(2,1)S(1)}, u32[]{:S(2)}, u32[]{:S(2)}) async-start(bf16[4,2,64,2048]{3,2,1,0:T(8,128)(2,1)} %copy-done), calls=%async_computation | async-start | bytes 4194304 | tf_op jit(solution)/shard_map/all_to_all | solution.py:285
  16.3 21.6 %collective-permute-start.2 = (bf16[4,16,2048]{2,1,0:T(8,128)(2,1)S(1)}, bf16[4,16,2048]{2,1,0:T(8,128)(2,1)S(1)}, u32[]{:S(2)}, u32[]{:S(2)}) collective-permute-start(bf16[4,16,2048]{2,1,0:T(8,128)(2,1)S(1)} %all-to-all-done.1.refs_1_), channel_id=1, source_target_pairs={{0,8},{4,12},{8,0},{12,4},{1,9},{5,13},{9,1},{13,5},{2,10},{6,14},... | collective-permute-start | bytes 786440 | tf_op jit(solution)/shard_map/ppermute | solution.py:264
  22.1 15.7 %collective-permute-start.1 = (bf16[4,16,2048]{2,1,0:T(8,128)(2,1)S(1)}, bf16[4,16,2048]{2,1,0:T(8,128)(2,1)S(1)}, u32[]{:S(2)}, u32[]{:S(2)}) collective-permute-start(bf16[4,16,2048]{2,1,0:T(8,128)(2,1)S(1)} %all-to-all-done.1.refs_1_), channel_id=1, source_target_pairs={{0,4},{4,8},{8,12},{12,0},{1,5},{5,9},{9,13},{13,1},{2,6},{6,10},{... | collective-permute-start | bytes 786440 | tf_op jit(solution)/shard_map/ppermute | solution.py:264
  26.1 17.1 %collective-permute-start = (bf16[4,16,2048]{2,1,0:T(8,128)(2,1)S(1)}, bf16[4,16,2048]{2,1,0:T(8,128)(2,1)S(1)}, u32[]{:S(2)}, u32[]{:S(2)}) collective-permute-start(bf16[4,16,2048]{2,1,0:T(8,128)(2,1)S(1)} %all-to-all-done.1.refs_1_), channel_id=1, source_target_pairs={{0,12},{4,0},{8,4},{12,8},{1,13},{5,1},{9,5},{13,9},{2,14},{6,2},{... | collective-permute-start | bytes 786440 | tf_op jit(solution)/shard_map/ppermute | solution.py:264
  52.0 30.6 %collective-permute-start.3 = (bf16[4,16,2048]{2,1,0:T(8,128)(2,1)S(1)}, bf16[4,16,2048]{2,1,0:T(8,128)(2,1)S(1)}, u32[]{:S(2)}, u32[]{:S(2)}) collective-permute-start(bf16[4,16,2048]{2,1,0:T(8,128)(2,1)S(1)} %get-tuple-element.25), channel_id=1, source_target_pairs={{0,12},{4,0},{8,4},{12,8},{1,13},{5,1},{9,5},{13,9},{2,14},{6,2},{... | collective-permute-start | bytes 786440 | tf_op jit(solution)/shard_map/ppermute | solution.py:264
  56.9 25.7 %collective-permute-start.4 = (bf16[4,16,2048]{2,1,0:T(8,128)(2,1)S(1)}, bf16[4,16,2048]{2,1,0:T(8,128)(2,1)S(1)}, u32[]{:S(2)}, u32[]{:S(2)}) collective-permute-start(bf16[4,16,2048]{2,1,0:T(8,128)(2,1)S(1)} %get-tuple-element.26), channel_id=1, source_target_pairs={{0,8},{4,12},{8,0},{12,4},{1,9},{5,13},{9,1},{13,5},{2,10},{6,14},... | collective-permute-start | bytes 786440 | tf_op jit(solution)/shard_map/ppermute | solution.py:264
  60.7 21.9 %collective-permute-start.5 = (bf16[4,16,2048]{2,1,0:T(8,128)(2,1)S(1)}, bf16[4,16,2048]{2,1,0:T(8,128)(2,1)S(1)}, u32[]{:S(2)}, u32[]{:S(2)}) collective-permute-start(bf16[4,16,2048]{2,1,0:T(8,128)(2,1)S(1)} %get-tuple-element.27), channel_id=1, source_target_pairs={{0,4},{4,8},{8,12},{12,0},{1,5},{5,9},{9,13},{13,1},{2,6},{6,10},{... | collective-permute-start | bytes 786440 | tf_op jit(solution)/shard_map/ppermute | solution.py:264
  83.7 27.6 %collective-permute-start.6 = (bf16[160,1024]{1,0:T(8,128)(2,1)S(1)}, bf16[160,1024]{1,0:T(8,128)(2,1)S(1)}, u32[]{:S(2)}, u32[]{:S(2)}) collective-permute-start(bf16[160,1024]{1,0:T(8,128)(2,1)S(1)} %get-tuple-element.33), channel_id=1, source_target_pairs={{0,2},{1,3},{2,0},{3,1},{4,6},{5,7},{6,4},{7,5},{8,10},{9,11},{10,... | collective-permute-start | bytes 983048 | tf_op jit(solution)/shard_map/ppermute | solution.py:264
  87.3 23.9 %collective-permute-start.7 = (bf16[160,1024]{1,0:T(8,128)(2,1)S(1)}, bf16[160,1024]{1,0:T(8,128)(2,1)S(1)}, u32[]{:S(2)}, u32[]{:S(2)}) collective-permute-start(bf16[160,1024]{1,0:T(8,128)(2,1)S(1)} %get-tuple-element.34), channel_id=1, source_target_pairs={{0,3},{1,0},{2,1},{3,2},{4,7},{5,4},{6,5},{7,6},{8,11},{9,8},{10,9... | collective-permute-start | bytes 983048 | tf_op jit(solution)/shard_map/ppermute | solution.py:264
  90.1 21.1 %collective-permute-start.8 = (bf16[160,1024]{1,0:T(8,128)(2,1)S(1)}, bf16[160,1024]{1,0:T(8,128)(2,1)S(1)}, u32[]{:S(2)}, u32[]{:S(2)}) collective-permute-start(bf16[160,1024]{1,0:T(8,128)(2,1)S(1)} %get-tuple-element.35), channel_id=1, source_target_pairs={{0,1},{1,2},{2,3},{3,0},{4,5},{5,6},{6,7},{7,4},{8,9},{9,10},{10,1... | collective-permute-start | bytes 983048 | tf_op jit(solution)/shard_map/ppermute | solution.py:264

commit v4 on v3

--- a/solution.py
+++ b/solution.py
@@ -11,8 +11,9 @@
 epsilon = 1e-05
 DP = ("y", "zh", "core")
 IMAGE = ("zl", "x")
-FIRST, SECOND = 32, 16
+FIRST, SECOND = 16, 32
 PARTS = 4
+GROUP = 2
 ORDER, LATE = (0, 2, 1, 3), (0, 3, 1, 2)
 VMEM = pl.BlockSpec(memory_space=pltpu.VMEM)
 SMEM = pl.BlockSpec(memory_space=pltpu.SMEM)
@@ -72,98 +73,137 @@
     text = refs[0]
     vision, payload, grad_vision = (refs[1 + i * PARTS : 1 + (i + 1) * PARTS] for i in range(3))
     vision = [vision[LATE.index(k)] for k in range(PARTS)]
-    stats = refs[1 + 3 * PARTS]
+    stats, gain, bias, raw_gain = refs[1 + 3 * PARTS :]
     zl, x = place[0], place[1]
     seqs, toks = text.shape[1:3]
     sources = [wrap(x - k) for k in ORDER]
+    rows = PARTS * toks
     frames = PARTS * PARTS
     keys = frames * patch
     width = heads * head_size
+    wide = 2 * head_size
     scale = head_size ** (-0.5)
-    output_scale = jnp.tanh(gate[...]) * (1.0 - rate_offset)
-    gain_row = norm_gain[...] * output_scale
     first_exp = jnp.exp(jnp.sum(lambdas[0] * lambdas[1], axis=-1, keepdims=True))
     second_exp = jnp.exp(jnp.sum(lambdas[2] * lambdas[3], axis=-1, keepdims=True))
     all_rates = first_exp - second_exp + rate_offset
     head_index = lax.broadcasted_iota(jnp.int32, all_rates.shape, 0)
-    spot = lax.broadcasted_iota(jnp.int32, (1, keys), 1) // patch
+    shape = (wide, wide)
+    diagonal = lax.broadcasted_iota(jnp.int32, shape, 0) == lax.broadcasted_iota(
+        jnp.int32, shape, 1
+    )
+    eye = jnp.where(diagonal, 1.0, 0.0).astype(bf16)
+    gain_row = norm_gain[...] * (jnp.tanh(gate[...]) * (1.0 - rate_offset))
+    gain[...] = jnp.broadcast_to(
+        jnp.sum(jnp.where(diagonal, gain_row, 0.0), axis=1, keepdims=True), gain.shape
+    )
+    spot = lax.broadcasted_iota(jnp.int32, (keys, rows), 0) // patch
     part = spot // PARTS
     frame = wrap(zl - part) * PARTS + spot - part * PARTS
-    raw_gain = jnp.zeros((1, 2 * head_size), f32)
+    for v in range(seqs):
+        bias[v] = jnp.where(frame < counts[v], 0.0, -jnp.inf)
     lane = lax.broadcasted_iota(jnp.int32, (1, head_size), 1)
     rate_row = jnp.zeros((1, head_size), f32)
 
+    def map_columns(h, m):
+        return pl.ds(m * width + h * head_size, head_size)
+
+    def value_columns(h):
+        return pl.ds(2 * width + h * wide, wide)
+
     def block(columns):
-        wide = jnp.concatenate([part[:, :, columns] for part in vision], axis=0)
-        return wide.astype(f32).reshape(frames, seqs, patch, -1)
-
-    def of_video(wide, v):
-        return wide[:, v].reshape(keys, -1).astype(bf16)
-
-    for h in range(heads):
-        rate = jnp.sum(
-            jnp.where(head_index == x * heads + h, all_rates, 0.0), axis=0, keepdims=True
-        )
-        map_columns = [pl.ds(m * width + h * head_size, head_size) for m in range(2)]
-        value_columns = pl.ds(2 * width + 2 * h * head_size, 2 * head_size)
-        wide_keys = [block(c) for c in map_columns]
-        wide_values = block(value_columns)
-        grad_keys, grad_values = ([[], []], [])
-        total_rate = jnp.zeros((1, 1), f32)
-        for v in range(seqs):
-            s = jnp.where(assignment[0, 0] == v, 0, 1)
-            usable = frame < counts[v]
-            value_rows = of_video(wide_values, v)
-            key_rows, query_rows, probs = [], [], []
+        joined = jnp.concatenate([part[:, :, columns] for part in vision], axis=0)
+        return joined.astype(f32).reshape(frames, seqs, patch, -1)
+
+    def of_video(joined, v):
+        return joined[:, v].reshape(keys, -1).astype(bf16)
+
+    place_of = [jnp.where(assignment[0, 0] == v, 0, 1) for v in range(seqs)]
+    for first in range(0, heads, GROUP):
+        chains = [(h, v) for h in range(first, first + GROUP) for v in range(seqs)]
+        both = [(h, v, m) for h, v in chains for m in range(2)]
+        rates, joined = {}, {}
+        for h in range(first, first + GROUP):
+            rates[h] = jnp.sum(
+                jnp.where(head_index == x * heads + h, all_rates, 0.0), axis=0, keepdims=True
+            )
+            joined[h] = block(value_columns(h))
             for m in range(2):
-                k = of_video(wide_keys[m], v)
-                q = jnp.concatenate([text[i, s, :, map_columns[m]] for i in sources], axis=0)
-                scores = dot(q, k, (1, 1)) * scale
-                scores = jnp.where(usable, scores, -jnp.inf)
-                shifted = jnp.exp(scores - jnp.max(scores, axis=-1, keepdims=True))
-                probs.append(shifted / jnp.sum(shifted, axis=-1, keepdims=True))
-                key_rows.append(k)
-                query_rows.append(q)
-            mixed = (probs[0] - rate * probs[1]).astype(bf16)
-            attended = dot(mixed, value_rows, (1, 0))
-            inverse_rms = lax.rsqrt(
-                jnp.mean(attended * attended, axis=-1, keepdims=True) + epsilon
+                joined[h, m] = block(map_columns(h, m))
+        values = {(h, v): of_video(joined[h], v) for h, v in chains}
+        key_rows = {(h, v, m): of_video(joined[h, m], v) for h, v, m in both}
+        queries = {
+            (h, v, m): jnp.concatenate(
+                [text[i, place_of[v], :, map_columns(h, m)] for i in sources], axis=0
             )
-            normed = attended * inverse_rms
-            grad_out = jnp.concatenate(
-                [text[i, s, :, value_columns] for i in sources], axis=0
-            ).astype(f32)
-            raw_gain = raw_gain + jnp.sum(grad_out * normed, axis=0, keepdims=True)
-            scaled = grad_out * gain_row
-            grad_attended = (
-                inverse_rms
-                * (scaled - normed * jnp.mean(scaled * normed, axis=-1, keepdims=True))
+            for h, v, m in both
+        }
+        scores = {c: dot(key_rows[c], queries[c], (1, 1)) + bias[c[1]] for c in both}
+        shifted = {
+            c: jnp.exp((scores[c] - jnp.max(scores[c], axis=0, keepdims=True)) * scale)
+            for c in both
+        }
+        probs = {
+            c: shifted[c] * (1.0 / jnp.sum(shifted[c], axis=0, keepdims=True)) for c in both
+        }
+        rated = {c: rates[c[0]] * probs[(*c, 1)] for c in chains}
+        mixed = {c: (probs[(*c, 0)] - rated[c]).astype(bf16) for c in chains}
+        attended = {c: dot(values[c], mixed[c], (0, 0)) for c in chains}
+        grad_out = {
+            (h, v): dot(
+                eye,
+                jnp.concatenate(
+                    [text[i, place_of[v], :, value_columns(h)] for i in sources], axis=0
+                ),
+                (1, 1),
+            )
+            for h, v in chains
+        }
+        inverse_rms = {
+            c: lax.rsqrt(jnp.mean(attended[c] * attended[c], axis=0, keepdims=True) + epsilon)
+            for c in chains
+        }
+        grad_attended = {}
+        for c in chains:
+            normed = attended[c] * inverse_rms[c]
+            product = grad_out[c] * normed
+            halves = product[:, :head_size] + product[:, head_size:]
+            raw_gain[...] = halves if c == (0, 0) else raw_gain[...] + halves
+            middle = jnp.mean(product * gain[...], axis=0, keepdims=True)
+            grad_attended[c] = (
+                inverse_rms[c] * (grad_out[c] * gain[...] - normed * middle)
             ).astype(bf16)
-            grad_mixed = dot(grad_attended, value_rows, (1, 1))
-            grad_values.append(dot(mixed, grad_attended, (0, 0)).reshape(frames, patch, -1))
-            sums = [jnp.sum(grad_mixed * p, axis=-1, keepdims=True) for p in probs]
-            total_rate = total_rate - jnp.sum(sums[1], axis=0, keepdims=True)
-            factors = (scale, -rate * scale)
-            for m in range(2):
-                grad_scores = (probs[m] * (grad_mixed - sums[m]) * factors[m]).astype(bf16)
-                grad_query = dot(grad_scores, key_rows[m], (1, 0)).astype(bf16)
-                own_rows = pl.ds(pl.multiple_of(s * toks, toks), toks)
-                for i in range(PARTS):
-                    payload[i][own_rows, map_columns[m]] = grad_query[i * toks : (i + 1) * toks]
-                grad_key = dot(grad_scores, query_rows[m], (0, 0))
-                grad_keys[m].append(grad_key.reshape(frames, patch, -1))
-        for columns, parts in (
-            (map_columns[0], grad_keys[0]),
-            (map_columns[1], grad_keys[1]),
-            (value_columns, grad_values),
-        ):
-            joined = jnp.concatenate(parts, axis=1).astype(bf16)
-            for j in range(PARTS):
-                grad_vision[j][:, :, columns] = joined[j * PARTS : (j + 1) * PARTS]
-        rate_row = jnp.where(lane == x * heads + h, total_rate, rate_row)
+        grad_mixed = {c: dot(values[c], grad_attended[c], (1, 0)) * scale for c in chains}
+        grad_values = {c: dot(mixed[c], grad_attended[c], (1, 1)) for c in chains}
+        sums = {
+            c: jnp.sum(grad_mixed[c[:2]] * probs[c], axis=0, keepdims=True) for c in both
+        }
+        grad_scores = {}
+        for c in chains:
+            grad_scores[(*c, 0)] = (probs[(*c, 0)] * (grad_mixed[c] - sums[(*c, 0)])).astype(bf16)
+            grad_scores[(*c, 1)] = (rated[c] * (sums[(*c, 1)] - grad_mixed[c])).astype(bf16)
+        grad_keys = {c: dot(grad_scores[c], queries[c], (1, 0)) for c in both}
+        for h, v, m in both:
+            grad_query = dot(grad_scores[h, v, m], key_rows[h, v, m], (0, 0)).astype(bf16)
+            own_rows = pl.ds(pl.multiple_of(place_of[v] * toks, toks), toks)
+            for i in range(PARTS):
+                payload[i][own_rows, map_columns(h, m)] = grad_query[i * toks : (i + 1) * toks]
+        for h in range(first, first + GROUP):
+            for columns, parts in (
+                (map_columns(h, 0), [grad_keys[h, v, 0] for v in range(seqs)]),
+                (map_columns(h, 1), [grad_keys[h, v, 1] for v in range(seqs)]),
+                (value_columns(h), [grad_values[h, v] for v in range(seqs)]),
+            ):
+                parts = [p.reshape(frames, patch, -1) for p in parts]
+                total = jnp.concatenate(parts, axis=1).astype(bf16)
+                for j in range(PARTS):
+                    grad_vision[j][:, :, columns] = total[j * PARTS : (j + 1) * PARTS]
+            total_rate = sum(sums[h, v, 1] for v in range(seqs))
+            own_rate = jnp.sum(total_rate, axis=1, keepdims=True) * (-1.0 / scale)
+            rate_row = jnp.where(lane == x * heads + h, own_rate, rate_row)
+    gains = jnp.sum(raw_gain[...].T, axis=0, keepdims=True)
     row = lax.broadcasted_iota(jnp.int32, stats.shape[1:], 0)
-    tile = jnp.where(row == 0, raw_gain[:, :head_size], 0.0)
-    tile = jnp.where(row == 1, raw_gain[:, head_size:], tile)
+    tile = jnp.where(row == 0, gains[:, :head_size], 0.0)
+    tile = jnp.where(row == 1, gains[:, head_size:], tile)
     tile = jnp.where(row == 2, rate_row, tile)
     for i in range(stats.shape[0]):
         stats[i] = tile
@@ -285,6 +325,29 @@
     return lax.all_to_all(value, axes, 0, 0, tiled=True)
 
 
+def attend_call(place, assignment, counts, lambdas, norm_gain, gate, text, *vision):
+    seqs, toks, columns = text.shape[1:]
+    head_count, head_size = lambdas.shape[1:]
+    heads = head_count // PARTS
+    slab = vision[0].shape
+    rows = slab[1]
+    return kernel(
+        functools.partial(
+            attend_body, heads=heads, head_size=head_size, patch=rows // seqs
+        ),
+        [shaped((seqs * toks + 2 * rows, columns // 2))] * PARTS
+        + [shaped(slab)] * PARTS
+        + [shaped((FIRST, 4, head_size), f32)],
+        [SMEM] * 3 + [VMEM] * (4 + PARTS),
+        [VMEM] * (2 * PARTS + 1),
+        scratch_shapes=[
+            pltpu.VMEM((2 * head_size, PARTS * toks), f32),
+            pltpu.VMEM((seqs, PARTS * PARTS * rows // seqs, PARTS * toks), f32),
+            pltpu.VMEM((2 * head_size, head_size), f32),
+        ],
+    )(place, assignment, counts, lambdas, norm_gain, gate, text, *vision)
+
+
 def shards(queries, vision, cotangent, assignment, frame_counts, lambdas, norm_gain, gate_logit):
     seqs, toks, text_columns = queries.shape
     frames_dev, patch, vision_columns = vision.shape[1:]
@@ -310,14 +373,7 @@
     held_text = exchange(sent_text, "x")
     held_vision = shift_all([row_vision] * PARTS, "zl", LATE, 1)
 
-    grads = kernel(
-        functools.partial(attend_body, heads=heads, head_size=head_size, patch=patch),
-        [shaped((seqs * toks + 2 * rows, text_columns // PARTS))] * PARTS
-        + [slab] * PARTS
-        + [shaped((FIRST, 4, head_size), f32)],
-        [SMEM] * 3 + [VMEM] * (4 + PARTS),
-        [VMEM] * (2 * PARTS + 1),
-    )(
+    grads = attend_call(
         place,
         assignment,
         frame_counts,
@@ -330,7 +386,7 @@
     payload, grad_vision, stats = grads[:PARTS], grads[PARTS : 2 * PARTS], grads[2 * PARTS]
 
     back_vision = shift_all(grad_vision, "zl", range(PARTS), -1)
-    stats = exchange(stats, ("y", "x"))
+    stats = exchange(stats, ("y", "core"))
     payload = kernel(
         sum_vision_body,
         [shaped(payload[0].shape)] * PARTS,
@@ -346,7 +402,7 @@
     stats = kernel(spread_sum_body, shaped((SECOND, 4, head_size), f32), [VMEM, ANY], VMEM)(
         stats, payload[0]
     )
-    stats = exchange(stats, ("zh", "core", "zl"))
+    stats = exchange(stats, ("zh", "zl", "x"))
     grad_queries, grad_vision, grad_lambdas, grad_gain, grad_gate = kernel(
         finish_body,
         [

time: 114 us -> 112 us (0.982)
  the two profiles are of different devices: /device:TPU:1 before, /device:TPU:48 now
where the time goes in v4:
time: 112 us
  starting transfers between devices  44.2 us (39%)
  blocking collectives  31.5 us (28%)
  waiting for transfers between devices  21.1 us (19%)
  Pallas kernels  8.65 us (8%)
  local copies, waits for them, and re-layouts  4.72 us (4%)
  between operations  1.44 us (1%)
    ppermute x9, starting transfers between devices, shift_all(): lax.ppermute(part, axis, [(i, (i + way * k) % PARTS) for i in range(PARTS)])  36.3 us
    all_to_all x2, blocking collectives, exchange(): return lax.all_to_all(value, axes, 0, 0, tiled=True)  31.5 us
    ppermute x9, waiting for transfers between devices, shift_all(): lax.ppermute(part, axis, [(i, (i + way * k) % PARTS) for i in range(PARTS)])  18.6 us
    all_to_all x2, starting transfers between devices, exchange(): return lax.all_to_all(value, axes, 0, 0, tiled=True)  7.9 us
    unnamed x16, local copies, waits for them, and re-layouts  4.72 us
    pallas_call x1, Pallas kernels, attend_call(): kernel(functools.partial(attend_body, heads=heads, head_size=head_size, p...  4.06 us
    all_to_all x2, waiting for transfers between devices, exchange(): return lax.all_to_all(value, axes, 0, 0, tiled=True)  2.53 us
    pallas_call x1, Pallas kernels, shards(): kernel(finish_body, [shaped((seqs * toks, text_columns)), shaped((rows, v...  2.4 us
  transfers between devices with their start and end apart: 11, of which 4 were waited for; matrix products, arithmetic and copies ran while one was open for 0% of the time, Pallas kernels for 0%

profile of v4, /device:TPU:48, one launch (start us, length us, event | category | flops | bytes accessed | tf_op | source)
XLA Modules:
  0.0 111.7 jit_solution(841364210981654806)
XLA Ops:
  0.6 0.9 copy-done.3
  2.3 4.3 %all-to-all-start.1 = ((bf16[4,16,2048]{2,1,0:T(8,128)(2,1)}), bf16[4,16,2048]{2,1,0:T(8,128)(2,1)S(1)}, u32[]{:S(2)}, u32[]{:S(2)}) async-start(bf16[4,16,2048]{2,1,0:T(8,128)(2,1)} %shard_map.120), calls=%async_computation.1 | async-start | bytes 524288 | tf_op jit(solution)/shard_map/all_to_all | solution.py:325
  6.6 1.2 %copy-done.1 = bf16[2,64,4096]{2,1,0:T(8,128)(2,1)S(1)} copy-done((bf16[2,64,4096]{2,1,0:T(8,128)(2,1)S(1)}, bf16[2,64,4096]{2,1,0:T(8,128)(2,1)}, u32[]{:S(2)}) %copy-start.1) | copy-done | bytes 1048600
  7.8 1.2 %copy-done.2 = bf16[2,64,4096]{2,1,0:T(8,128)(2,1)S(1)} copy-done((bf16[2,64,4096]{2,1,0:T(8,128)(2,1)S(1)}, bf16[2,64,4096]{2,1,0:T(8,128)(2,1)}, u32[]{:S(2)}) %copy-start.2) | copy-done | bytes 1048600
  9.4 1.3 %copy-done = bf16[4,2,64,2048]{3,2,1,0:T(8,128)(2,1)} copy-done((bf16[4,2,64,2048]{3,2,1,0:T(8,128)(2,1)}, bf16[4,2,64,2048]{3,2,1,0:T(8,128)(2,1)S(1)}, u32[]{:S(2)}) %copy-start) | copy-done | bytes 2097176
  10.8 2.5 %all-to-all-done.1.refs_1_ = bf16[4,16,2048]{2,1,0:T(8,128)(2,1)S(1)} async-done(((bf16[4,16,2048]{2,1,0:T(8,128)(2,1)}), bf16[4,16,2048]{2,1,0:T(8,128)(2,1)S(1)}, u32[]{:S(2)}, u32[]{:S(2)}) %all-to-all-start.1) | async-done | bytes 262176 | tf_op jit(solution)/shard_map/all_to_all | solution.py:325
  13.3 3.6 %all-to-all-start = ((bf16[4,2,64,2048]{3,2,1,0:T(8,128)(2,1)}), bf16[4,2,64,2048]{3,2,1,0:T(8,128)(2,1)S(1)}, u32[]{:S(2)}, u32[]{:S(2)}) async-start(bf16[4,2,64,2048]{3,2,1,0:T(8,128)(2,1)} %copy-done), calls=%async_computation | async-start | bytes 4194304 | tf_op jit(solution)/shard_map/all_to_all | solution.py:325
  16.9 6.1 %collective-permute-start.2 = (bf16[4,16,2048]{2,1,0:T(8,128)(2,1)S(1)}, bf16[4,16,2048]{2,1,0:T(8,128)(2,1)S(1)}, u32[]{:S(2)}, u32[]{:S(2)}) collective-permute-start(bf16[4,16,2048]{2,1,0:T(8,128)(2,1)S(1)} %all-to-all-done.1.refs_1_), channel_id=1, source_target_pairs={{0,8},{4,12},{8,0},{12,4},{1,9},{5,13},{9,1},{13,5},{2,10},{6,14},... | collective-permute-start | bytes 786440 | tf_op jit(solution)/shard_map/ppermute | solution.py:304
  23.0 4.3 %collective-permute-start.1 = (bf16[4,16,2048]{2,1,0:T(8,128)(2,1)S(1)}, bf16[4,16,2048]{2,1,0:T(8,128)(2,1)S(1)}, u32[]{:S(2)}, u32[]{:S(2)}) collective-permute-start(bf16[4,16,2048]{2,1,0:T(8,128)(2,1)S(1)} %all-to-all-done.1.refs_1_), channel_id=1, source_target_pairs={{0,4},{4,8},{8,12},{12,0},{1,5},{5,9},{9,13},{13,1},{2,6},{6,10},{... | collective-permute-start | bytes 786440 | tf_op jit(solution)/shard_map/ppermute | solution.py:304
  27.3 3.4 %collective-permute-start = (bf16[4,16,2048]{2,1,0:T(8,128)(2,1)S(1)}, bf16[4,16,2048]{2,1,0:T(8,128)(2,1)S(1)}, u32[]{:S(2)}, u32[]{:S(2)}) collective-permute-start(bf16[4,16,2048]{2,1,0:T(8,128)(2,1)S(1)} %all-to-all-done.1.refs_1_), channel_id=1, source_target_pairs={{0,12},{4,0},{8,4},{12,8},{1,13},{5,1},{9,5},{13,9},{2,14},{6,2},{... | collective-permute-start | bytes 786440 | tf_op jit(solution)/shard_map/ppermute | solution.py:304
  31.4 9.8 %collective-permute-done.2.refs_4_ = bf16[4,16,2048]{2,1,0:T(8,128)(2,1)S(1)} collective-permute-done((bf16[4,16,2048]{2,1,0:T(8,128)(2,1)S(1)}, bf16[4,16,2048]{2,1,0:T(8,128)(2,1)S(1)}, u32[]{:S(2)}, u32[]{:S(2)}) %collective-permute-start.2) | collective-permute-done | bytes 262176 | tf_op jit(solution)/shard_map/ppermute | solution.py:304
  41.1 2.4 %collective-permute-done.refs_2_ = bf16[4,16,2048]{2,1,0:T(8,128)(2,1)S(1)} collective-permute-done((bf16[4,16,2048]{2,1,0:T(8,128)(2,1)S(1)}, bf16[4,16,2048]{2,1,0:T(8,128)(2,1)S(1)}, u32[]{:S(2)}, u32[]{:S(2)}) %collective-permute-start) | collective-permute-done | bytes 262176 | tf_op jit(solution)/shard_map/ppermute | solution.py:304
  43.5 4.1 %shard_map.121 = (bf16[160,1024]{1,0:T(8,128)(2,1)S(1)}, bf16[160,1024]{1,0:T(8,128)(2,1)S(1)}, bf16[160,1024]{1,0:T(8,128)(2,1)S(1)}, bf16[160,1024]{1,0:T(8,12...) custom-call(s32[2]{0:T(128)S(1)} %pad_add_fusion.place, ...), custom_call_target="tpu_custom_call" | custom-call | tf_op jit(solution)/shard_map/pallas_call | solution.py:334
  47.6 6.4 %collective-permute-start.3 = (bf16[4,16,2048]{2,1,0:T(8,128)(2,1)S(1)}, bf16[4,16,2048]{2,1,0:T(8,128)(2,1)S(1)}, u32[]{:S(2)}, u32[]{:S(2)}) collective-permute-start(bf16[4,16,2048]{2,1,0:T(8,128)(2,1)S(1)} %get-tuple-element.25), channel_id=1, source_target_pairs={{0,12},{4,0},{8,4},{12,8},{1,13},{5,1},{9,5},{13,9},{2,14},{6,2},{... | collective-permute-start | bytes 786440 | tf_op jit(solution)/shard_map/ppermute | solution.py:304
  54.0 1.9 %collective-permute-start.4 = (bf16[4,16,2048]{2,1,0:T(8,128)(2,1)S(1)}, bf16[4,16,2048]{2,1,0:T(8,128)(2,1)S(1)}, u32[]{:S(2)}, u32[]{:S(2)}) collective-permute-start(bf16[4,16,2048]{2,1,0:T(8,128)(2,1)S(1)} %get-tuple-element.26), channel_id=1, source_target_pairs={{0,8},{4,12},{8,0},{12,4},{1,9},{5,13},{9,1},{13,5},{2,10},{6,14},... | collective-permute-start | bytes 786440 | tf_op jit(solution)/shard_map/ppermute | solution.py:304
  56.0 3.3 %collective-permute-start.5 = (bf16[4,16,2048]{2,1,0:T(8,128)(2,1)S(1)}, bf16[4,16,2048]{2,1,0:T(8,128)(2,1)S(1)}, u32[]{:S(2)}, u32[]{:S(2)}) collective-permute-start(bf16[4,16,2048]{2,1,0:T(8,128)(2,1)S(1)} %get-tuple-element.27), channel_id=1, source_target_pairs={{0,4},{4,8},{8,12},{12,0},{1,5},{5,9},{9,13},{13,1},{2,6},{6,10},{... | collective-permute-start | bytes 786440 | tf_op jit(solution)/shard_map/ppermute | solution.py:304
  59.3 11.0 %all_to_all.20.after.tiles = f32[16,4,128]{2,1,0:T(4,128)S(1)} all-to-all(f32[16,4,128]{2,1,0:T(4,128)S(1)} %get-tuple-element.23), channel_id=1, replica_groups=mesh['y'=8,'zh'=2,'core'=2,'zl'=4,'x'=4] {'y','core'}, dimensions={0} | all-to-all | bytes 65536 | tf_op jit(solution)/shard_map/all_to_all | solution.py:325
  70.3 6.4 %collective-permute-done.4.refs_2_ = bf16[4,16,2048]{2,1,0:T(8,128)(2,1)S(1)} collective-permute-done((bf16[4,16,2048]{2,1,0:T(8,128)(2,1)S(1)}, bf16[4,16,2048]{2,1,0:T(8,128)(2,1)S(1)}, u32[]{:S(2)}, u32[]{:S(2)}) %collective-permute-start.4) | collective-permute-done | bytes 262176 | tf_op jit(solution)/shard_map/ppermute | solution.py:304
  76.8 1.1 shard_map.122
  77.9 5.1 %collective-permute-start.6 = (bf16[160,1024]{1,0:T(8,128)(2,1)S(1)}, bf16[160,1024]{1,0:T(8,128)(2,1)S(1)}, u32[]{:S(2)}, u32[]{:S(2)}) collective-permute-start(bf16[160,1024]{1,0:T(8,128)(2,1)S(1)} %get-tuple-element.33), channel_id=1, source_target_pairs={{0,2},{1,3},{2,0},{3,1},{4,6},{5,7},{6,4},{7,5},{8,10},{9,11},{10,... | collective-permute-start | bytes 983048 | tf_op jit(solution)/shard_map/ppermute | solution.py:304
  83.0 3.1 %collective-permute-start.7 = (bf16[160,1024]{1,0:T(8,128)(2,1)S(1)}, bf16[160,1024]{1,0:T(8,128)(2,1)S(1)}, u32[]{:S(2)}, u32[]{:S(2)}) collective-permute-start(bf16[160,1024]{1,0:T(8,128)(2,1)S(1)} %get-tuple-element.34), channel_id=1, source_target_pairs={{0,3},{1,0},{2,1},{3,2},{4,7},{5,4},{6,5},{7,6},{8,11},{9,8},{10,9... | collective-permute-start | bytes 983048 | tf_op jit(solution)/shard_map/ppermute | solution.py:304
  86.0 2.8 %collective-permute-start.8 = (bf16[160,1024]{1,0:T(8,128)(2,1)S(1)}, bf16[160,1024]{1,0:T(8,128)(2,1)S(1)}, u32[]{:S(2)}, u32[]{:S(2)}) collective-permute-start(bf16[160,1024]{1,0:T(8,128)(2,1)S(1)} %get-tuple-element.35), channel_id=1, source_target_pairs={{0,1},{1,2},{2,3},{3,0},{4,5},{5,6},{6,7},{7,4},{8,9},{9,10},{10,1... | collective-permute-start | bytes 983048 | tf_op jit(solution)/shard_map/ppermute | solution.py:304
  88.9 20.5 %all_to_all.21.tiles = f32[32,4,128]{2,1,0:T(4,128)S(1)} all-to-all(f32[32,4,128]{2,1,0:T(4,128)S(1)} %shard_map.123), channel_id=1, replica_groups=mesh['y'=8,'zh'=2,'core'=2,'zl'=4,'x'=4] {'zh','zl','x'}, dimensions={0} | all-to-all | bytes 131072 | tf_op jit(solution)/shard_map/all_to_all | solution.py:325
  109.3 2.4 %shard_map.124 = (bf16[128,4096]{1,0:T(8,128)(2,1)}, bf16[16,8192]{1,0:T(8,128)(2,1)}, f32[4,16,128]{2,1,0:T(8,128)}, f32[2,128]{1,0:T(2,128)}, f32[1,1]{1,0:T(1,128)}) custom-call(s32[2]{0:T(128)S(1)} %pad_add_fusion.place, f32[32,4,128]{2,1,0:T(4,128)S(1)} %all_to_all.21.tiles, f32[4,16,128]{2,1,0:T(8,128)S(1)} %copy-done.4, f32[2,128]{1,0:T(2,128)S(1)} %bitcast.16, ...), custom_call_target="tpu_custom_call" | custom-call | tf_op jit(solution)/shard_map/pallas_call | solution.py:406
  (23 shorter events, 1.2 us)
Async XLA Ops:
  0.6 1.0 copy-start.3
  2.3 11.0 %all-to-all-start.1 = ((bf16[4,16,2048]{2,1,0:T(8,128)(2,1)}), bf16[4,16,2048]{2,1,0:T(8,128)(2,1)S(1)}, u32[]{:S(2)}, u32[]{:S(2)}) async-start(bf16[4,16,2048]{2,1,0:T(8,128)(2,1)} %shard_map.120), calls=%async_computation.1 | async-start | bytes 524288 | tf_op jit(solution)/shard_map/all_to_all | solution.py:325
  6.6 1.2 %copy-start.1 = (bf16[2,64,4096]{2,1,0:T(8,128)(2,1)S(1)}, bf16[2,64,4096]{2,1,0:T(8,128)(2,1)}, u32[]{:S(2)}) copy-start(bf16[2,64,4096]{2,1,0:T(8,128)(2,1)} %queries.1) | copy-start | bytes 3145732
  7.8 1.2 %copy-start.2 = (bf16[2,64,4096]{2,1,0:T(8,128)(2,1)S(1)}, bf16[2,64,4096]{2,1,0:T(8,128)(2,1)}, u32[]{:S(2)}) copy-start(bf16[2,64,4096]{2,1,0:T(8,128)(2,1)} %cotangent.1) | copy-start | bytes 3145732
  9.4 1.3 %copy-start = (bf16[4,2,64,2048]{3,2,1,0:T(8,128)(2,1)}, bf16[4,2,64,2048]{3,2,1,0:T(8,128)(2,1)S(1)}, u32[]{:S(2)}) copy-start(bf16[4,2,64,2048]{3,2,1,0:T(8,128)(2,1)S(1)} %shard_map.119) | copy-start | bytes 6291460
  10.7 32.8 %copy-start.4 = (f32[4,16,128]{2,1,0:T(8,128)S(1)}, f32[4,16,128]{2,1,0:T(8,128)}, u32[]{:S(2)}) copy-start(f32[4,16,128]{2,1,0:T(8,128)} %lambdas.3) | copy-start | bytes 98308
  10.7 32.8 %copy-start.5 = (f32[256]{0:T(256)S(1)}, f32[256]{0:T(256)}, u32[]{:S(2)}) copy-start(f32[256]{0:T(256)} %param.14) | copy-start | bytes 3076
  10.7 32.8 %copy-start.6 = (s32[1,2]{1,0:T(1,128)S(1)}, s32[1,2]{1,0:T(1,128)}, u32[]{:S(2)}) copy-start(s32[1,2]{1,0:T(1,128)} %assignment.1) | copy-start | bytes 28
  10.7 32.8 %copy-start.7 = (s32[2]{0:T(128)S(1)}, s32[2]{0:T(128)}, u32[]{:S(2)}) copy-start(s32[2]{0:T(128)} %counts.1) | copy-start | bytes 28
  13.3 30.2 %all-to-all-start = ((bf16[4,2,64,2048]{3,2,1,0:T(8,128)(2,1)}), bf16[4,2,64,2048]{3,2,1,0:T(8,128)(2,1)S(1)}, u32[]{:S(2)}, u32[]{:S(2)}) async-start(bf16[4,2,64,2048]{3,2,1,0:T(8,128)(2,1)} %copy-done), calls=%async_computation | async-start | bytes 4194304 | tf_op jit(solution)/shard_map/all_to_all | solution.py:325
  16.9 24.2 %collective-permute-start.2 = (bf16[4,16,2048]{2,1,0:T(8,128)(2,1)S(1)}, bf16[4,16,2048]{2,1,0:T(8,128)(2,1)S(1)}, u32[]{:S(2)}, u32[]{:S(2)}) collective-permute-start(bf16[4,16,2048]{2,1,0:T(8,128)(2,1)S(1)} %all-to-all-done.1.refs_1_), channel_id=1, source_target_pairs={{0,8},{4,12},{8,0},{12,4},{1,9},{5,13},{9,1},{13,5},{2,10},{6,14},... | collective-permute-start | bytes 786440 | tf_op jit(solution)/shard_map/ppermute | solution.py:304
  23.0 18.1 %collective-permute-start.1 = (bf16[4,16,2048]{2,1,0:T(8,128)(2,1)S(1)}, bf16[4,16,2048]{2,1,0:T(8,128)(2,1)S(1)}, u32[]{:S(2)}, u32[]{:S(2)}) collective-permute-start(bf16[4,16,2048]{2,1,0:T(8,128)(2,1)S(1)} %all-to-all-done.1.refs_1_), channel_id=1, source_target_pairs={{0,4},{4,8},{8,12},{12,0},{1,5},{5,9},{9,13},{13,1},{2,6},{6,10},{... | collective-permute-start | bytes 786440 | tf_op jit(solution)/shard_map/ppermute | solution.py:304
  27.3 16.2 %collective-permute-start = (bf16[4,16,2048]{2,1,0:T(8,128)(2,1)S(1)}, bf16[4,16,2048]{2,1,0:T(8,128)(2,1)S(1)}, u32[]{:S(2)}, u32[]{:S(2)}) collective-permute-start(bf16[4,16,2048]{2,1,0:T(8,128)(2,1)S(1)} %all-to-all-done.1.refs_1_), channel_id=1, source_target_pairs={{0,12},{4,0},{8,4},{12,8},{1,13},{5,1},{9,5},{13,9},{2,14},{6,2},{... | collective-permute-start | bytes 786440 | tf_op jit(solution)/shard_map/ppermute | solution.py:304
  47.6 22.7 %collective-permute-start.3 = (bf16[4,16,2048]{2,1,0:T(8,128)(2,1)S(1)}, bf16[4,16,2048]{2,1,0:T(8,128)(2,1)S(1)}, u32[]{:S(2)}, u32[]{:S(2)}) collective-permute-start(bf16[4,16,2048]{2,1,0:T(8,128)(2,1)S(1)} %get-tuple-element.25), channel_id=1, source_target_pairs={{0,12},{4,0},{8,4},{12,8},{1,13},{5,1},{9,5},{13,9},{2,14},{6,2},{... | collective-permute-start | bytes 786440 | tf_op jit(solution)/shard_map/ppermute | solution.py:304
  54.0 22.7 %collective-permute-start.4 = (bf16[4,16,2048]{2,1,0:T(8,128)(2,1)S(1)}, bf16[4,16,2048]{2,1,0:T(8,128)(2,1)S(1)}, u32[]{:S(2)}, u32[]{:S(2)}) collective-permute-start(bf16[4,16,2048]{2,1,0:T(8,128)(2,1)S(1)} %get-tuple-element.26), channel_id=1, source_target_pairs={{0,8},{4,12},{8,0},{12,4},{1,9},{5,13},{9,1},{13,5},{2,10},{6,14},... | collective-permute-start | bytes 786440 | tf_op jit(solution)/shard_map/ppermute | solution.py:304
  56.0 20.8 %collective-permute-start.5 = (bf16[4,16,2048]{2,1,0:T(8,128)(2,1)S(1)}, bf16[4,16,2048]{2,1,0:T(8,128)(2,1)S(1)}, u32[]{:S(2)}, u32[]{:S(2)}) collective-permute-start(bf16[4,16,2048]{2,1,0:T(8,128)(2,1)S(1)} %get-tuple-element.27), channel_id=1, source_target_pairs={{0,4},{4,8},{8,12},{12,0},{1,5},{5,9},{9,13},{13,1},{2,6},{6,10},{... | collective-permute-start | bytes 786440 | tf_op jit(solution)/shard_map/ppermute | solution.py:304
  77.9 31.5 %collective-permute-start.6 = (bf16[160,1024]{1,0:T(8,128)(2,1)S(1)}, bf16[160,1024]{1,0:T(8,128)(2,1)S(1)}, u32[]{:S(2)}, u32[]{:S(2)}) collective-permute-start(bf16[160,1024]{1,0:T(8,128)(2,1)S(1)} %get-tuple-element.33), channel_id=1, source_target_pairs={{0,2},{1,3},{2,0},{3,1},{4,6},{5,7},{6,4},{7,5},{8,10},{9,11},{10,... | collective-permute-start | bytes 983048 | tf_op jit(solution)/shard_map/ppermute | solution.py:304
  83.0 26.3 %collective-permute-start.7 = (bf16[160,1024]{1,0:T(8,128)(2,1)S(1)}, bf16[160,1024]{1,0:T(8,128)(2,1)S(1)}, u32[]{:S(2)}, u32[]{:S(2)}) collective-permute-start(bf16[160,1024]{1,0:T(8,128)(2,1)S(1)} %get-tuple-element.34), channel_id=1, source_target_pairs={{0,3},{1,0},{2,1},{3,2},{4,7},{5,4},{6,5},{7,6},{8,11},{9,8},{10,9... | collective-permute-start | bytes 983048 | tf_op jit(solution)/shard_map/ppermute | solution.py:304
  86.0 23.3 %collective-permute-start.8 = (bf16[160,1024]{1,0:T(8,128)(2,1)S(1)}, bf16[160,1024]{1,0:T(8,128)(2,1)S(1)}, u32[]{:S(2)}, u32[]{:S(2)}) collective-permute-start(bf16[160,1024]{1,0:T(8,128)(2,1)S(1)} %get-tuple-element.35), channel_id=1, source_target_pairs={{0,1},{1,2},{2,3},{3,0},{4,5},{5,6},{6,7},{7,4},{8,9},{9,10},{10,1... | collective-permute-start | bytes 983048 | tf_op jit(solution)/shard_map/ppermute | solution.py:304

commit v5 on v4

--- a/solution.py
+++ b/solution.py
@@ -11,7 +11,7 @@
 epsilon = 1e-05
 DP = ("y", "zh", "core")
 IMAGE = ("zl", "x")
-FIRST, SECOND = 16, 32
+FIRST, SECOND = 32, 16
 PARTS = 4
 GROUP = 2
 ORDER, LATE = (0, 2, 1, 3), (0, 3, 1, 2)
@@ -244,37 +244,24 @@
 
 
 def finish_body(place, tiles, lambdas, norm_gain, gate, *refs):
-    parts, grad_queries, grad_vision, grad_lambdas, grad_gain, grad_gate, sems = (
+    parts, grad_queries, grad_vision, grad_lambdas, grad_gain, grad_gate = (
         refs[:PARTS],
         *refs[PARTS:],
     )
     text_rows, rows = grad_queries.shape[0], grad_vision.shape[0]
     half = grad_queries.shape[1] // 2
     width = half // PARTS
-    copies = []
     for k in range(PARTS):
         g = wrap(place[1] + ORDER[k])
         first = pl.multiple_of(g * width, width)
         second = pl.multiple_of(half + g * width, width)
         wide = pl.multiple_of(2 * half + 2 * g * width, 2 * width)
-        text, keys = pl.ds(0, text_rows), pl.ds(text_rows, rows)
-        values = pl.ds(text_rows + rows, rows)
-        left, right, both = pl.ds(0, width), pl.ds(width, width), pl.ds(0, 2 * width)
-        pieces = (
-            (text, left, grad_queries, pl.ds(first, width)),
-            (text, right, grad_queries, pl.ds(second, width)),
-            (keys, left, grad_vision, pl.ds(first, width)),
-            (keys, right, grad_vision, pl.ds(second, width)),
-            (values, both, grad_vision, pl.ds(wide, 2 * width)),
-        )
-        for i, (own_rows, columns, out, to) in enumerate(pieces):
-            copies.append(
-                pltpu.make_async_copy(
-                    parts[k].at[own_rows, columns], out.at[:, to], sems.at[k, i]
-                )
-            )
-    for copy in copies:
-        copy.start()
+        own = parts[k]
+        grad_queries[:, pl.ds(first, width)] = own[:text_rows, :width]
+        grad_queries[:, pl.ds(second, width)] = own[:text_rows, width:]
+        grad_vision[:, pl.ds(first, width)] = own[text_rows : text_rows + rows, :width]
+        grad_vision[:, pl.ds(second, width)] = own[text_rows : text_rows + rows, width:]
+        grad_vision[:, pl.ds(wide, 2 * width)] = own[text_rows + rows :, :]
     total = jnp.sum(tiles[...], axis=0)
     head_count, head_size = lambdas.shape[1:]
     gate_tanh = jnp.tanh(gate[...])
@@ -295,8 +282,6 @@
     grad_lambdas[1] = weight_one * lambdas[0]
     grad_lambdas[2] = -weight_two * lambdas[3]
     grad_lambdas[3] = -weight_two * lambdas[2]
-    for copy in copies:
-        copy.wait()
 
 
 def shift_all(parts, axis, order, way):
@@ -386,7 +371,7 @@
     payload, grad_vision, stats = grads[:PARTS], grads[PARTS : 2 * PARTS], grads[2 * PARTS]
 
     back_vision = shift_all(grad_vision, "zl", range(PARTS), -1)
-    stats = exchange(stats, ("y", "core"))
+    stats = exchange(stats, ("y", "x"))
     payload = kernel(
         sum_vision_body,
         [shaped(payload[0].shape)] * PARTS,
@@ -402,7 +387,7 @@
     stats = kernel(spread_sum_body, shaped((SECOND, 4, head_size), f32), [VMEM, ANY], VMEM)(
         stats, payload[0]
     )
-    stats = exchange(stats, ("zh", "zl", "x"))
+    stats = exchange(stats, ("zh", "core", "zl"))
     grad_queries, grad_vision, grad_lambdas, grad_gain, grad_gate = kernel(
         finish_body,
         [
@@ -412,9 +397,8 @@
             shaped(gain_rows.shape, f32),
             shaped((1, 1), f32),
         ],
-        [SMEM] + [VMEM] * 4 + [ANY] * PARTS,
-        [ANY] * 2 + [VMEM] * 3,
-        scratch_shapes=[pltpu.SemaphoreType.DMA((PARTS, 5))],
+        [SMEM] + [VMEM] * (4 + PARTS),
+        [VMEM] * 5,
     )(place, stats, lambdas, gain_rows, gate, *back)
     return (
         grad_queries.reshape(queries.shape),

time: 112 us -> 109 us (0.973)
  the two profiles are of different devices: /device:TPU:48 before, /device:TPU:1 now
where the time goes in v5:
time: 109 us; the launch traced here: 108 us
  starting transfers between devices  42.4 us (39%)
  blocking collectives  37.1 us (34%)
  waiting for transfers between devices  14.7 us (13%)
  Pallas kernels  7.94 us (7%)
  local copies, waits for them, and re-layouts  4.72 us (4%)
  between operations  1.44 us (1%)
    all_to_all x2, blocking collectives, exchange(): return lax.all_to_all(value, axes, 0, 0, tiled=True)  37.1 us
    ppermute x9, starting transfers between devices, shift_all(): lax.ppermute(part, axis, [(i, (i + way * k) % PARTS) for i in range(PARTS)])  33.9 us
    ppermute x9, waiting for transfers between devices, shift_all(): lax.ppermute(part, axis, [(i, (i + way * k) % PARTS) for i in range(PARTS)])  13.3 us
    all_to_all x2, starting transfers between devices, exchange(): return lax.all_to_all(value, axes, 0, 0, tiled=True)  8.45 us
    unnamed x16, local copies, waits for them, and re-layouts  4.72 us
    pallas_call x1, Pallas kernels, attend_call(): kernel(functools.partial(attend_body, heads=heads, head_size=head_size, p...  4.06 us
  transfers between devices with their start and end apart: 11, of which 3 were waited for; matrix products, arithmetic and copies ran while one was open for 0% of the time, Pallas kernels for 0%

profile of v5, /device:TPU:1, one launch (start us, length us, event | category | flops | bytes accessed | tf_op | source)
XLA Modules:
  0.0 108.3 jit_solution(15974824175404657817)
XLA Ops:
  0.6 0.9 copy-done.3
  1.6 0.7 shard_map.120
  2.3 4.8 %all-to-all-start.1 = ((bf16[4,16,2048]{2,1,0:T(8,128)(2,1)}), bf16[4,16,2048]{2,1,0:T(8,128)(2,1)S(1)}, u32[]{:S(2)}, u32[]{:S(2)}) async-start(bf16[4,16,2048]{2,1,0:T(8,128)(2,1)} %shard_map.120), calls=%async_computation.1 | async-start | bytes 524288 | tf_op jit(solution)/shard_map/all_to_all | solution.py:310
  7.1 1.2 %copy-done.1 = bf16[2,64,4096]{2,1,0:T(8,128)(2,1)S(1)} copy-done((bf16[2,64,4096]{2,1,0:T(8,128)(2,1)S(1)}, bf16[2,64,4096]{2,1,0:T(8,128)(2,1)}, u32[]{:S(2)}) %copy-start.1) | copy-done | bytes 1048600
  8.4 1.2 %copy-done.2 = bf16[2,64,4096]{2,1,0:T(8,128)(2,1)S(1)} copy-done((bf16[2,64,4096]{2,1,0:T(8,128)(2,1)S(1)}, bf16[2,64,4096]{2,1,0:T(8,128)(2,1)}, u32[]{:S(2)}) %copy-start.2) | copy-done | bytes 1048600
  10.0 1.3 %copy-done = bf16[4,2,64,2048]{3,2,1,0:T(8,128)(2,1)} copy-done((bf16[4,2,64,2048]{3,2,1,0:T(8,128)(2,1)}, bf16[4,2,64,2048]{3,2,1,0:T(8,128)(2,1)S(1)}, u32[]{:S(2)}) %copy-start) | copy-done | bytes 2097176
  11.3 1.4 %all-to-all-done.1.refs_1_ = bf16[4,16,2048]{2,1,0:T(8,128)(2,1)S(1)} async-done(((bf16[4,16,2048]{2,1,0:T(8,128)(2,1)}), bf16[4,16,2048]{2,1,0:T(8,128)(2,1)S(1)}, u32[]{:S(2)}, u32[]{:S(2)}) %all-to-all-start.1) | async-done | bytes 262176 | tf_op jit(solution)/shard_map/all_to_all | solution.py:310
  12.7 3.6 %all-to-all-start = ((bf16[4,2,64,2048]{3,2,1,0:T(8,128)(2,1)}), bf16[4,2,64,2048]{3,2,1,0:T(8,128)(2,1)S(1)}, u32[]{:S(2)}, u32[]{:S(2)}) async-start(bf16[4,2,64,2048]{3,2,1,0:T(8,128)(2,1)} %copy-done), calls=%async_computation | async-start | bytes 4194304 | tf_op jit(solution)/shard_map/all_to_all | solution.py:310
  16.3 5.8 %collective-permute-start.2 = (bf16[4,16,2048]{2,1,0:T(8,128)(2,1)S(1)}, bf16[4,16,2048]{2,1,0:T(8,128)(2,1)S(1)}, u32[]{:S(2)}, u32[]{:S(2)}) collective-permute-start(bf16[4,16,2048]{2,1,0:T(8,128)(2,1)S(1)} %all-to-all-done.1.refs_1_), channel_id=1, source_target_pairs={{0,8},{4,12},{8,0},{12,4},{1,9},{5,13},{9,1},{13,5},{2,10},{6,14},... | collective-permute-start | bytes 786440 | tf_op jit(solution)/shard_map/ppermute | solution.py:289
  22.1 4.0 %collective-permute-start.1 = (bf16[4,16,2048]{2,1,0:T(8,128)(2,1)S(1)}, bf16[4,16,2048]{2,1,0:T(8,128)(2,1)S(1)}, u32[]{:S(2)}, u32[]{:S(2)}) collective-permute-start(bf16[4,16,2048]{2,1,0:T(8,128)(2,1)S(1)} %all-to-all-done.1.refs_1_), channel_id=1, source_target_pairs={{0,4},{4,8},{8,12},{12,0},{1,5},{5,9},{9,13},{13,1},{2,6},{6,10},{... | collective-permute-start | bytes 786440 | tf_op jit(solution)/shard_map/ppermute | solution.py:289
  26.1 3.1 %collective-permute-start = (bf16[4,16,2048]{2,1,0:T(8,128)(2,1)S(1)}, bf16[4,16,2048]{2,1,0:T(8,128)(2,1)S(1)}, u32[]{:S(2)}, u32[]{:S(2)}) collective-permute-start(bf16[4,16,2048]{2,1,0:T(8,128)(2,1)S(1)} %all-to-all-done.1.refs_1_), channel_id=1, source_target_pairs={{0,12},{4,0},{8,4},{12,8},{1,13},{5,1},{9,5},{13,9},{2,14},{6,2},{... | collective-permute-start | bytes 786440 | tf_op jit(solution)/shard_map/ppermute | solution.py:289
  30.0 7.9 %collective-permute-done.2.refs_4_ = bf16[4,16,2048]{2,1,0:T(8,128)(2,1)S(1)} collective-permute-done((bf16[4,16,2048]{2,1,0:T(8,128)(2,1)S(1)}, bf16[4,16,2048]{2,1,0:T(8,128)(2,1)S(1)}, u32[]{:S(2)}, u32[]{:S(2)}) %collective-permute-start.2) | collective-permute-done | bytes 262176 | tf_op jit(solution)/shard_map/ppermute | solution.py:289
  37.8 5.4 %collective-permute-done.refs_2_ = bf16[4,16,2048]{2,1,0:T(8,128)(2,1)S(1)} collective-permute-done((bf16[4,16,2048]{2,1,0:T(8,128)(2,1)S(1)}, bf16[4,16,2048]{2,1,0:T(8,128)(2,1)S(1)}, u32[]{:S(2)}, u32[]{:S(2)}) %collective-permute-start) | collective-permute-done | bytes 262176 | tf_op jit(solution)/shard_map/ppermute | solution.py:289
  43.3 4.1 %shard_map.121 = (bf16[160,1024]{1,0:T(8,128)(2,1)S(1)}, bf16[160,1024]{1,0:T(8,128)(2,1)S(1)}, bf16[160,1024]{1,0:T(8,128)(2,1)S(1)}, bf16[160,1024]{1,0:T(8,12...) custom-call(s32[2]{0:T(128)S(1)} %pad_add_fusion.place, ...), custom_call_target="tpu_custom_call" | custom-call | tf_op jit(solution)/shard_map/pallas_call | solution.py:319
  47.3 4.9 %collective-permute-start.3 = (bf16[4,16,2048]{2,1,0:T(8,128)(2,1)S(1)}, bf16[4,16,2048]{2,1,0:T(8,128)(2,1)S(1)}, u32[]{:S(2)}, u32[]{:S(2)}) collective-permute-start(bf16[4,16,2048]{2,1,0:T(8,128)(2,1)S(1)} %get-tuple-element.25), channel_id=1, source_target_pairs={{0,12},{4,0},{8,4},{12,8},{1,13},{5,1},{9,5},{13,9},{2,14},{6,2},{... | collective-permute-start | bytes 786440 | tf_op jit(solution)/shard_map/ppermute | solution.py:289
  52.3 3.8 %collective-permute-start.4 = (bf16[4,16,2048]{2,1,0:T(8,128)(2,1)S(1)}, bf16[4,16,2048]{2,1,0:T(8,128)(2,1)S(1)}, u32[]{:S(2)}, u32[]{:S(2)}) collective-permute-start(bf16[4,16,2048]{2,1,0:T(8,128)(2,1)S(1)} %get-tuple-element.26), channel_id=1, source_target_pairs={{0,8},{4,12},{8,0},{12,4},{1,9},{5,13},{9,1},{13,5},{2,10},{6,14},... | collective-permute-start | bytes 786440 | tf_op jit(solution)/shard_map/ppermute | solution.py:289
  56.1 3.4 %collective-permute-start.5 = (bf16[4,16,2048]{2,1,0:T(8,128)(2,1)S(1)}, bf16[4,16,2048]{2,1,0:T(8,128)(2,1)S(1)}, u32[]{:S(2)}, u32[]{:S(2)}) collective-permute-start(bf16[4,16,2048]{2,1,0:T(8,128)(2,1)S(1)} %get-tuple-element.27), channel_id=1, source_target_pairs={{0,4},{4,8},{8,12},{12,0},{1,5},{5,9},{9,13},{13,1},{2,6},{6,10},{... | collective-permute-start | bytes 786440 | tf_op jit(solution)/shard_map/ppermute | solution.py:289
  59.5 18.5 %all_to_all.20.after.tiles = f32[32,4,128]{2,1,0:T(4,128)S(1)} all-to-all(f32[32,4,128]{2,1,0:T(4,128)S(1)} %get-tuple-element.23), channel_id=1, replica_groups=mesh['y'=8,'zh'=2,'core'=2,'zl'=4,'x'=4] {'y','x'}, dimensions={0} | all-to-all | bytes 131072 | tf_op jit(solution)/shard_map/all_to_all | solution.py:310
  78.0 1.1 %shard_map.122 = (bf16[160,1024]{1,0:T(8,128)(2,1)S(1)}, bf16[160,1024]{1,0:T(8,128)(2,1)S(1)}, bf16[160,1024]{1,0:T(8,128)(2,1)S(1)}, bf16[160,1024]{1,0:T(8,128)(2,1)S(1)}) custom-call(s32[2]{0:T(128)S(1)} %pad_add_fusion.place, f32[32,4,128]{2,1,0:T(4,128)S(1)} %all_to_all.20.after.tiles, ...), custom_call_target="tpu_custom_call", output_to_operand_aliasing={{0}: (6, {}), {1}: (7, {}), {2}: (8, {}), {3}: (9, {})} | custom-call | tf_op jit(solution)/shard_map/pallas_call | solution.py:375
  79.0 3.6 %collective-permute-start.6 = (bf16[160,1024]{1,0:T(8,128)(2,1)S(1)}, bf16[160,1024]{1,0:T(8,128)(2,1)S(1)}, u32[]{:S(2)}, u32[]{:S(2)}) collective-permute-start(bf16[160,1024]{1,0:T(8,128)(2,1)S(1)} %get-tuple-element.33), channel_id=1, source_target_pairs={{0,2},{1,3},{2,0},{3,1},{4,6},{5,7},{6,4},{7,5},{8,10},{9,11},{10,... | collective-permute-start | bytes 983048 | tf_op jit(solution)/shard_map/ppermute | solution.py:289
  82.7 2.8 %collective-permute-start.7 = (bf16[160,1024]{1,0:T(8,128)(2,1)S(1)}, bf16[160,1024]{1,0:T(8,128)(2,1)S(1)}, u32[]{:S(2)}, u32[]{:S(2)}) collective-permute-start(bf16[160,1024]{1,0:T(8,128)(2,1)S(1)} %get-tuple-element.34), channel_id=1, source_target_pairs={{0,3},{1,0},{2,1},{3,2},{4,7},{5,4},{6,5},{7,6},{8,11},{9,8},{10,9... | collective-permute-start | bytes 983048 | tf_op jit(solution)/shard_map/ppermute | solution.py:289
  85.5 2.5 %collective-permute-start.8 = (bf16[160,1024]{1,0:T(8,128)(2,1)S(1)}, bf16[160,1024]{1,0:T(8,128)(2,1)S(1)}, u32[]{:S(2)}, u32[]{:S(2)}) collective-permute-start(bf16[160,1024]{1,0:T(8,128)(2,1)S(1)} %get-tuple-element.35), channel_id=1, source_target_pairs={{0,1},{1,2},{2,3},{3,0},{4,5},{5,6},{6,7},{7,4},{8,9},{9,10},{10,1... | collective-permute-start | bytes 983048 | tf_op jit(solution)/shard_map/ppermute | solution.py:289
  88.0 18.6 %all_to_all.21.tiles = f32[16,4,128]{2,1,0:T(4,128)S(1)} all-to-all(f32[16,4,128]{2,1,0:T(4,128)S(1)} %shard_map.123), channel_id=1, replica_groups=mesh['y'=8,'zh'=2,'core'=2,'zl'=4,'x'=4] {'zh','core','zl'}, dimensions={0} | all-to-all | bytes 65536 | tf_op jit(solution)/shard_map/all_to_all | solution.py:310
  106.7 1.7 %shard_map.124 = (bf16[128,4096]{1,0:T(8,128)(2,1)}, bf16[16,8192]{1,0:T(8,128)(2,1)}, f32[4,16,128]{2,1,0:T(8,128)}, f32[2,128]{1,0:T(2,128)}, f32[1,1]{1,0:T(1,128)}) custom-call(s32[2]{0:T(128)S(1)} %pad_add_fusion.place, f32[16,4,128]{2,1,0:T(4,128)S(1)} %all_to_all.21.tiles, f32[4,16,128]{2,1,0:T(8,128)S(1)} %copy-done.4, f32[2,128]{1,0:T(2,128)S(1)} %bitcast.16, ...), custom_call_target="tpu_custom_call" | custom-call | tf_op jit(solution)/shard_map/pallas_call | solution.py:391
  (23 shorter events, 0.5 us)
Async XLA Ops:
  0.6 1.0 copy-start.3
  2.3 10.4 %all-to-all-start.1 = ((bf16[4,16,2048]{2,1,0:T(8,128)(2,1)}), bf16[4,16,2048]{2,1,0:T(8,128)(2,1)S(1)}, u32[]{:S(2)}, u32[]{:S(2)}) async-start(bf16[4,16,2048]{2,1,0:T(8,128)(2,1)} %shard_map.120), calls=%async_computation.1 | async-start | bytes 524288 | tf_op jit(solution)/shard_map/all_to_all | solution.py:310
  7.1 1.2 %copy-start.1 = (bf16[2,64,4096]{2,1,0:T(8,128)(2,1)S(1)}, bf16[2,64,4096]{2,1,0:T(8,128)(2,1)}, u32[]{:S(2)}) copy-start(bf16[2,64,4096]{2,1,0:T(8,128)(2,1)} %queries.1) | copy-start | bytes 3145732
  8.4 1.2 %copy-start.2 = (bf16[2,64,4096]{2,1,0:T(8,128)(2,1)S(1)}, bf16[2,64,4096]{2,1,0:T(8,128)(2,1)}, u32[]{:S(2)}) copy-start(bf16[2,64,4096]{2,1,0:T(8,128)(2,1)} %cotangent.1) | copy-start | bytes 3145732
  10.0 1.3 %copy-start = (bf16[4,2,64,2048]{3,2,1,0:T(8,128)(2,1)}, bf16[4,2,64,2048]{3,2,1,0:T(8,128)(2,1)S(1)}, u32[]{:S(2)}) copy-start(bf16[4,2,64,2048]{3,2,1,0:T(8,128)(2,1)S(1)} %shard_map.119) | copy-start | bytes 6291460
  11.3 32.0 %copy-start.4 = (f32[4,16,128]{2,1,0:T(8,128)S(1)}, f32[4,16,128]{2,1,0:T(8,128)}, u32[]{:S(2)}) copy-start(f32[4,16,128]{2,1,0:T(8,128)} %lambdas.3) | copy-start | bytes 98308
  11.3 32.0 %copy-start.5 = (f32[256]{0:T(256)S(1)}, f32[256]{0:T(256)}, u32[]{:S(2)}) copy-start(f32[256]{0:T(256)} %param.14) | copy-start | bytes 3076
  11.3 32.0 %copy-start.6 = (s32[1,2]{1,0:T(1,128)S(1)}, s32[1,2]{1,0:T(1,128)}, u32[]{:S(2)}) copy-start(s32[1,2]{1,0:T(1,128)} %assignment.1) | copy-start | bytes 28
  11.3 32.0 %copy-start.7 = (s32[2]{0:T(128)S(1)}, s32[2]{0:T(128)}, u32[]{:S(2)}) copy-start(s32[2]{0:T(128)} %counts.1) | copy-start | bytes 28
  12.7 30.6 %all-to-all-start = ((bf16[4,2,64,2048]{3,2,1,0:T(8,128)(2,1)}), bf16[4,2,64,2048]{3,2,1,0:T(8,128)(2,1)S(1)}, u32[]{:S(2)}, u32[]{:S(2)}) async-start(bf16[4,2,64,2048]{3,2,1,0:T(8,128)(2,1)} %copy-done), calls=%async_computation | async-start | bytes 4194304 | tf_op jit(solution)/shard_map/all_to_all | solution.py:310
  16.3 21.6 %collective-permute-start.2 = (bf16[4,16,2048]{2,1,0:T(8,128)(2,1)S(1)}, bf16[4,16,2048]{2,1,0:T(8,128)(2,1)S(1)}, u32[]{:S(2)}, u32[]{:S(2)}) collective-permute-start(bf16[4,16,2048]{2,1,0:T(8,128)(2,1)S(1)} %all-to-all-done.1.refs_1_), channel_id=1, source_target_pairs={{0,8},{4,12},{8,0},{12,4},{1,9},{5,13},{9,1},{13,5},{2,10},{6,14},... | collective-permute-start | bytes 786440 | tf_op jit(solution)/shard_map/ppermute | solution.py:289
  22.1 15.7 %collective-permute-start.1 = (bf16[4,16,2048]{2,1,0:T(8,128)(2,1)S(1)}, bf16[4,16,2048]{2,1,0:T(8,128)(2,1)S(1)}, u32[]{:S(2)}, u32[]{:S(2)}) collective-permute-start(bf16[4,16,2048]{2,1,0:T(8,128)(2,1)S(1)} %all-to-all-done.1.refs_1_), channel_id=1, source_target_pairs={{0,4},{4,8},{8,12},{12,0},{1,5},{5,9},{9,13},{13,1},{2,6},{6,10},{... | collective-permute-start | bytes 786440 | tf_op jit(solution)/shard_map/ppermute | solution.py:289
  26.1 17.1 %collective-permute-start = (bf16[4,16,2048]{2,1,0:T(8,128)(2,1)S(1)}, bf16[4,16,2048]{2,1,0:T(8,128)(2,1)S(1)}, u32[]{:S(2)}, u32[]{:S(2)}) collective-permute-start(bf16[4,16,2048]{2,1,0:T(8,128)(2,1)S(1)} %all-to-all-done.1.refs_1_), channel_id=1, source_target_pairs={{0,12},{4,0},{8,4},{12,8},{1,13},{5,1},{9,5},{13,9},{2,14},{6,2},{... | collective-permute-start | bytes 786440 | tf_op jit(solution)/shard_map/ppermute | solution.py:289
  47.3 30.6 %collective-permute-start.3 = (bf16[4,16,2048]{2,1,0:T(8,128)(2,1)S(1)}, bf16[4,16,2048]{2,1,0:T(8,128)(2,1)S(1)}, u32[]{:S(2)}, u32[]{:S(2)}) collective-permute-start(bf16[4,16,2048]{2,1,0:T(8,128)(2,1)S(1)} %get-tuple-element.25), channel_id=1, source_target_pairs={{0,12},{4,0},{8,4},{12,8},{1,13},{5,1},{9,5},{13,9},{2,14},{6,2},{... | collective-permute-start | bytes 786440 | tf_op jit(solution)/shard_map/ppermute | solution.py:289
  52.3 25.7 %collective-permute-start.4 = (bf16[4,16,2048]{2,1,0:T(8,128)(2,1)S(1)}, bf16[4,16,2048]{2,1,0:T(8,128)(2,1)S(1)}, u32[]{:S(2)}, u32[]{:S(2)}) collective-permute-start(bf16[4,16,2048]{2,1,0:T(8,128)(2,1)S(1)} %get-tuple-element.26), channel_id=1, source_target_pairs={{0,8},{4,12},{8,0},{12,4},{1,9},{5,13},{9,1},{13,5},{2,10},{6,14},... | collective-permute-start | bytes 786440 | tf_op jit(solution)/shard_map/ppermute | solution.py:289
  56.1 21.9 %collective-permute-start.5 = (bf16[4,16,2048]{2,1,0:T(8,128)(2,1)S(1)}, bf16[4,16,2048]{2,1,0:T(8,128)(2,1)S(1)}, u32[]{:S(2)}, u32[]{:S(2)}) collective-permute-start(bf16[4,16,2048]{2,1,0:T(8,128)(2,1)S(1)} %get-tuple-element.27), channel_id=1, source_target_pairs={{0,4},{4,8},{8,12},{12,0},{1,5},{5,9},{9,13},{13,1},{2,6},{6,10},{... | collective-permute-start | bytes 786440 | tf_op jit(solution)/shard_map/ppermute | solution.py:289
  79.0 27.6 %collective-permute-start.6 = (bf16[160,1024]{1,0:T(8,128)(2,1)S(1)}, bf16[160,1024]{1,0:T(8,128)(2,1)S(1)}, u32[]{:S(2)}, u32[]{:S(2)}) collective-permute-start(bf16[160,1024]{1,0:T(8,128)(2,1)S(1)} %get-tuple-element.33), channel_id=1, source_target_pairs={{0,2},{1,3},{2,0},{3,1},{4,6},{5,7},{6,4},{7,5},{8,10},{9,11},{10,... | collective-permute-start | bytes 983048 | tf_op jit(solution)/shard_map/ppermute | solution.py:289
  82.7 24.0 %collective-permute-start.7 = (bf16[160,1024]{1,0:T(8,128)(2,1)S(1)}, bf16[160,1024]{1,0:T(8,128)(2,1)S(1)}, u32[]{:S(2)}, u32[]{:S(2)}) collective-permute-start(bf16[160,1024]{1,0:T(8,128)(2,1)S(1)} %get-tuple-element.34), channel_id=1, source_target_pairs={{0,3},{1,0},{2,1},{3,2},{4,7},{5,4},{6,5},{7,6},{8,11},{9,8},{10,9... | collective-permute-start | bytes 983048 | tf_op jit(solution)/shard_map/ppermute | solution.py:289
  85.5 21.1 %collective-permute-start.8 = (bf16[160,1024]{1,0:T(8,128)(2,1)S(1)}, bf16[160,1024]{1,0:T(8,128)(2,1)S(1)}, u32[]{:S(2)}, u32[]{:S(2)}) collective-permute-start(bf16[160,1024]{1,0:T(8,128)(2,1)S(1)} %get-tuple-element.35), channel_id=1, source_target_pairs={{0,1},{1,2},{2,3},{3,0},{4,5},{5,6},{6,7},{7,4},{8,9},{9,10},{10,1... | collective-permute-start | bytes 983048 | tf_op jit(solution)/shard_map/ppermute | solution.py:289

commit v6 on v5

--- a/solution.py
+++ b/solution.py
@@ -43,23 +43,25 @@
         ]
 
 
-def pack_text_body(queries, cotangent, out, sems):
+def pack_text_body(place, queries, cotangent, after, *refs, shifts):
+    del after
+    outs, sems = refs[:-1], refs[-1]
     half = queries.shape[2] // 2
     width = half // PARTS
     copies = []
-    for g in range(PARTS):
+    for n, shift in enumerate(shifts):
+        g = wrap(place[1] + shift)
+        first = pl.multiple_of(g * width, width)
+        second = pl.multiple_of(half + g * width, width)
+        wide = pl.multiple_of(2 * g * width, 2 * width)
         pieces = (
-            (queries, g * width, 0, width),
-            (queries, half + g * width, width, width),
-            (cotangent, 2 * g * width, 2 * width, 2 * width),
+            (queries.at[:, :, pl.ds(first, width)], pl.ds(0, width)),
+            (queries.at[:, :, pl.ds(second, width)], pl.ds(width, width)),
+            (cotangent.at[:, :, pl.ds(wide, 2 * width)], pl.ds(2 * width, 2 * width)),
         )
-        for i, (source, first, to, size) in enumerate(pieces):
+        for i, (source, columns) in enumerate(pieces):
             copies.append(
-                pltpu.make_async_copy(
-                    source.at[:, :, pl.ds(first, size)],
-                    out.at[g, :, :, pl.ds(to, size)],
-                    sems.at[g, i],
-                )
+                pltpu.make_async_copy(source, outs[n].at[:, :, columns], sems.at[n, i])
             )
     for copy in copies:
         copy.start()
@@ -70,13 +72,11 @@
 def attend_body(
     place, assignment, counts, lambdas, norm_gain, gate, *refs, heads, head_size, patch
 ):
-    text = refs[0]
-    vision, payload, grad_vision = (refs[1 + i * PARTS : 1 + (i + 1) * PARTS] for i in range(3))
+    text, vision, payload, grad_vision = (refs[i * PARTS : (i + 1) * PARTS] for i in range(4))
     vision = [vision[LATE.index(k)] for k in range(PARTS)]
-    stats, gain, bias, raw_gain = refs[1 + 3 * PARTS :]
+    stats, gain, bias, raw_gain = refs[4 * PARTS :]
     zl, x = place[0], place[1]
-    seqs, toks = text.shape[1:3]
-    sources = [wrap(x - k) for k in ORDER]
+    seqs, toks = text[0].shape[:2]
     rows = PARTS * toks
     frames = PARTS * PARTS
     keys = frames * patch
@@ -133,7 +133,7 @@
         key_rows = {(h, v, m): of_video(joined[h, m], v) for h, v, m in both}
         queries = {
             (h, v, m): jnp.concatenate(
-                [text[i, place_of[v], :, map_columns(h, m)] for i in sources], axis=0
+                [part[place_of[v], :, map_columns(h, m)] for part in text], axis=0
             )
             for h, v, m in both
         }
@@ -152,7 +152,7 @@
             (h, v): dot(
                 eye,
                 jnp.concatenate(
-                    [text[i, place_of[v], :, value_columns(h)] for i in sources], axis=0
+                    [part[place_of[v], :, value_columns(h)] for part in text], axis=0
                 ),
                 (1, 1),
             )
@@ -310,8 +310,8 @@
     return lax.all_to_all(value, axes, 0, 0, tiled=True)
 
 
-def attend_call(place, assignment, counts, lambdas, norm_gain, gate, text, *vision):
-    seqs, toks, columns = text.shape[1:]
+def attend_call(place, assignment, counts, lambdas, norm_gain, gate, text, vision):
+    seqs, toks, columns = text[0].shape
     head_count, head_size = lambdas.shape[1:]
     heads = head_count // PARTS
     slab = vision[0].shape
@@ -323,14 +323,14 @@
         [shaped((seqs * toks + 2 * rows, columns // 2))] * PARTS
         + [shaped(slab)] * PARTS
         + [shaped((FIRST, 4, head_size), f32)],
-        [SMEM] * 3 + [VMEM] * (4 + PARTS),
+        [SMEM] * 3 + [VMEM] * (3 + 2 * PARTS),
         [VMEM] * (2 * PARTS + 1),
         scratch_shapes=[
             pltpu.VMEM((2 * head_size, PARTS * toks), f32),
             pltpu.VMEM((seqs, PARTS * PARTS * rows // seqs, PARTS * toks), f32),
             pltpu.VMEM((2 * head_size, head_size), f32),
         ],
-    )(place, assignment, counts, lambdas, norm_gain, gate, text, *vision)
+    )(place, assignment, counts, lambdas, norm_gain, gate, *text, *vision)
 
 
 def shards(queries, vision, cotangent, assignment, frame_counts, lambdas, norm_gain, gate_logit):
@@ -348,14 +348,17 @@
         vision.reshape(rows, vision_columns)
     )
     row_vision = exchange(sent_vision, "x")
-    sent_text = kernel(
-        pack_text_body,
-        shaped((PARTS, seqs, toks, 2 * text_columns // PARTS)),
-        [ANY] * 2,
-        ANY,
-        scratch_shapes=[pltpu.SemaphoreType.DMA((PARTS, 3))],
-    )(queries, cotangent)
-    held_text = exchange(sent_text, "x")
+    sent_text = {}
+    for shifts, after in (((2,), place), ((0, 1, 3), row_vision)):
+        packed = kernel(
+            functools.partial(pack_text_body, shifts=shifts),
+            [shaped((seqs, toks, 2 * text_columns // PARTS))] * len(shifts),
+            [SMEM, ANY, ANY, ANY],
+            [ANY] * len(shifts),
+            scratch_shapes=[pltpu.SemaphoreType.DMA((len(shifts), 3))],
+        )(place, queries, cotangent, after)
+        sent_text.update(zip(shifts, packed))
+    held_text = shift_all([sent_text[k] for k in ORDER], "x", ORDER, 1)
     held_vision = shift_all([row_vision] * PARTS, "zl", LATE, 1)
 
     grads = attend_call(
@@ -366,7 +369,7 @@
         norm_gain.reshape(1, -1),
         gate,
         held_text,
-        *held_vision,
+        held_vision,
     )
     payload, grad_vision, stats = grads[:PARTS], grads[PARTS : 2 * PARTS], grads[2 * PARTS]
 

time: 109 us -> 107 us (0.982)
  waiting for transfers between devices: 14.7 us -> 3.34 us
  starting transfers between devices: 42.4 us -> 50.4 us
  local copies, waits for them, and re-layouts: 4.72 us -> 2.92 us
  blocking collectives: 37.1 us -> 38.9 us
    ppermute x9 -> x12, starting transfers between devices: 33.9 us -> 45.6 us  [shift_all(): lax.ppermute(part, axis, [(i, (i + way * k) % PARTS) for i in range(PARTS)])]
    ppermute x9 -> x12, waiting for transfers between devices: 13.3 us -> 3.34 us  [shift_all(): lax.ppermute(part, axis, [(i, (i + way * k) % PARTS) for i in range(PARTS)])]
    all_to_all x2 -> x1, starting transfers between devices: 8.45 us -> 4.84 us  [exchange(): return lax.all_to_all(value, axes, 0, 0, tiled=True)]
    all_to_all x2, blocking collectives: 37.1 us -> 38.9 us  [exchange(): return lax.all_to_all(value, axes, 0, 0, tiled=True)]
    unnamed x16, local copies, waits for them, and re-layouts: 4.72 us -> 2.92 us
    all_to_all x2 -> x1, waiting for transfers between devices: 1.38 us -> 0.01 us  [exchange(): return lax.all_to_all(value, axes, 0, 0, tiled=True)]
    pallas_call x1 -> x2, Pallas kernels: 0.36 us -> 1.47 us  [shards(): kernel(functools.partial(pack_text_body, shifts=shifts), [shaped((seqs, t...]
  transfers between devices with their start and end apart: 11 -> 13, of which waited for: 3 -> 1; matrix products, arithmetic and copies ran while one was open for 0% -> 0% of each run, Pallas kernels for 0% -> 1%
where the time goes in v6:
time: 107 us; the launch traced here: 106 us
  starting transfers between devices  50.4 us (47%)
  blocking collectives  38.9 us (36%)
  Pallas kernels  9.03 us (8%)
  waiting for transfers between devices  3.34 us (3%)
  local copies, waits for them, and re-layouts  2.92 us (3%)
  between operations  1.52 us (1%)
    ppermute x12, starting transfers between devices, shift_all(): lax.ppermute(part, axis, [(i, (i + way * k) % PARTS) for i in range(PARTS)])  45.6 us
    all_to_all x2, blocking collectives, exchange(): return lax.all_to_all(value, axes, 0, 0, tiled=True)  38.9 us
    all_to_all x1, starting transfers between devices, exchange(): return lax.all_to_all(value, axes, 0, 0, tiled=True)  4.84 us
    pallas_call x1, Pallas kernels, attend_call(): kernel(functools.partial(attend_body, heads=heads, head_size=head_size, p...  4.04 us
    ppermute x12, waiting for transfers between devices, shift_all(): lax.ppermute(part, axis, [(i, (i + way * k) % PARTS) for i in range(PARTS)])  3.34 us
    unnamed x16, local copies, waits for them, and re-layouts  2.92 us
  transfers between devices with their start and end apart: 13, of which 1 were waited for; matrix products, arithmetic and copies ran while one was open for 0% of the time, Pallas kernels for 1%

profile of v6, /device:TPU:1, one launch (start us, length us, event | category | flops | bytes accessed | tf_op | source)
XLA Modules:
  0.0 106.3 jit_solution(9527166832632225563)
XLA Ops:
  0.7 1.0 copy-done.3
  1.7 0.7 shard_map.119
  2.4 4.8 %all-to-all-start = ((bf16[4,16,2048]{2,1,0:T(8,128)(2,1)}), bf16[4,16,2048]{2,1,0:T(8,128)(2,1)S(1)}, u32[]{:S(2)}, u32[]{:S(2)}) async-start(bf16[4,16,2048]{2,1,0:T(8,128)(2,1)} %shard_map.119), calls=%async_computation | async-start | bytes 524288 | tf_op jit(solution)/shard_map/all_to_all | solution.py:310
  7.3 1.2 %copy-done.1 = bf16[2,64,4096]{2,1,0:T(8,128)(2,1)S(1)} copy-done((bf16[2,64,4096]{2,1,0:T(8,128)(2,1)S(1)}, bf16[2,64,4096]{2,1,0:T(8,128)(2,1)}, u32[]{:S(2)}) %copy-start.1) | copy-done | bytes 1048600
  8.5 0.6 shard_map.121
  9.2 4.9 %collective-permute-start = (bf16[2,64,2048]{2,1,0:T(8,128)(2,1)S(1)}, bf16[2,64,2048]{2,1,0:T(8,128)(2,1)S(1)}, u32[]{:S(2)}, u32[]{:S(2)}) collective-permute-start(bf16[2,64,2048]{2,1,0:T(8,128)(2,1)S(1)} %shard_map.121), channel_id=1, source_target_pairs={{0,2},{1,3},{2,0},{3,1},{4,6},{5,7},{6,4},{7,5},{8,10},{9,11},{10,... | collective-permute-start | bytes 1572872 | tf_op jit(solution)/shard_map/ppermute | solution.py:289
  14.1 5.8 %collective-permute-start.5 = (bf16[4,16,2048]{2,1,0:T(8,128)(2,1)S(1)}, bf16[4,16,2048]{2,1,0:T(8,128)(2,1)S(1)}, u32[]{:S(2)}, u32[]{:S(2)}) collective-permute-start(bf16[4,16,2048]{2,1,0:T(8,128)(2,1)S(1)} %all-to-all-done.after.refs_4_), channel_id=1, source_target_pairs={{0,8},{4,12},{8,0},{12,4},{1,9},{5,13},{9,1},{13,5},{2,10},{6,14},... | collective-permute-start | bytes 786440 | tf_op jit(solution)/shard_map/ppermute | solution.py:289
  19.9 0.8 shard_map.120
  20.8 2.2 %collective-permute-start.1 = (bf16[2,64,2048]{2,1,0:T(8,128)(2,1)S(1)}, bf16[2,64,2048]{2,1,0:T(8,128)(2,1)S(1)}, u32[]{:S(2)}, u32[]{:S(2)}) collective-permute-start(bf16[2,64,2048]{2,1,0:T(8,128)(2,1)S(1)} %get-tuple-element.27), channel_id=1, source_target_pairs={{0,1},{1,2},{2,3},{3,0},{4,5},{5,6},{6,7},{7,4},{8,9},{9,10},{10,1... | collective-permute-start | bytes 1572872 | tf_op jit(solution)/shard_map/ppermute | solution.py:289
  23.0 4.3 %collective-permute-start.2 = (bf16[2,64,2048]{2,1,0:T(8,128)(2,1)S(1)}, bf16[2,64,2048]{2,1,0:T(8,128)(2,1)S(1)}, u32[]{:S(2)}, u32[]{:S(2)}) collective-permute-start(bf16[2,64,2048]{2,1,0:T(8,128)(2,1)S(1)} %get-tuple-element.28), channel_id=1, source_target_pairs={{0,3},{1,0},{2,1},{3,2},{4,7},{5,4},{6,5},{7,6},{8,11},{9,8},{10,9... | collective-permute-start | bytes 1572872 | tf_op jit(solution)/shard_map/ppermute | solution.py:289
  27.3 4.0 %collective-permute-start.4 = (bf16[4,16,2048]{2,1,0:T(8,128)(2,1)S(1)}, bf16[4,16,2048]{2,1,0:T(8,128)(2,1)S(1)}, u32[]{:S(2)}, u32[]{:S(2)}) collective-permute-start(bf16[4,16,2048]{2,1,0:T(8,128)(2,1)S(1)} %all-to-all-done.after.refs_4_), channel_id=1, source_target_pairs={{0,4},{4,8},{8,12},{12,0},{1,5},{5,9},{9,13},{13,1},{2,6},{6,10},{... | collective-permute-start | bytes 786440 | tf_op jit(solution)/shard_map/ppermute | solution.py:289
  31.3 6.2 %collective-permute-start.3 = (bf16[4,16,2048]{2,1,0:T(8,128)(2,1)S(1)}, bf16[4,16,2048]{2,1,0:T(8,128)(2,1)S(1)}, u32[]{:S(2)}, u32[]{:S(2)}) collective-permute-start(bf16[4,16,2048]{2,1,0:T(8,128)(2,1)S(1)} %all-to-all-done.after.refs_4_), channel_id=1, source_target_pairs={{0,12},{4,0},{8,4},{12,8},{1,13},{5,1},{9,5},{13,9},{2,14},{6,2},{... | collective-permute-start | bytes 786440 | tf_op jit(solution)/shard_map/ppermute | solution.py:289
  38.1 3.3 %collective-permute-done.3.refs_5_ = bf16[4,16,2048]{2,1,0:T(8,128)(2,1)S(1)} collective-permute-done((bf16[4,16,2048]{2,1,0:T(8,128)(2,1)S(1)}, bf16[4,16,2048]{2,1,0:T(8,128)(2,1)S(1)}, u32[]{:S(2)}, u32[]{:S(2)}) %collective-permute-start.3) | collective-permute-done | bytes 262176 | tf_op jit(solution)/shard_map/ppermute | solution.py:289
  42.1 4.0 %shard_map.122 = (bf16[160,1024]{1,0:T(8,128)(2,1)S(1)}, bf16[160,1024]{1,0:T(8,128)(2,1)S(1)}, bf16[160,1024]{1,0:T(8,128)(2,1)S(1)}, bf16[160,1024]{1,0:T(8,12...) custom-call(s32[2]{0:T(128)S(1)} %pad_add_fusion.place.after, ...), custom_call_target="tpu_custom_call" | custom-call | tf_op jit(solution)/shard_map/pallas_call | solution.py:319
  46.2 5.7 %collective-permute-start.6 = (bf16[4,16,2048]{2,1,0:T(8,128)(2,1)S(1)}, bf16[4,16,2048]{2,1,0:T(8,128)(2,1)S(1)}, u32[]{:S(2)}, u32[]{:S(2)}) collective-permute-start(bf16[4,16,2048]{2,1,0:T(8,128)(2,1)S(1)} %get-tuple-element.31), channel_id=1, source_target_pairs={{0,12},{4,0},{8,4},{12,8},{1,13},{5,1},{9,5},{13,9},{2,14},{6,2},{... | collective-permute-start | bytes 786440 | tf_op jit(solution)/shard_map/ppermute | solution.py:289
  51.9 1.9 %collective-permute-start.7 = (bf16[4,16,2048]{2,1,0:T(8,128)(2,1)S(1)}, bf16[4,16,2048]{2,1,0:T(8,128)(2,1)S(1)}, u32[]{:S(2)}, u32[]{:S(2)}) collective-permute-start(bf16[4,16,2048]{2,1,0:T(8,128)(2,1)S(1)} %get-tuple-element.32), channel_id=1, source_target_pairs={{0,8},{4,12},{8,0},{12,4},{1,9},{5,13},{9,1},{13,5},{2,10},{6,14},... | collective-permute-start | bytes 786440 | tf_op jit(solution)/shard_map/ppermute | solution.py:289
  53.9 2.2 %collective-permute-start.8 = (bf16[4,16,2048]{2,1,0:T(8,128)(2,1)S(1)}, bf16[4,16,2048]{2,1,0:T(8,128)(2,1)S(1)}, u32[]{:S(2)}, u32[]{:S(2)}) collective-permute-start(bf16[4,16,2048]{2,1,0:T(8,128)(2,1)S(1)} %get-tuple-element.33), channel_id=1, source_target_pairs={{0,4},{4,8},{8,12},{12,0},{1,5},{5,9},{9,13},{13,1},{2,6},{6,10},{... | collective-permute-start | bytes 786440 | tf_op jit(solution)/shard_map/ppermute | solution.py:289
  56.1 17.8 %all_to_all.15.after.tiles = f32[32,4,128]{2,1,0:T(4,128)S(1)} all-to-all(f32[32,4,128]{2,1,0:T(4,128)S(1)} %get-tuple-element.29), channel_id=1, replica_groups=mesh['y'=8,'zh'=2,'core'=2,'zl'=4,'x'=4] {'y','x'}, dimensions={0} | all-to-all | bytes 131072 | tf_op jit(solution)/shard_map/all_to_all | solution.py:310
  73.8 1.1 %shard_map.123 = (bf16[160,1024]{1,0:T(8,128)(2,1)S(1)}, bf16[160,1024]{1,0:T(8,128)(2,1)S(1)}, bf16[160,1024]{1,0:T(8,128)(2,1)S(1)}, bf16[160,1024]{1,0:T(8,128)(2,1)S(1)}) custom-call(s32[2]{0:T(128)S(1)} %pad_add_fusion.place.after, ...), custom_call_target="tpu_custom_call", output_to_operand_aliasing={{0}: (6, {}), {1}: (7, {}), {2}: (8, {}), {3}: (9, {})} | custom-call | tf_op jit(solution)/shard_map/pallas_call | solution.py:378
  74.9 2.9 %collective-permute-start.9 = (bf16[160,1024]{1,0:T(8,128)(2,1)S(1)}, bf16[160,1024]{1,0:T(8,128)(2,1)S(1)}, u32[]{:S(2)}, u32[]{:S(2)}) collective-permute-start(bf16[160,1024]{1,0:T(8,128)(2,1)S(1)} %get-tuple-element.39), channel_id=1, source_target_pairs={{0,2},{1,3},{2,0},{3,1},{4,6},{5,7},{6,4},{7,5},{8,10},{9,11},{10,... | collective-permute-start | bytes 983048 | tf_op jit(solution)/shard_map/ppermute | solution.py:289
  77.8 3.6 %collective-permute-start.10 = (bf16[160,1024]{1,0:T(8,128)(2,1)S(1)}, bf16[160,1024]{1,0:T(8,128)(2,1)S(1)}, u32[]{:S(2)}, u32[]{:S(2)}) collective-permute-start(bf16[160,1024]{1,0:T(8,128)(2,1)S(1)} %get-tuple-element.40), channel_id=1, source_target_pairs={{0,3},{1,0},{2,1},{3,2},{4,7},{5,4},{6,5},{7,6},{8,11},{9,8},{10,9... | collective-permute-start | bytes 983048 | tf_op jit(solution)/shard_map/ppermute | solution.py:289
  81.4 1.9 %collective-permute-start.11 = (bf16[160,1024]{1,0:T(8,128)(2,1)S(1)}, bf16[160,1024]{1,0:T(8,128)(2,1)S(1)}, u32[]{:S(2)}, u32[]{:S(2)}) collective-permute-start(bf16[160,1024]{1,0:T(8,128)(2,1)S(1)} %get-tuple-element.41), channel_id=1, source_target_pairs={{0,1},{1,2},{2,3},{3,0},{4,5},{5,6},{6,7},{7,4},{8,9},{9,10},{10,1... | collective-permute-start | bytes 983048 | tf_op jit(solution)/shard_map/ppermute | solution.py:289
  83.4 21.2 %all_to_all.16.tiles = f32[16,4,128]{2,1,0:T(4,128)S(1)} all-to-all(f32[16,4,128]{2,1,0:T(4,128)S(1)} %shard_map.124), channel_id=1, replica_groups=mesh['y'=8,'zh'=2,'core'=2,'zl'=4,'x'=4] {'zh','core','zl'}, dimensions={0} | all-to-all | bytes 65536 | tf_op jit(solution)/shard_map/all_to_all | solution.py:310
  104.6 1.7 %shard_map.125 = (bf16[128,4096]{1,0:T(8,128)(2,1)}, bf16[16,8192]{1,0:T(8,128)(2,1)}, f32[4,16,128]{2,1,0:T(8,128)}, f32[2,128]{1,0:T(2,128)}, f32[1,1]{1,0:T(1,128)}) custom-call(s32[2]{0:T(128)S(1)} %pad_add_fusion.place.after, f32[16,4,128]{2,1,0:T(4,128)S(1)} %all_to_all.16.tiles, f32[4,16,128]{2,1,0:T(8,128)S(1)} %copy-done.4, f32[2,128]{1,0:T(2,128)S(1)} %bitcast.16, ...), custom_call_target="tpu_custom_call" | custom-call | tf_op jit(solution)/shard_map/pallas_call | solution.py:394
  (28 shorter events, 0.8 us)
Async XLA Ops:
  0.6 6.7 %copy-start = (bf16[2,64,4096]{2,1,0:T(8,128)(2,1)S(1)}, bf16[2,64,4096]{2,1,0:T(8,128)(2,1)}, u32[]{:S(2)}) copy-start(bf16[2,64,4096]{2,1,0:T(8,128)(2,1)} %queries.3) | copy-start | bytes 3145732
  0.6 1.0 copy-start.3
  2.4 11.7 %all-to-all-start = ((bf16[4,16,2048]{2,1,0:T(8,128)(2,1)}), bf16[4,16,2048]{2,1,0:T(8,128)(2,1)S(1)}, u32[]{:S(2)}, u32[]{:S(2)}) async-start(bf16[4,16,2048]{2,1,0:T(8,128)(2,1)} %shard_map.119), calls=%async_computation | async-start | bytes 524288 | tf_op jit(solution)/shard_map/all_to_all | solution.py:310
  7.3 1.2 %copy-start.1 = (bf16[2,64,4096]{2,1,0:T(8,128)(2,1)S(1)}, bf16[2,64,4096]{2,1,0:T(8,128)(2,1)}, u32[]{:S(2)}) copy-start(bf16[2,64,4096]{2,1,0:T(8,128)(2,1)} %cotangent.3) | copy-start | bytes 3145732
  8.5 11.4 %copy-start.2 = (bf16[2,64,4096]{2,1,0:T(8,128)(2,1)S(1)}, bf16[2,64,4096]{2,1,0:T(8,128)(2,1)}, u32[]{:S(2)}) copy-start(bf16[2,64,4096]{2,1,0:T(8,128)(2,1)} %cotangent.3) | copy-start | bytes 3145732
  9.2 32.3 %collective-permute-start = (bf16[2,64,2048]{2,1,0:T(8,128)(2,1)S(1)}, bf16[2,64,2048]{2,1,0:T(8,128)(2,1)S(1)}, u32[]{:S(2)}, u32[]{:S(2)}) collective-permute-start(bf16[2,64,2048]{2,1,0:T(8,128)(2,1)S(1)} %shard_map.121), channel_id=1, source_target_pairs={{0,2},{1,3},{2,0},{3,1},{4,6},{5,7},{6,4},{7,5},{8,10},{9,11},{10,... | collective-permute-start | bytes 1572872 | tf_op jit(solution)/shard_map/ppermute | solution.py:289
  14.1 17.2 %collective-permute-start.5 = (bf16[4,16,2048]{2,1,0:T(8,128)(2,1)S(1)}, bf16[4,16,2048]{2,1,0:T(8,128)(2,1)S(1)}, u32[]{:S(2)}, u32[]{:S(2)}) collective-permute-start(bf16[4,16,2048]{2,1,0:T(8,128)(2,1)S(1)} %all-to-all-done.after.refs_4_), channel_id=1, source_target_pairs={{0,8},{4,12},{8,0},{12,4},{1,9},{5,13},{9,1},{13,5},{2,10},{6,14},... | collective-permute-start | bytes 786440 | tf_op jit(solution)/shard_map/ppermute | solution.py:289
  19.9 21.6 %copy-start.4 = (f32[4,16,128]{2,1,0:T(8,128)S(1)}, f32[4,16,128]{2,1,0:T(8,128)}, u32[]{:S(2)}) copy-start(f32[4,16,128]{2,1,0:T(8,128)} %lambdas.3) | copy-start | bytes 98308
  19.9 21.6 %copy-start.7 = (s32[2]{0:T(128)S(1)}, s32[2]{0:T(128)}, u32[]{:S(2)}) copy-start(s32[2]{0:T(128)} %counts.1) | copy-start | bytes 28
  20.8 20.7 %collective-permute-start.1 = (bf16[2,64,2048]{2,1,0:T(8,128)(2,1)S(1)}, bf16[2,64,2048]{2,1,0:T(8,128)(2,1)S(1)}, u32[]{:S(2)}, u32[]{:S(2)}) collective-permute-start(bf16[2,64,2048]{2,1,0:T(8,128)(2,1)S(1)} %get-tuple-element.27), channel_id=1, source_target_pairs={{0,1},{1,2},{2,3},{3,0},{4,5},{5,6},{6,7},{7,4},{8,9},{9,10},{10,1... | collective-permute-start | bytes 1572872 | tf_op jit(solution)/shard_map/ppermute | solution.py:289
  23.0 18.5 %collective-permute-start.2 = (bf16[2,64,2048]{2,1,0:T(8,128)(2,1)S(1)}, bf16[2,64,2048]{2,1,0:T(8,128)(2,1)S(1)}, u32[]{:S(2)}, u32[]{:S(2)}) collective-permute-start(bf16[2,64,2048]{2,1,0:T(8,128)(2,1)S(1)} %get-tuple-element.28), channel_id=1, source_target_pairs={{0,3},{1,0},{2,1},{3,2},{4,7},{5,4},{6,5},{7,6},{8,11},{9,8},{10,9... | collective-permute-start | bytes 1572872 | tf_op jit(solution)/shard_map/ppermute | solution.py:289
  27.3 10.8 %collective-permute-start.4 = (bf16[4,16,2048]{2,1,0:T(8,128)(2,1)S(1)}, bf16[4,16,2048]{2,1,0:T(8,128)(2,1)S(1)}, u32[]{:S(2)}, u32[]{:S(2)}) collective-permute-start(bf16[4,16,2048]{2,1,0:T(8,128)(2,1)S(1)} %all-to-all-done.after.refs_4_), channel_id=1, source_target_pairs={{0,4},{4,8},{8,12},{12,0},{1,5},{5,9},{9,13},{13,1},{2,6},{6,10},{... | collective-permute-start | bytes 786440 | tf_op jit(solution)/shard_map/ppermute | solution.py:289
  31.3 10.1 %collective-permute-start.3 = (bf16[4,16,2048]{2,1,0:T(8,128)(2,1)S(1)}, bf16[4,16,2048]{2,1,0:T(8,128)(2,1)S(1)}, u32[]{:S(2)}, u32[]{:S(2)}) collective-permute-start(bf16[4,16,2048]{2,1,0:T(8,128)(2,1)S(1)} %all-to-all-done.after.refs_4_), channel_id=1, source_target_pairs={{0,12},{4,0},{8,4},{12,8},{1,13},{5,1},{9,5},{13,9},{2,14},{6,2},{... | collective-permute-start | bytes 786440 | tf_op jit(solution)/shard_map/ppermute | solution.py:289
  41.5 0.7 copy-start.5
  41.5 0.7 copy-start.6
  46.2 27.6 %collective-permute-start.6 = (bf16[4,16,2048]{2,1,0:T(8,128)(2,1)S(1)}, bf16[4,16,2048]{2,1,0:T(8,128)(2,1)S(1)}, u32[]{:S(2)}, u32[]{:S(2)}) collective-permute-start(bf16[4,16,2048]{2,1,0:T(8,128)(2,1)S(1)} %get-tuple-element.31), channel_id=1, source_target_pairs={{0,12},{4,0},{8,4},{12,8},{1,13},{5,1},{9,5},{13,9},{2,14},{6,2},{... | collective-permute-start | bytes 786440 | tf_op jit(solution)/shard_map/ppermute | solution.py:289
  51.9 21.9 %collective-permute-start.7 = (bf16[4,16,2048]{2,1,0:T(8,128)(2,1)S(1)}, bf16[4,16,2048]{2,1,0:T(8,128)(2,1)S(1)}, u32[]{:S(2)}, u32[]{:S(2)}) collective-permute-start(bf16[4,16,2048]{2,1,0:T(8,128)(2,1)S(1)} %get-tuple-element.32), channel_id=1, source_target_pairs={{0,8},{4,12},{8,0},{12,4},{1,9},{5,13},{9,1},{13,5},{2,10},{6,14},... | collective-permute-start | bytes 786440 | tf_op jit(solution)/shard_map/ppermute | solution.py:289
  53.9 20.0 %collective-permute-start.8 = (bf16[4,16,2048]{2,1,0:T(8,128)(2,1)S(1)}, bf16[4,16,2048]{2,1,0:T(8,128)(2,1)S(1)}, u32[]{:S(2)}, u32[]{:S(2)}) collective-permute-start(bf16[4,16,2048]{2,1,0:T(8,128)(2,1)S(1)} %get-tuple-element.33), channel_id=1, source_target_pairs={{0,4},{4,8},{8,12},{12,0},{1,5},{5,9},{9,13},{13,1},{2,6},{6,10},{... | collective-permute-start | bytes 786440 | tf_op jit(solution)/shard_map/ppermute | solution.py:289
  74.9 29.7 %collective-permute-start.9 = (bf16[160,1024]{1,0:T(8,128)(2,1)S(1)}, bf16[160,1024]{1,0:T(8,128)(2,1)S(1)}, u32[]{:S(2)}, u32[]{:S(2)}) collective-permute-start(bf16[160,1024]{1,0:T(8,128)(2,1)S(1)} %get-tuple-element.39), channel_id=1, source_target_pairs={{0,2},{1,3},{2,0},{3,1},{4,6},{5,7},{6,4},{7,5},{8,10},{9,11},{10,... | collective-permute-start | bytes 983048 | tf_op jit(solution)/shard_map/ppermute | solution.py:289
  77.8 26.8 %collective-permute-start.10 = (bf16[160,1024]{1,0:T(8,128)(2,1)S(1)}, bf16[160,1024]{1,0:T(8,128)(2,1)S(1)}, u32[]{:S(2)}, u32[]{:S(2)}) collective-permute-start(bf16[160,1024]{1,0:T(8,128)(2,1)S(1)} %get-tuple-element.40), channel_id=1, source_target_pairs={{0,3},{1,0},{2,1},{3,2},{4,7},{5,4},{6,5},{7,6},{8,11},{9,8},{10,9... | collective-permute-start | bytes 983048 | tf_op jit(solution)/shard_map/ppermute | solution.py:289
  81.4 23.2 %collective-permute-start.11 = (bf16[160,1024]{1,0:T(8,128)(2,1)S(1)}, bf16[160,1024]{1,0:T(8,128)(2,1)S(1)}, u32[]{:S(2)}, u32[]{:S(2)}) collective-permute-start(bf16[160,1024]{1,0:T(8,128)(2,1)S(1)} %get-tuple-element.41), channel_id=1, source_target_pairs={{0,1},{1,2},{2,3},{3,0},{4,5},{5,6},{6,7},{7,4},{8,9},{9,10},{10,1... | collective-permute-start | bytes 983048 | tf_op jit(solution)/shard_map/ppermute | solution.py:289

commit v7 on v6

--- a/solution.py
+++ b/solution.py
@@ -14,7 +14,8 @@
 FIRST, SECOND = 32, 16
 PARTS = 4
 GROUP = 2
-ORDER, LATE = (0, 2, 1, 3), (0, 3, 1, 2)
+ORDER = (0, 2, 1, 3)
+LATE = (0, 1, 3, 2)
 VMEM = pl.BlockSpec(memory_space=pltpu.VMEM)
 SMEM = pl.BlockSpec(memory_space=pltpu.SMEM)
 ANY = pl.BlockSpec(memory_space=pl.ANY)
@@ -43,9 +44,8 @@
         ]
 
 
-def pack_text_body(place, queries, cotangent, after, *refs, shifts):
-    del after
-    outs, sems = refs[:-1], refs[-1]
+def pack_text_body(place, queries, cotangent, *refs, shifts):
+    outs, sems = refs[-1 - len(shifts) : -1], refs[-1]
     half = queries.shape[2] // 2
     width = half // PARTS
     copies = []
@@ -98,7 +98,7 @@
     )
     spot = lax.broadcasted_iota(jnp.int32, (keys, rows), 0) // patch
     part = spot // PARTS
-    frame = wrap(zl - part) * PARTS + spot - part * PARTS
+    frame = (zl ^ part) * PARTS + spot - part * PARTS
     for v in range(seqs):
         bias[v] = jnp.where(frame < counts[v], 0.0, -jnp.inf)
     lane = lax.broadcasted_iota(jnp.int32, (1, head_size), 1)
@@ -284,11 +284,19 @@
     grad_lambdas[3] = -weight_two * lambdas[2]
 
 
-def shift_all(parts, axis, order, way):
+def send_all(parts, axis, targets):
     return [
-        lax.ppermute(part, axis, [(i, (i + way * k) % PARTS) for i in range(PARTS)]) if k else part
-        for part, k in zip(parts, order)
+        part if target is None else lax.ppermute(part, axis, [(i, target(i)) for i in range(PARTS)])
+        for part, target in zip(parts, targets)
     ]
+
+
+def shifts(order, way):
+    return [(lambda i, k=k: (i + way * k) % PARTS) if k else None for k in order]
+
+
+def partners(order):
+    return [(lambda i, k=k: i ^ k) if k else None for k in order]
 
 
 def kernel(body, out_shape, in_specs, out_specs, **more):
@@ -349,17 +357,18 @@
     )
     row_vision = exchange(sent_vision, "x")
     sent_text = {}
-    for shifts, after in (((2,), place), ((0, 1, 3), row_vision)):
+    early = (row_vision, norm_gain.reshape(1, -1), assignment, frame_counts)
+    for held, others in (((2,), ()), ((0, 1, 3), early)):
         packed = kernel(
-            functools.partial(pack_text_body, shifts=shifts),
-            [shaped((seqs, toks, 2 * text_columns // PARTS))] * len(shifts),
-            [SMEM, ANY, ANY, ANY],
-            [ANY] * len(shifts),
-            scratch_shapes=[pltpu.SemaphoreType.DMA((len(shifts), 3))],
-        )(place, queries, cotangent, after)
-        sent_text.update(zip(shifts, packed))
-    held_text = shift_all([sent_text[k] for k in ORDER], "x", ORDER, 1)
-    held_vision = shift_all([row_vision] * PARTS, "zl", LATE, 1)
+            functools.partial(pack_text_body, shifts=held),
+            [shaped((seqs, toks, 2 * text_columns // PARTS))] * len(held),
+            [SMEM, ANY, ANY] + [ANY, VMEM, SMEM, SMEM][: len(others)],
+            [ANY] * len(held),
+            scratch_shapes=[pltpu.SemaphoreType.DMA((len(held), 3))],
+        )(place, queries, cotangent, *others)
+        sent_text.update(zip(held, packed))
+    held_text = send_all([sent_text[k] for k in ORDER], "x", shifts(ORDER, 1))
+    held_vision = send_all([row_vision] * PARTS, "zl", partners(LATE))
 
     grads = attend_call(
         place,
@@ -373,7 +382,7 @@
     )
     payload, grad_vision, stats = grads[:PARTS], grads[PARTS : 2 * PARTS], grads[2 * PARTS]
 
-    back_vision = shift_all(grad_vision, "zl", range(PARTS), -1)
+    back_vision = send_all(grad_vision, "zl", partners(range(PARTS)))
     stats = exchange(stats, ("y", "x"))
     payload = kernel(
         sum_vision_body,
@@ -386,7 +395,7 @@
         ],
         input_output_aliases={2 + PARTS + k: k for k in range(PARTS)},
     )(place, stats, *back_vision, *payload)
-    back = shift_all(payload, "x", ORDER, -1)
+    back = send_all(payload, "x", shifts(ORDER, -1))
     stats = kernel(spread_sum_body, shaped((SECOND, 4, head_size), f32), [VMEM, ANY], VMEM)(
         stats, payload[0]
     )

time: 107 us -> 110 us (1.028)
  blocking collectives: 38.9 us -> 41.8 us
  waiting for transfers between devices: 3.34 us -> 5.06 us
    all_to_all x2, blocking collectives: 38.9 us -> 41.8 us  [exchange(): return lax.all_to_all(value, axes, 0, 0, tiled=True)]
    ppermute x12, waiting for transfers between devices: 3.34 us -> 5.06 us  [send_all(): lax.ppermute(part, axis, [(i, target(i)) for i in range(PARTS)])]
  transfers between devices with their start and end apart: 13 -> 13, of which waited for: 1 -> 2; matrix products, arithmetic and copies ran while one was open for 0% -> 0% of each run, Pallas kernels for 1% -> 1%
where the time goes in v7:
time: 110 us
  starting transfers between devices  49.7 us (45%)
  blocking collectives  41.8 us (38%)
  Pallas kernels  9.06 us (8%)
  waiting for transfers between devices  5.06 us (5%)
  local copies, waits for them, and re-layouts  2.29 us (2%)
  between operations  1.52 us (1%)
    ppermute x12, starting transfers between devices, send_all(): lax.ppermute(part, axis, [(i, target(i)) for i in range(PARTS)])  44.9 us
    all_to_all x2, blocking collectives, exchange(): return lax.all_to_all(value, axes, 0, 0, tiled=True)  41.8 us
    ppermute x12, waiting for transfers between devices, send_all(): lax.ppermute(part, axis, [(i, target(i)) for i in range(PARTS)])  5.06 us
    all_to_all x1, starting transfers between devices, exchange(): return lax.all_to_all(value, axes, 0, 0, tiled=True)  4.84 us
    pallas_call x1, Pallas kernels, attend_call(): kernel(functools.partial(attend_body, heads=heads, head_size=head_size, p...  4.05 us
    unnamed x16, local copies, waits for them, and re-layouts  2.29 us
  transfers between devices with their start and end apart: 13, of which 2 were waited for; matrix products, arithmetic and copies ran while one was open for 0% of the time, Pallas kernels for 1%

profile of v7, /device:TPU:1, one launch (start us, length us, event | category | flops | bytes accessed | tf_op | source)
XLA Modules:
  0.0 109.5 jit_solution(6593481939233900659)
XLA Ops:
  0.7 1.0 copy-done.3
  1.7 0.7 shard_map.119
  2.4 4.8 %all-to-all-start = ((bf16[4,16,2048]{2,1,0:T(8,128)(2,1)}), bf16[4,16,2048]{2,1,0:T(8,128)(2,1)S(1)}, u32[]{:S(2)}, u32[]{:S(2)}) async-start(bf16[4,16,2048]{2,1,0:T(8,128)(2,1)} %shard_map.119), calls=%async_computation | async-start | bytes 524288 | tf_op jit(solution)/shard_map/all_to_all | solution.py:318
  7.3 1.2 %copy-done.1 = bf16[2,64,4096]{2,1,0:T(8,128)(2,1)S(1)} copy-done((bf16[2,64,4096]{2,1,0:T(8,128)(2,1)S(1)}, bf16[2,64,4096]{2,1,0:T(8,128)(2,1)}, u32[]{:S(2)}) %copy-start.1) | copy-done | bytes 1048600
  9.2 4.9 %collective-permute-start = (bf16[2,64,2048]{2,1,0:T(8,128)(2,1)S(1)}, bf16[2,64,2048]{2,1,0:T(8,128)(2,1)S(1)}, u32[]{:S(2)}, u32[]{:S(2)}) collective-permute-start(bf16[2,64,2048]{2,1,0:T(8,128)(2,1)S(1)} %shard_map.121), channel_id=1, source_target_pairs={{0,2},{1,3},{2,0},{3,1},{4,6},{5,7},{6,4},{7,5},{8,10},{9,11},{10,... | collective-permute-start | bytes 1572872 | tf_op jit(solution)/shard_map/ppermute | solution.py:289
  14.1 5.8 %collective-permute-start.5 = (bf16[4,16,2048]{2,1,0:T(8,128)(2,1)S(1)}, bf16[4,16,2048]{2,1,0:T(8,128)(2,1)S(1)}, u32[]{:S(2)}, u32[]{:S(2)}) collective-permute-start(bf16[4,16,2048]{2,1,0:T(8,128)(2,1)S(1)} %all-to-all-done.refs_0_.refs_4_), channel_id=1, source_target_pairs={{0,8},{4,12},{8,0},{12,4},{1,9},{5,13},{9,1},{13,5},{2,10},{6,14},... | collective-permute-start | bytes 786440 | tf_op jit(solution)/shard_map/ppermute | solution.py:289
  20.0 0.8 shard_map.120
  20.8 2.2 %collective-permute-start.1 = (bf16[2,64,2048]{2,1,0:T(8,128)(2,1)S(1)}, bf16[2,64,2048]{2,1,0:T(8,128)(2,1)S(1)}, u32[]{:S(2)}, u32[]{:S(2)}) collective-permute-start(bf16[2,64,2048]{2,1,0:T(8,128)(2,1)S(1)} %get-tuple-element.27), channel_id=1, source_target_pairs={{0,1},{1,2},{2,3},{3,0},{4,5},{5,6},{6,7},{7,4},{8,9},{9,10},{10,1... | collective-permute-start | bytes 1572872 | tf_op jit(solution)/shard_map/ppermute | solution.py:289
  23.0 4.3 %collective-permute-start.2 = (bf16[2,64,2048]{2,1,0:T(8,128)(2,1)S(1)}, bf16[2,64,2048]{2,1,0:T(8,128)(2,1)S(1)}, u32[]{:S(2)}, u32[]{:S(2)}) collective-permute-start(bf16[2,64,2048]{2,1,0:T(8,128)(2,1)S(1)} %get-tuple-element.28), channel_id=1, source_target_pairs={{0,3},{1,0},{2,1},{3,2},{4,7},{5,4},{6,5},{7,6},{8,11},{9,8},{10,9... | collective-permute-start | bytes 1572872 | tf_op jit(solution)/shard_map/ppermute | solution.py:289
  27.3 3.7 %collective-permute-start.4 = (bf16[4,16,2048]{2,1,0:T(8,128)(2,1)S(1)}, bf16[4,16,2048]{2,1,0:T(8,128)(2,1)S(1)}, u32[]{:S(2)}, u32[]{:S(2)}) collective-permute-start(bf16[4,16,2048]{2,1,0:T(8,128)(2,1)S(1)} %all-to-all-done.refs_0_.refs_4_), channel_id=1, source_target_pairs={{0,12},{4,8},{8,4},{12,0},{1,13},{5,9},{9,5},{13,1},{2,14},{6,10},... | collective-permute-start | bytes 786440 | tf_op jit(solution)/shard_map/ppermute | solution.py:289
  31.1 3.5 %collective-permute-start.3 = (bf16[4,16,2048]{2,1,0:T(8,128)(2,1)S(1)}, bf16[4,16,2048]{2,1,0:T(8,128)(2,1)S(1)}, u32[]{:S(2)}, u32[]{:S(2)}) collective-permute-start(bf16[4,16,2048]{2,1,0:T(8,128)(2,1)S(1)} %all-to-all-done.refs_0_.refs_4_), channel_id=1, source_target_pairs={{0,4},{4,0},{8,12},{12,8},{1,5},{5,1},{9,13},{13,9},{2,6},{6,2},{1... | collective-permute-start | bytes 786440 | tf_op jit(solution)/shard_map/ppermute | solution.py:289
  35.3 1.1 %collective-permute-done.4.refs_6_ = bf16[4,16,2048]{2,1,0:T(8,128)(2,1)S(1)} collective-permute-done((bf16[4,16,2048]{2,1,0:T(8,128)(2,1)S(1)}, bf16[4,16,2048]{2,1,0:T(8,128)(2,1)S(1)}, u32[]{:S(2)}, u32[]{:S(2)}) %collective-permute-start.4) | collective-permute-done | bytes 262176 | tf_op jit(solution)/shard_map/ppermute | solution.py:289
  36.4 3.9 %collective-permute-done.3.refs_5_ = bf16[4,16,2048]{2,1,0:T(8,128)(2,1)S(1)} collective-permute-done((bf16[4,16,2048]{2,1,0:T(8,128)(2,1)S(1)}, bf16[4,16,2048]{2,1,0:T(8,128)(2,1)S(1)}, u32[]{:S(2)}, u32[]{:S(2)}) %collective-permute-start.3) | collective-permute-done | bytes 262176 | tf_op jit(solution)/shard_map/ppermute | solution.py:289
  40.3 4.1 %shard_map.122 = (bf16[160,1024]{1,0:T(8,128)(2,1)S(1)}, bf16[160,1024]{1,0:T(8,128)(2,1)S(1)}, bf16[160,1024]{1,0:T(8,128)(2,1)S(1)}, bf16[160,1024]{1,0:T(8,12...) custom-call(s32[2]{0:T(128)S(1)} %pad_add_fusion.place, ...), custom_call_target="tpu_custom_call" | custom-call | tf_op jit(solution)/shard_map/pallas_call | solution.py:327
  44.4 4.1 %collective-permute-start.6 = (bf16[4,16,2048]{2,1,0:T(8,128)(2,1)S(1)}, bf16[4,16,2048]{2,1,0:T(8,128)(2,1)S(1)}, u32[]{:S(2)}, u32[]{:S(2)}) collective-permute-start(bf16[4,16,2048]{2,1,0:T(8,128)(2,1)S(1)} %get-tuple-element.31), channel_id=1, source_target_pairs={{0,4},{4,0},{8,12},{12,8},{1,5},{5,1},{9,13},{13,9},{2,6},{6,2},{1... | collective-permute-start | bytes 786440 | tf_op jit(solution)/shard_map/ppermute | solution.py:289
  48.5 5.9 %collective-permute-start.7 = (bf16[4,16,2048]{2,1,0:T(8,128)(2,1)S(1)}, bf16[4,16,2048]{2,1,0:T(8,128)(2,1)S(1)}, u32[]{:S(2)}, u32[]{:S(2)}) collective-permute-start(bf16[4,16,2048]{2,1,0:T(8,128)(2,1)S(1)} %get-tuple-element.32), channel_id=1, source_target_pairs={{0,8},{4,12},{8,0},{12,4},{1,9},{5,13},{9,1},{13,5},{2,10},{6,14},... | collective-permute-start | bytes 786440 | tf_op jit(solution)/shard_map/ppermute | solution.py:289
  54.5 1.9 %collective-permute-start.8 = (bf16[4,16,2048]{2,1,0:T(8,128)(2,1)S(1)}, bf16[4,16,2048]{2,1,0:T(8,128)(2,1)S(1)}, u32[]{:S(2)}, u32[]{:S(2)}) collective-permute-start(bf16[4,16,2048]{2,1,0:T(8,128)(2,1)S(1)} %get-tuple-element.33), channel_id=1, source_target_pairs={{0,12},{4,8},{8,4},{12,0},{1,13},{5,9},{9,5},{13,1},{2,14},{6,10},... | collective-permute-start | bytes 786440 | tf_op jit(solution)/shard_map/ppermute | solution.py:289
  56.4 20.6 %all_to_all.15.after.tiles = f32[32,4,128]{2,1,0:T(4,128)S(1)} all-to-all(f32[32,4,128]{2,1,0:T(4,128)S(1)} %get-tuple-element.29), channel_id=1, replica_groups=mesh['y'=8,'zh'=2,'core'=2,'zl'=4,'x'=4] {'y','x'}, dimensions={0} | all-to-all | bytes 131072 | tf_op jit(solution)/shard_map/all_to_all | solution.py:318
  77.0 1.1 shard_map.123
  78.1 2.9 %collective-permute-start.9 = (bf16[160,1024]{1,0:T(8,128)(2,1)S(1)}, bf16[160,1024]{1,0:T(8,128)(2,1)S(1)}, u32[]{:S(2)}, u32[]{:S(2)}) collective-permute-start(bf16[160,1024]{1,0:T(8,128)(2,1)S(1)} %get-tuple-element.39), channel_id=1, source_target_pairs={{0,2},{1,3},{2,0},{3,1},{4,6},{5,7},{6,4},{7,5},{8,10},{9,11},{10,... | collective-permute-start | bytes 983048 | tf_op jit(solution)/shard_map/ppermute | solution.py:289
  81.0 3.6 %collective-permute-start.10 = (bf16[160,1024]{1,0:T(8,128)(2,1)S(1)}, bf16[160,1024]{1,0:T(8,128)(2,1)S(1)}, u32[]{:S(2)}, u32[]{:S(2)}) collective-permute-start(bf16[160,1024]{1,0:T(8,128)(2,1)S(1)} %get-tuple-element.40), channel_id=1, source_target_pairs={{0,3},{1,0},{2,1},{3,2},{4,7},{5,4},{6,5},{7,6},{8,11},{9,8},{10,9... | collective-permute-start | bytes 983048 | tf_op jit(solution)/shard_map/ppermute | solution.py:289
  84.6 1.9 %collective-permute-start.11 = (bf16[160,1024]{1,0:T(8,128)(2,1)S(1)}, bf16[160,1024]{1,0:T(8,128)(2,1)S(1)}, u32[]{:S(2)}, u32[]{:S(2)}) collective-permute-start(bf16[160,1024]{1,0:T(8,128)(2,1)S(1)} %get-tuple-element.41), channel_id=1, source_target_pairs={{0,1},{1,2},{2,3},{3,0},{4,5},{5,6},{6,7},{7,4},{8,9},{9,10},{10,1... | collective-permute-start | bytes 983048 | tf_op jit(solution)/shard_map/ppermute | solution.py:289
  86.6 21.3 %all_to_all.16.tiles = f32[16,4,128]{2,1,0:T(4,128)S(1)} all-to-all(f32[16,4,128]{2,1,0:T(4,128)S(1)} %shard_map.124), channel_id=1, replica_groups=mesh['y'=8,'zh'=2,'core'=2,'zl'=4,'x'=4] {'zh','core','zl'}, dimensions={0} | all-to-all | bytes 65536 | tf_op jit(solution)/shard_map/all_to_all | solution.py:318
  107.9 1.7 %shard_map.125 = (bf16[128,4096]{1,0:T(8,128)(2,1)}, bf16[16,8192]{1,0:T(8,128)(2,1)}, f32[4,16,128]{2,1,0:T(8,128)}, f32[2,128]{1,0:T(2,128)}, f32[1,1]{1,0:T(1,128)}) custom-call(s32[2]{0:T(128)S(1)} %pad_add_fusion.place, f32[16,4,128]{2,1,0:T(4,128)S(1)} %all_to_all.16.tiles, f32[4,16,128]{2,1,0:T(8,128)S(1)} %copy-done.4, f32[2,128]{1,0:T(2,128)S(1)} %bitcast.17, ...), custom_call_target="tpu_custom_call" | custom-call | tf_op jit(solution)/shard_map/pallas_call | solution.py:403
  (28 shorter events, 0.8 us)
Async XLA Ops:
  0.6 6.7 %copy-start = (bf16[2,64,4096]{2,1,0:T(8,128)(2,1)S(1)}, bf16[2,64,4096]{2,1,0:T(8,128)(2,1)}, u32[]{:S(2)}) copy-start(bf16[2,64,4096]{2,1,0:T(8,128)(2,1)} %queries.3) | copy-start | bytes 3145732
  0.6 1.0 copy-start.3
  2.4 11.7 %all-to-all-start = ((bf16[4,16,2048]{2,1,0:T(8,128)(2,1)}), bf16[4,16,2048]{2,1,0:T(8,128)(2,1)S(1)}, u32[]{:S(2)}, u32[]{:S(2)}) async-start(bf16[4,16,2048]{2,1,0:T(8,128)(2,1)} %shard_map.119), calls=%async_computation | async-start | bytes 524288 | tf_op jit(solution)/shard_map/all_to_all | solution.py:318
  7.3 1.2 %copy-start.1 = (bf16[2,64,4096]{2,1,0:T(8,128)(2,1)S(1)}, bf16[2,64,4096]{2,1,0:T(8,128)(2,1)}, u32[]{:S(2)}) copy-start(bf16[2,64,4096]{2,1,0:T(8,128)(2,1)} %cotangent.3) | copy-start | bytes 3145732
  8.5 11.4 %copy-start.2 = (bf16[2,64,4096]{2,1,0:T(8,128)(2,1)S(1)}, bf16[2,64,4096]{2,1,0:T(8,128)(2,1)}, u32[]{:S(2)}) copy-start(bf16[2,64,4096]{2,1,0:T(8,128)(2,1)} %cotangent.3) | copy-start | bytes 3145732
  8.5 11.4 %copy-start.7 = (s32[2]{0:T(128)S(1)}, s32[2]{0:T(128)}, u32[]{:S(2)}) copy-start(s32[2]{0:T(128)} %counts.1) | copy-start | bytes 28
  9.2 10.8 %copy-start.5 = (f32[256]{0:T(256)S(1)}, f32[256]{0:T(256)}, u32[]{:S(2)}) copy-start(f32[256]{0:T(256)} %param.14) | copy-start | bytes 3076
  9.2 10.8 %copy-start.6 = (s32[1,2]{1,0:T(1,128)S(1)}, s32[1,2]{1,0:T(1,128)}, u32[]{:S(2)}) copy-start(s32[1,2]{1,0:T(1,128)} %assignment.1) | copy-start | bytes 28
  9.2 31.1 %collective-permute-start = (bf16[2,64,2048]{2,1,0:T(8,128)(2,1)S(1)}, bf16[2,64,2048]{2,1,0:T(8,128)(2,1)S(1)}, u32[]{:S(2)}, u32[]{:S(2)}) collective-permute-start(bf16[2,64,2048]{2,1,0:T(8,128)(2,1)S(1)} %shard_map.121), channel_id=1, source_target_pairs={{0,2},{1,3},{2,0},{3,1},{4,6},{5,7},{6,4},{7,5},{8,10},{9,11},{10,... | collective-permute-start | bytes 1572872 | tf_op jit(solution)/shard_map/ppermute | solution.py:289
  14.1 17.0 %collective-permute-start.5 = (bf16[4,16,2048]{2,1,0:T(8,128)(2,1)S(1)}, bf16[4,16,2048]{2,1,0:T(8,128)(2,1)S(1)}, u32[]{:S(2)}, u32[]{:S(2)}) collective-permute-start(bf16[4,16,2048]{2,1,0:T(8,128)(2,1)S(1)} %all-to-all-done.refs_0_.refs_4_), channel_id=1, source_target_pairs={{0,8},{4,12},{8,0},{12,4},{1,9},{5,13},{9,1},{13,5},{2,10},{6,14},... | collective-permute-start | bytes 786440 | tf_op jit(solution)/shard_map/ppermute | solution.py:289
  20.0 20.4 %copy-start.4 = (f32[4,16,128]{2,1,0:T(8,128)S(1)}, f32[4,16,128]{2,1,0:T(8,128)}, u32[]{:S(2)}) copy-start(f32[4,16,128]{2,1,0:T(8,128)} %lambdas.3) | copy-start | bytes 98308
  20.8 19.5 %collective-permute-start.1 = (bf16[2,64,2048]{2,1,0:T(8,128)(2,1)S(1)}, bf16[2,64,2048]{2,1,0:T(8,128)(2,1)S(1)}, u32[]{:S(2)}, u32[]{:S(2)}) collective-permute-start(bf16[2,64,2048]{2,1,0:T(8,128)(2,1)S(1)} %get-tuple-element.27), channel_id=1, source_target_pairs={{0,1},{1,2},{2,3},{3,0},{4,5},{5,6},{6,7},{7,4},{8,9},{9,10},{10,1... | collective-permute-start | bytes 1572872 | tf_op jit(solution)/shard_map/ppermute | solution.py:289
  23.0 17.3 %collective-permute-start.2 = (bf16[2,64,2048]{2,1,0:T(8,128)(2,1)S(1)}, bf16[2,64,2048]{2,1,0:T(8,128)(2,1)S(1)}, u32[]{:S(2)}, u32[]{:S(2)}) collective-permute-start(bf16[2,64,2048]{2,1,0:T(8,128)(2,1)S(1)} %get-tuple-element.28), channel_id=1, source_target_pairs={{0,3},{1,0},{2,1},{3,2},{4,7},{5,4},{6,5},{7,6},{8,11},{9,8},{10,9... | collective-permute-start | bytes 1572872 | tf_op jit(solution)/shard_map/ppermute | solution.py:289
  27.3 9.1 %collective-permute-start.4 = (bf16[4,16,2048]{2,1,0:T(8,128)(2,1)S(1)}, bf16[4,16,2048]{2,1,0:T(8,128)(2,1)S(1)}, u32[]{:S(2)}, u32[]{:S(2)}) collective-permute-start(bf16[4,16,2048]{2,1,0:T(8,128)(2,1)S(1)} %all-to-all-done.refs_0_.refs_4_), channel_id=1, source_target_pairs={{0,12},{4,8},{8,4},{12,0},{1,13},{5,9},{9,5},{13,1},{2,14},{6,10},... | collective-permute-start | bytes 786440 | tf_op jit(solution)/shard_map/ppermute | solution.py:289
  31.1 9.2 %collective-permute-start.3 = (bf16[4,16,2048]{2,1,0:T(8,128)(2,1)S(1)}, bf16[4,16,2048]{2,1,0:T(8,128)(2,1)S(1)}, u32[]{:S(2)}, u32[]{:S(2)}) collective-permute-start(bf16[4,16,2048]{2,1,0:T(8,128)(2,1)S(1)} %all-to-all-done.refs_0_.refs_4_), channel_id=1, source_target_pairs={{0,4},{4,0},{8,12},{12,8},{1,5},{5,1},{9,13},{13,9},{2,6},{6,2},{1... | collective-permute-start | bytes 786440 | tf_op jit(solution)/shard_map/ppermute | solution.py:289
  44.4 32.6 %collective-permute-start.6 = (bf16[4,16,2048]{2,1,0:T(8,128)(2,1)S(1)}, bf16[4,16,2048]{2,1,0:T(8,128)(2,1)S(1)}, u32[]{:S(2)}, u32[]{:S(2)}) collective-permute-start(bf16[4,16,2048]{2,1,0:T(8,128)(2,1)S(1)} %get-tuple-element.31), channel_id=1, source_target_pairs={{0,4},{4,0},{8,12},{12,8},{1,5},{5,1},{9,13},{13,9},{2,6},{6,2},{1... | collective-permute-start | bytes 786440 | tf_op jit(solution)/shard_map/ppermute | solution.py:289
  48.5 28.5 %collective-permute-start.7 = (bf16[4,16,2048]{2,1,0:T(8,128)(2,1)S(1)}, bf16[4,16,2048]{2,1,0:T(8,128)(2,1)S(1)}, u32[]{:S(2)}, u32[]{:S(2)}) collective-permute-start(bf16[4,16,2048]{2,1,0:T(8,128)(2,1)S(1)} %get-tuple-element.32), channel_id=1, source_target_pairs={{0,8},{4,12},{8,0},{12,4},{1,9},{5,13},{9,1},{13,5},{2,10},{6,14},... | collective-permute-start | bytes 786440 | tf_op jit(solution)/shard_map/ppermute | solution.py:289
  54.5 22.5 %collective-permute-start.8 = (bf16[4,16,2048]{2,1,0:T(8,128)(2,1)S(1)}, bf16[4,16,2048]{2,1,0:T(8,128)(2,1)S(1)}, u32[]{:S(2)}, u32[]{:S(2)}) collective-permute-start(bf16[4,16,2048]{2,1,0:T(8,128)(2,1)S(1)} %get-tuple-element.33), channel_id=1, source_target_pairs={{0,12},{4,8},{8,4},{12,0},{1,13},{5,9},{9,5},{13,1},{2,14},{6,10},... | collective-permute-start | bytes 786440 | tf_op jit(solution)/shard_map/ppermute | solution.py:289
  78.1 29.7 %collective-permute-start.9 = (bf16[160,1024]{1,0:T(8,128)(2,1)S(1)}, bf16[160,1024]{1,0:T(8,128)(2,1)S(1)}, u32[]{:S(2)}, u32[]{:S(2)}) collective-permute-start(bf16[160,1024]{1,0:T(8,128)(2,1)S(1)} %get-tuple-element.39), channel_id=1, source_target_pairs={{0,2},{1,3},{2,0},{3,1},{4,6},{5,7},{6,4},{7,5},{8,10},{9,11},{10,... | collective-permute-start | bytes 983048 | tf_op jit(solution)/shard_map/ppermute | solution.py:289
  81.0 26.8 %collective-permute-start.10 = (bf16[160,1024]{1,0:T(8,128)(2,1)S(1)}, bf16[160,1024]{1,0:T(8,128)(2,1)S(1)}, u32[]{:S(2)}, u32[]{:S(2)}) collective-permute-start(bf16[160,1024]{1,0:T(8,128)(2,1)S(1)} %get-tuple-element.40), channel_id=1, source_target_pairs={{0,3},{1,0},{2,1},{3,2},{4,7},{5,4},{6,5},{7,6},{8,11},{9,8},{10,9... | collective-permute-start | bytes 983048 | tf_op jit(solution)/shard_map/ppermute | solution.py:289
  84.6 23.2 %collective-permute-start.11 = (bf16[160,1024]{1,0:T(8,128)(2,1)S(1)}, bf16[160,1024]{1,0:T(8,128)(2,1)S(1)}, u32[]{:S(2)}, u32[]{:S(2)}) collective-permute-start(bf16[160,1024]{1,0:T(8,128)(2,1)S(1)} %get-tuple-element.41), channel_id=1, source_target_pairs={{0,1},{1,2},{2,3},{3,0},{4,5},{5,6},{6,7},{7,4},{8,9},{9,10},{10,1... | collective-permute-start | bytes 983048 | tf_op jit(solution)/shard_map/ppermute | solution.py:289

commit v8 on v6

--- a/solution.py
+++ b/solution.py
@@ -18,7 +18,6 @@
 VMEM = pl.BlockSpec(memory_space=pltpu.VMEM)
 SMEM = pl.BlockSpec(memory_space=pltpu.SMEM)
 ANY = pl.BlockSpec(memory_space=pl.ANY)
-LIMIT = pltpu.CompilerParams(vmem_limit_bytes=32 * 2**20)
 f32, bf16 = jnp.float32, jnp.bfloat16
 
 
@@ -32,20 +31,30 @@
     return lax.rem(index + PARTS, PARTS)
 
 
-def pack_vision_body(vision, out):
+def pack_vision_body(vision, out, sems):
     half = vision.shape[1] // 4
     width = half // PARTS
+    copies = []
     for g in range(PARTS):
-        out[g, :, :width] = vision[:, g * width : (g + 1) * width]
-        out[g, :, width : 2 * width] = vision[:, half + g * width : half + (g + 1) * width]
-        out[g, :, 2 * width :] = vision[
-            :, 2 * half + 2 * g * width : 2 * half + 2 * (g + 1) * width
-        ]
-
-
-def pack_text_body(place, queries, cotangent, after, *refs, shifts):
-    del after
-    outs, sems = refs[:-1], refs[-1]
+        pieces = (
+            (g * width, 0, width),
+            (half + g * width, width, width),
+            (2 * half + 2 * g * width, 2 * width, 2 * width),
+        )
+        for i, (first, to, size) in enumerate(pieces):
+            copies.append(
+                pltpu.make_async_copy(
+                    vision.at[:, pl.ds(first, size)], out.at[g, :, pl.ds(to, size)], sems.at[g, i]
+                )
+            )
+    for copy in copies:
+        copy.start()
+    for copy in copies:
+        copy.wait()
+
+
+def pack_text_body(place, queries, cotangent, *refs, shifts):
+    outs, sems = refs[-1 - len(shifts) : -1], refs[-1]
     half = queries.shape[2] // 2
     width = half // PARTS
     copies = []
@@ -291,13 +300,13 @@
     ]
 
 
-def kernel(body, out_shape, in_specs, out_specs, **more):
+def kernel(body, out_shape, in_specs, out_specs, limit=20 * 2**20, **more):
     return pl.pallas_call(
         body,
         out_shape=out_shape,
         in_specs=in_specs,
         out_specs=out_specs,
-        compiler_params=LIMIT,
+        compiler_params=pltpu.CompilerParams(vmem_limit_bytes=limit),
         **more,
     )
 
@@ -344,20 +353,26 @@
     gain_rows = norm_gain.reshape(-1, head_size)
     gate = gate_logit.reshape(1, 1)
 
-    sent_vision = kernel(pack_vision_body, slab, [VMEM], VMEM)(
-        vision.reshape(rows, vision_columns)
-    )
+    sent_vision = kernel(
+        pack_vision_body,
+        slab,
+        [ANY],
+        ANY,
+        limit=62 * 2**20,
+        scratch_shapes=[pltpu.SemaphoreType.DMA((PARTS, 3))],
+    )(vision.reshape(rows, vision_columns))
     row_vision = exchange(sent_vision, "x")
     sent_text = {}
-    for shifts, after in (((2,), place), ((0, 1, 3), row_vision)):
+    early = (row_vision, norm_gain.reshape(1, -1), assignment, frame_counts)
+    for held, others in (((2,), ()), ((0, 1, 3), early)):
         packed = kernel(
-            functools.partial(pack_text_body, shifts=shifts),
-            [shaped((seqs, toks, 2 * text_columns // PARTS))] * len(shifts),
-            [SMEM, ANY, ANY, ANY],
-            [ANY] * len(shifts),
-            scratch_shapes=[pltpu.SemaphoreType.DMA((len(shifts), 3))],
-        )(place, queries, cotangent, after)
-        sent_text.update(zip(shifts, packed))
+            functools.partial(pack_text_body, shifts=held),
+            [shaped((seqs, toks, 2 * text_columns // PARTS))] * len(held),
+            [SMEM, ANY, ANY] + [ANY, VMEM, SMEM, SMEM][: len(others)],
+            [ANY] * len(held),
+            scratch_shapes=[pltpu.SemaphoreType.DMA((len(held), 3))],
+        )(place, queries, cotangent, *others)
+        sent_text.update(zip(held, packed))
     held_text = shift_all([sent_text[k] for k in ORDER], "x", ORDER, 1)
     held_vision = shift_all([row_vision] * PARTS, "zl", LATE, 1)
 

time: 107 us -> 114 us (1.065)
  Pallas kernels: 9.03 us -> 18.2 us
  waiting for transfers between devices: 3.34 us -> 7.94 us
  starting transfers between devices: 50.4 us -> 48 us
  blocking collectives: 38.9 us -> 36.8 us
  local copies, waits for them, and re-layouts: 2.92 us -> 1.26 us
    pallas_call x3, Pallas kernels: 2.19 us -> 11.4 us  [the longest x1 9.15 us: shards(): kernel(pack_vision_body, slab, [ANY], ANY, limit=62 * 2 ** 20, scratch_sh...]
    ppermute x12, waiting for transfers between devices: 3.34 us -> 7.94 us  [shift_all(): lax.ppermute(part, axis, [(i, (i + way * k) % PARTS) for i in range(PARTS)])]
    ppermute x12, starting transfers between devices: 45.6 us -> 43.1 us  [shift_all(): lax.ppermute(part, axis, [(i, (i + way * k) % PARTS) for i in range(PARTS)])]
    all_to_all x2, blocking collectives: 38.9 us -> 36.8 us  [exchange(): return lax.all_to_all(value, axes, 0, 0, tiled=True)]
    unnamed x16 -> x14, local copies, waits for them, and re-layouts: 2.92 us -> 1.26 us
  transfers between devices with their start and end apart: 13 -> 13, of which waited for: 1 -> 2; matrix products, arithmetic and copies ran while one was open for 0% -> 0% of each run, Pallas kernels for 1% -> 2%
where the time goes in v8:
time: 114 us
  starting transfers between devices  48 us (42%)
  blocking collectives  36.8 us (32%)
  Pallas kernels  18.2 us (16%)
  waiting for transfers between devices  7.94 us (7%)
  between operations  1.52 us (1%)
  local copies, waits for them, and re-layouts  1.26 us (1%)
    ppermute x12, starting transfers between devices, shift_all(): lax.ppermute(part, axis, [(i, (i + way * k) % PARTS) for i in range(PARTS)])  43.1 us
    all_to_all x2, blocking collectives, exchange(): return lax.all_to_all(value, axes, 0, 0, tiled=True)  36.8 us
    pallas_call x1, Pallas kernels, shards(): kernel(pack_vision_body, slab, [ANY], ANY, limit=62 * 2 ** 20, scratch_sh...  9.15 us
    ppermute x12, waiting for transfers between devices, shift_all(): lax.ppermute(part, axis, [(i, (i + way * k) % PARTS) for i in range(PARTS)])  7.94 us
    all_to_all x1, starting transfers between devices, exchange(): return lax.all_to_all(value, axes, 0, 0, tiled=True)  4.85 us
    pallas_call x1, Pallas kernels, attend_call(): kernel(functools.partial(attend_body, heads=heads, head_size=head_size, p...  4.06 us
  transfers between devices with their start and end apart: 13, of which 2 were waited for; matrix products, arithmetic and copies ran while one was open for 0% of the time, Pallas kernels for 2%

profile of v8, /device:TPU:1, one launch (start us, length us, event | category | flops | bytes accessed | tf_op | source)
XLA Modules:
  0.0 113.8 jit_solution(4923023324215461012)
XLA Ops:
  0.6 9.2 %shard_map.119 = bf16[4,16,2048]{2,1,0:T(8,128)(2,1)} custom-call(bf16[16,8192]{1,0:T(8,128)(2,1)} %bitcast.17), custom_call_target="tpu_custom_call" | custom-call | tf_op jit(solution)/shard_map/pallas_call | solution.py:356
  9.8 4.9 %all-to-all-start = ((bf16[4,16,2048]{2,1,0:T(8,128)(2,1)}), bf16[4,16,2048]{2,1,0:T(8,128)(2,1)S(1)}, u32[]{:S(2)}, u32[]{:S(2)}) async-start(bf16[4,16,2048]{2,1,0:T(8,128)(2,1)} %shard_map.119), calls=%async_computation | async-start | bytes 524288 | tf_op jit(solution)/shard_map/all_to_all | solution.py:319
  14.7 1.2 %copy-done.1 = bf16[2,64,4096]{2,1,0:T(8,128)(2,1)S(1)} copy-done((bf16[2,64,4096]{2,1,0:T(8,128)(2,1)S(1)}, bf16[2,64,4096]{2,1,0:T(8,128)(2,1)}, u32[]{:S(2)}) %copy-start.1) | copy-done | bytes 1048600
  16.0 1.4 %shard_map.121 = bf16[2,64,2048]{2,1,0:T(8,128)(2,1)} custom-call(s32[2]{0:T(128)S(1)} %pad_add_fusion.place, bf16[2,64,4096]{2,1,0:T(8,128)(2,1)S(1)} %copy-done, bf16[2,64,4096]{2,1,0:T(8,128)(2,1)S(1)} %copy-done.1), custom_call_target="tpu_custom_call" | custom-call | tf_op jit(solution)/shard_map/pallas_call | solution.py:368
  17.4 4.9 %collective-permute-start = (bf16[2,64,2048]{2,1,0:T(8,128)(2,1)}, bf16[2,64,2048]{2,1,0:T(8,128)(2,1)S(1)}, u32[]{:S(2)}, u32[]{:S(2)}) collective-permute-start(bf16[2,64,2048]{2,1,0:T(8,128)(2,1)} %shard_map.121), channel_id=1, source_target_pairs={{0,2},{1,3},{2,0},{3,1},{4,6},{5,7},{6,4},{7,5},{8,10},{9,11},{10,... | collective-permute-start | bytes 1572872 | tf_op jit(solution)/shard_map/ppermute | solution.py:298
  22.3 5.8 %collective-permute-start.5 = (bf16[4,16,2048]{2,1,0:T(8,128)(2,1)S(1)}, bf16[4,16,2048]{2,1,0:T(8,128)(2,1)S(1)}, u32[]{:S(2)}, u32[]{:S(2)}) collective-permute-start(bf16[4,16,2048]{2,1,0:T(8,128)(2,1)S(1)} %all-to-all-done.refs_0_.refs_4_), channel_id=1, source_target_pairs={{0,8},{4,12},{8,0},{12,4},{1,9},{5,13},{9,1},{13,5},{2,10},{6,14},... | collective-permute-start | bytes 786440 | tf_op jit(solution)/shard_map/ppermute | solution.py:298
  28.1 0.8 shard_map.120
  29.0 2.2 %collective-permute-start.1 = (bf16[2,64,2048]{2,1,0:T(8,128)(2,1)S(1)}, bf16[2,64,2048]{2,1,0:T(8,128)(2,1)S(1)}, u32[]{:S(2)}, u32[]{:S(2)}) collective-permute-start(bf16[2,64,2048]{2,1,0:T(8,128)(2,1)S(1)} %get-tuple-element.27), channel_id=1, source_target_pairs={{0,1},{1,2},{2,3},{3,0},{4,5},{5,6},{6,7},{7,4},{8,9},{9,10},{10,1... | collective-permute-start | bytes 1572872 | tf_op jit(solution)/shard_map/ppermute | solution.py:298
  31.2 4.3 %collective-permute-start.2 = (bf16[2,64,2048]{2,1,0:T(8,128)(2,1)S(1)}, bf16[2,64,2048]{2,1,0:T(8,128)(2,1)S(1)}, u32[]{:S(2)}, u32[]{:S(2)}) collective-permute-start(bf16[2,64,2048]{2,1,0:T(8,128)(2,1)S(1)} %get-tuple-element.28), channel_id=1, source_target_pairs={{0,3},{1,0},{2,1},{3,2},{4,7},{5,4},{6,5},{7,6},{8,11},{9,8},{10,9... | collective-permute-start | bytes 1572872 | tf_op jit(solution)/shard_map/ppermute | solution.py:298
  35.5 4.0 %collective-permute-start.4 = (bf16[4,16,2048]{2,1,0:T(8,128)(2,1)S(1)}, bf16[4,16,2048]{2,1,0:T(8,128)(2,1)S(1)}, u32[]{:S(2)}, u32[]{:S(2)}) collective-permute-start(bf16[4,16,2048]{2,1,0:T(8,128)(2,1)S(1)} %all-to-all-done.refs_0_.refs_4_), channel_id=1, source_target_pairs={{0,4},{4,8},{8,12},{12,0},{1,5},{5,9},{9,13},{13,1},{2,6},{6,10},{... | collective-permute-start | bytes 786440 | tf_op jit(solution)/shard_map/ppermute | solution.py:298
  39.5 6.1 %collective-permute-start.3 = (bf16[4,16,2048]{2,1,0:T(8,128)(2,1)S(1)}, bf16[4,16,2048]{2,1,0:T(8,128)(2,1)S(1)}, u32[]{:S(2)}, u32[]{:S(2)}) collective-permute-start(bf16[4,16,2048]{2,1,0:T(8,128)(2,1)S(1)} %all-to-all-done.refs_0_.refs_4_), channel_id=1, source_target_pairs={{0,12},{4,0},{8,4},{12,8},{1,13},{5,1},{9,5},{13,9},{2,14},{6,2},{... | collective-permute-start | bytes 786440 | tf_op jit(solution)/shard_map/ppermute | solution.py:298
  46.3 6.3 %collective-permute-done.3.refs_5_ = bf16[4,16,2048]{2,1,0:T(8,128)(2,1)S(1)} collective-permute-done((bf16[4,16,2048]{2,1,0:T(8,128)(2,1)S(1)}, bf16[4,16,2048]{2,1,0:T(8,128)(2,1)S(1)}, u32[]{:S(2)}, u32[]{:S(2)}) %collective-permute-start.3) | collective-permute-done | bytes 262176 | tf_op jit(solution)/shard_map/ppermute | solution.py:298
  52.6 4.1 %shard_map.122 = (bf16[160,1024]{1,0:T(8,128)(2,1)S(1)}, bf16[160,1024]{1,0:T(8,128)(2,1)S(1)}, bf16[160,1024]{1,0:T(8,128)(2,1)S(1)}, bf16[160,1024]{1,0:T(8,12...) custom-call(s32[2]{0:T(128)S(1)} %pad_add_fusion.place, ...), custom_call_target="tpu_custom_call" | custom-call | tf_op jit(solution)/shard_map/pallas_call | solution.py:328
  56.7 4.0 %collective-permute-start.6 = (bf16[4,16,2048]{2,1,0:T(8,128)(2,1)S(1)}, bf16[4,16,2048]{2,1,0:T(8,128)(2,1)S(1)}, u32[]{:S(2)}, u32[]{:S(2)}) collective-permute-start(bf16[4,16,2048]{2,1,0:T(8,128)(2,1)S(1)} %get-tuple-element.31), channel_id=1, source_target_pairs={{0,12},{4,0},{8,4},{12,8},{1,13},{5,1},{9,5},{13,9},{2,14},{6,2},{... | collective-permute-start | bytes 786440 | tf_op jit(solution)/shard_map/ppermute | solution.py:298
  60.7 1.9 %collective-permute-start.7 = (bf16[4,16,2048]{2,1,0:T(8,128)(2,1)S(1)}, bf16[4,16,2048]{2,1,0:T(8,128)(2,1)S(1)}, u32[]{:S(2)}, u32[]{:S(2)}) collective-permute-start(bf16[4,16,2048]{2,1,0:T(8,128)(2,1)S(1)} %get-tuple-element.32), channel_id=1, source_target_pairs={{0,8},{4,12},{8,0},{12,4},{1,9},{5,13},{9,1},{13,5},{2,10},{6,14},... | collective-permute-start | bytes 786440 | tf_op jit(solution)/shard_map/ppermute | solution.py:298
  62.6 2.2 %collective-permute-start.8 = (bf16[4,16,2048]{2,1,0:T(8,128)(2,1)S(1)}, bf16[4,16,2048]{2,1,0:T(8,128)(2,1)S(1)}, u32[]{:S(2)}, u32[]{:S(2)}) collective-permute-start(bf16[4,16,2048]{2,1,0:T(8,128)(2,1)S(1)} %get-tuple-element.33), channel_id=1, source_target_pairs={{0,4},{4,8},{8,12},{12,0},{1,5},{5,9},{9,13},{13,1},{2,6},{6,10},{... | collective-permute-start | bytes 786440 | tf_op jit(solution)/shard_map/ppermute | solution.py:298
  64.8 16.5 %all_to_all.15.after.tiles = f32[32,4,128]{2,1,0:T(4,128)S(1)} all-to-all(f32[32,4,128]{2,1,0:T(4,128)S(1)} %get-tuple-element.29), channel_id=1, replica_groups=mesh['y'=8,'zh'=2,'core'=2,'zl'=4,'x'=4] {'y','x'}, dimensions={0} | all-to-all | bytes 131072 | tf_op jit(solution)/shard_map/all_to_all | solution.py:319
  81.3 1.6 %collective-permute-done.7.refs_2_ = bf16[4,16,2048]{2,1,0:T(8,128)(2,1)S(1)} collective-permute-done((bf16[4,16,2048]{2,1,0:T(8,128)(2,1)S(1)}, bf16[4,16,2048]{2,1,0:T(8,128)(2,1)S(1)}, u32[]{:S(2)}, u32[]{:S(2)}) %collective-permute-start.7) | collective-permute-done | bytes 262176 | tf_op jit(solution)/shard_map/ppermute | solution.py:298
  82.9 1.1 shard_map.123
  84.0 1.9 %collective-permute-start.9 = (bf16[160,1024]{1,0:T(8,128)(2,1)S(1)}, bf16[160,1024]{1,0:T(8,128)(2,1)S(1)}, u32[]{:S(2)}, u32[]{:S(2)}) collective-permute-start(bf16[160,1024]{1,0:T(8,128)(2,1)S(1)} %get-tuple-element.39), channel_id=1, source_target_pairs={{0,2},{1,3},{2,0},{3,1},{4,6},{5,7},{6,4},{7,5},{8,10},{9,11},{10,... | collective-permute-start | bytes 983048 | tf_op jit(solution)/shard_map/ppermute | solution.py:298
  86.0 3.9 %collective-permute-start.10 = (bf16[160,1024]{1,0:T(8,128)(2,1)S(1)}, bf16[160,1024]{1,0:T(8,128)(2,1)S(1)}, u32[]{:S(2)}, u32[]{:S(2)}) collective-permute-start(bf16[160,1024]{1,0:T(8,128)(2,1)S(1)} %get-tuple-element.40), channel_id=1, source_target_pairs={{0,3},{1,0},{2,1},{3,2},{4,7},{5,4},{6,5},{7,6},{8,11},{9,8},{10,9... | collective-permute-start | bytes 983048 | tf_op jit(solution)/shard_map/ppermute | solution.py:298
  89.8 1.9 %collective-permute-start.11 = (bf16[160,1024]{1,0:T(8,128)(2,1)S(1)}, bf16[160,1024]{1,0:T(8,128)(2,1)S(1)}, u32[]{:S(2)}, u32[]{:S(2)}) collective-permute-start(bf16[160,1024]{1,0:T(8,128)(2,1)S(1)} %get-tuple-element.41), channel_id=1, source_target_pairs={{0,1},{1,2},{2,3},{3,0},{4,5},{5,6},{6,7},{7,4},{8,9},{9,10},{10,1... | collective-permute-start | bytes 983048 | tf_op jit(solution)/shard_map/ppermute | solution.py:298
  91.8 20.3 %all_to_all.16.tiles = f32[16,4,128]{2,1,0:T(4,128)S(1)} all-to-all(f32[16,4,128]{2,1,0:T(4,128)S(1)} %shard_map.124), channel_id=1, replica_groups=mesh['y'=8,'zh'=2,'core'=2,'zl'=4,'x'=4] {'zh','core','zl'}, dimensions={0} | all-to-all | bytes 65536 | tf_op jit(solution)/shard_map/all_to_all | solution.py:319
  112.1 1.7 %shard_map.125 = (bf16[128,4096]{1,0:T(8,128)(2,1)}, bf16[16,8192]{1,0:T(8,128)(2,1)}, f32[4,16,128]{2,1,0:T(8,128)}, f32[2,128]{1,0:T(2,128)}, f32[1,1]{1,0:T(1,128)}) custom-call(s32[2]{0:T(128)S(1)} %pad_add_fusion.place, f32[16,4,128]{2,1,0:T(4,128)S(1)} %all_to_all.16.tiles, f32[4,16,128]{2,1,0:T(8,128)S(1)} %copy-done.3, f32[2,128]{1,0:T(2,128)S(1)} %bitcast.16, ...), custom_call_target="tpu_custom_call" | custom-call | tf_op jit(solution)/shard_map/pallas_call | solution.py:409
  (26 shorter events, 0.2 us)
Async XLA Ops:
  0.6 14.1 %copy-start = (bf16[2,64,4096]{2,1,0:T(8,128)(2,1)S(1)}, bf16[2,64,4096]{2,1,0:T(8,128)(2,1)}, u32[]{:S(2)}) copy-start(bf16[2,64,4096]{2,1,0:T(8,128)(2,1)} %queries.3) | copy-start | bytes 3145732
  9.8 12.4 %all-to-all-start = ((bf16[4,16,2048]{2,1,0:T(8,128)(2,1)}), bf16[4,16,2048]{2,1,0:T(8,128)(2,1)S(1)}, u32[]{:S(2)}, u32[]{:S(2)}) async-start(bf16[4,16,2048]{2,1,0:T(8,128)(2,1)} %shard_map.119), calls=%async_computation | async-start | bytes 524288 | tf_op jit(solution)/shard_map/all_to_all | solution.py:319
  14.7 1.2 %copy-start.1 = (bf16[2,64,4096]{2,1,0:T(8,128)(2,1)S(1)}, bf16[2,64,4096]{2,1,0:T(8,128)(2,1)}, u32[]{:S(2)}) copy-start(bf16[2,64,4096]{2,1,0:T(8,128)(2,1)} %cotangent.3) | copy-start | bytes 3145732
  16.0 12.1 %copy-start.2 = (bf16[2,64,4096]{2,1,0:T(8,128)(2,1)S(1)}, bf16[2,64,4096]{2,1,0:T(8,128)(2,1)}, u32[]{:S(2)}) copy-start(bf16[2,64,4096]{2,1,0:T(8,128)(2,1)} %cotangent.3) | copy-start | bytes 3145732
  16.0 12.1 %copy-start.6 = (s32[2]{0:T(128)S(1)}, s32[2]{0:T(128)}, u32[]{:S(2)}) copy-start(s32[2]{0:T(128)} %counts.1) | copy-start | bytes 28
  17.3 10.8 %copy-start.4 = (f32[256]{0:T(256)S(1)}, f32[256]{0:T(256)}, u32[]{:S(2)}) copy-start(f32[256]{0:T(256)} %param.14) | copy-start | bytes 3076
  17.3 10.8 %copy-start.5 = (s32[1,2]{1,0:T(1,128)S(1)}, s32[1,2]{1,0:T(1,128)}, u32[]{:S(2)}) copy-start(s32[1,2]{1,0:T(1,128)} %assignment.1) | copy-start | bytes 28
  17.4 35.2 %collective-permute-start = (bf16[2,64,2048]{2,1,0:T(8,128)(2,1)}, bf16[2,64,2048]{2,1,0:T(8,128)(2,1)S(1)}, u32[]{:S(2)}, u32[]{:S(2)}) collective-permute-start(bf16[2,64,2048]{2,1,0:T(8,128)(2,1)} %shard_map.121), channel_id=1, source_target_pairs={{0,2},{1,3},{2,0},{3,1},{4,6},{5,7},{6,4},{7,5},{8,10},{9,11},{10,... | collective-permute-start | bytes 1572872 | tf_op jit(solution)/shard_map/ppermute | solution.py:298
  22.3 17.2 %collective-permute-start.5 = (bf16[4,16,2048]{2,1,0:T(8,128)(2,1)S(1)}, bf16[4,16,2048]{2,1,0:T(8,128)(2,1)S(1)}, u32[]{:S(2)}, u32[]{:S(2)}) collective-permute-start(bf16[4,16,2048]{2,1,0:T(8,128)(2,1)S(1)} %all-to-all-done.refs_0_.refs_4_), channel_id=1, source_target_pairs={{0,8},{4,12},{8,0},{12,4},{1,9},{5,13},{9,1},{13,5},{2,10},{6,14},... | collective-permute-start | bytes 786440 | tf_op jit(solution)/shard_map/ppermute | solution.py:298
  28.1 24.5 %copy-start.3 = (f32[4,16,128]{2,1,0:T(8,128)S(1)}, f32[4,16,128]{2,1,0:T(8,128)}, u32[]{:S(2)}) copy-start(f32[4,16,128]{2,1,0:T(8,128)} %lambdas.3) | copy-start | bytes 98308
  29.0 23.6 %collective-permute-start.1 = (bf16[2,64,2048]{2,1,0:T(8,128)(2,1)S(1)}, bf16[2,64,2048]{2,1,0:T(8,128)(2,1)S(1)}, u32[]{:S(2)}, u32[]{:S(2)}) collective-permute-start(bf16[2,64,2048]{2,1,0:T(8,128)(2,1)S(1)} %get-tuple-element.27), channel_id=1, source_target_pairs={{0,1},{1,2},{2,3},{3,0},{4,5},{5,6},{6,7},{7,4},{8,9},{9,10},{10,1... | collective-permute-start | bytes 1572872 | tf_op jit(solution)/shard_map/ppermute | solution.py:298
  31.2 21.4 %collective-permute-start.2 = (bf16[2,64,2048]{2,1,0:T(8,128)(2,1)S(1)}, bf16[2,64,2048]{2,1,0:T(8,128)(2,1)S(1)}, u32[]{:S(2)}, u32[]{:S(2)}) collective-permute-start(bf16[2,64,2048]{2,1,0:T(8,128)(2,1)S(1)} %get-tuple-element.28), channel_id=1, source_target_pairs={{0,3},{1,0},{2,1},{3,2},{4,7},{5,4},{6,5},{7,6},{8,11},{9,8},{10,9... | collective-permute-start | bytes 1572872 | tf_op jit(solution)/shard_map/ppermute | solution.py:298
  35.5 10.8 %collective-permute-start.4 = (bf16[4,16,2048]{2,1,0:T(8,128)(2,1)S(1)}, bf16[4,16,2048]{2,1,0:T(8,128)(2,1)S(1)}, u32[]{:S(2)}, u32[]{:S(2)}) collective-permute-start(bf16[4,16,2048]{2,1,0:T(8,128)(2,1)S(1)} %all-to-all-done.refs_0_.refs_4_), channel_id=1, source_target_pairs={{0,4},{4,8},{8,12},{12,0},{1,5},{5,9},{9,13},{13,1},{2,6},{6,10},{... | collective-permute-start | bytes 786440 | tf_op jit(solution)/shard_map/ppermute | solution.py:298
  39.5 13.1 %collective-permute-start.3 = (bf16[4,16,2048]{2,1,0:T(8,128)(2,1)S(1)}, bf16[4,16,2048]{2,1,0:T(8,128)(2,1)S(1)}, u32[]{:S(2)}, u32[]{:S(2)}) collective-permute-start(bf16[4,16,2048]{2,1,0:T(8,128)(2,1)S(1)} %all-to-all-done.refs_0_.refs_4_), channel_id=1, source_target_pairs={{0,12},{4,0},{8,4},{12,8},{1,13},{5,1},{9,5},{13,9},{2,14},{6,2},{... | collective-permute-start | bytes 786440 | tf_op jit(solution)/shard_map/ppermute | solution.py:298
  56.7 24.6 %collective-permute-start.6 = (bf16[4,16,2048]{2,1,0:T(8,128)(2,1)S(1)}, bf16[4,16,2048]{2,1,0:T(8,128)(2,1)S(1)}, u32[]{:S(2)}, u32[]{:S(2)}) collective-permute-start(bf16[4,16,2048]{2,1,0:T(8,128)(2,1)S(1)} %get-tuple-element.31), channel_id=1, source_target_pairs={{0,12},{4,0},{8,4},{12,8},{1,13},{5,1},{9,5},{13,9},{2,14},{6,2},{... | collective-permute-start | bytes 786440 | tf_op jit(solution)/shard_map/ppermute | solution.py:298
  60.7 22.2 %collective-permute-start.7 = (bf16[4,16,2048]{2,1,0:T(8,128)(2,1)S(1)}, bf16[4,16,2048]{2,1,0:T(8,128)(2,1)S(1)}, u32[]{:S(2)}, u32[]{:S(2)}) collective-permute-start(bf16[4,16,2048]{2,1,0:T(8,128)(2,1)S(1)} %get-tuple-element.32), channel_id=1, source_target_pairs={{0,8},{4,12},{8,0},{12,4},{1,9},{5,13},{9,1},{13,5},{2,10},{6,14},... | collective-permute-start | bytes 786440 | tf_op jit(solution)/shard_map/ppermute | solution.py:298
  62.6 20.3 %collective-permute-start.8 = (bf16[4,16,2048]{2,1,0:T(8,128)(2,1)S(1)}, bf16[4,16,2048]{2,1,0:T(8,128)(2,1)S(1)}, u32[]{:S(2)}, u32[]{:S(2)}) collective-permute-start(bf16[4,16,2048]{2,1,0:T(8,128)(2,1)S(1)} %get-tuple-element.33), channel_id=1, source_target_pairs={{0,4},{4,8},{8,12},{12,0},{1,5},{5,9},{9,13},{13,1},{2,6},{6,10},{... | collective-permute-start | bytes 786440 | tf_op jit(solution)/shard_map/ppermute | solution.py:298
  84.0 28.1 %collective-permute-start.9 = (bf16[160,1024]{1,0:T(8,128)(2,1)S(1)}, bf16[160,1024]{1,0:T(8,128)(2,1)S(1)}, u32[]{:S(2)}, u32[]{:S(2)}) collective-permute-start(bf16[160,1024]{1,0:T(8,128)(2,1)S(1)} %get-tuple-element.39), channel_id=1, source_target_pairs={{0,2},{1,3},{2,0},{3,1},{4,6},{5,7},{6,4},{7,5},{8,10},{9,11},{10,... | collective-permute-start | bytes 983048 | tf_op jit(solution)/shard_map/ppermute | solution.py:298
  86.0 26.1 %collective-permute-start.10 = (bf16[160,1024]{1,0:T(8,128)(2,1)S(1)}, bf16[160,1024]{1,0:T(8,128)(2,1)S(1)}, u32[]{:S(2)}, u32[]{:S(2)}) collective-permute-start(bf16[160,1024]{1,0:T(8,128)(2,1)S(1)} %get-tuple-element.40), channel_id=1, source_target_pairs={{0,3},{1,0},{2,1},{3,2},{4,7},{5,4},{6,5},{7,6},{8,11},{9,8},{10,9... | collective-permute-start | bytes 983048 | tf_op jit(solution)/shard_map/ppermute | solution.py:298
  89.8 22.3 %collective-permute-start.11 = (bf16[160,1024]{1,0:T(8,128)(2,1)S(1)}, bf16[160,1024]{1,0:T(8,128)(2,1)S(1)}, u32[]{:S(2)}, u32[]{:S(2)}) collective-permute-start(bf16[160,1024]{1,0:T(8,128)(2,1)S(1)} %get-tuple-element.41), channel_id=1, source_target_pairs={{0,1},{1,2},{2,3},{3,0},{4,5},{5,6},{6,7},{7,4},{8,9},{9,10},{10,1... | collective-permute-start | bytes 983048 | tf_op jit(solution)/shard_map/ppermute | solution.py:298

commit v9 on v6

--- a/solution.py
+++ b/solution.py
@@ -43,9 +43,8 @@
         ]
 
 
-def pack_text_body(place, queries, cotangent, after, *refs, shifts):
-    del after
-    outs, sems = refs[:-1], refs[-1]
+def pack_text_body(place, queries, cotangent, *refs, shifts):
+    outs, sems = refs[-1 - len(shifts) : -1], refs[-1]
     half = queries.shape[2] // 2
     width = half // PARTS
     copies = []
@@ -349,15 +348,16 @@
     )
     row_vision = exchange(sent_vision, "x")
     sent_text = {}
-    for shifts, after in (((2,), place), ((0, 1, 3), row_vision)):
+    early = (row_vision, norm_gain.reshape(1, -1), assignment, frame_counts)
+    for held, others in (((2,), ()), ((0, 1, 3), early)):
         packed = kernel(
-            functools.partial(pack_text_body, shifts=shifts),
-            [shaped((seqs, toks, 2 * text_columns // PARTS))] * len(shifts),
-            [SMEM, ANY, ANY, ANY],
-            [ANY] * len(shifts),
-            scratch_shapes=[pltpu.SemaphoreType.DMA((len(shifts), 3))],
-        )(place, queries, cotangent, after)
-        sent_text.update(zip(shifts, packed))
+            functools.partial(pack_text_body, shifts=held),
+            [shaped((seqs, toks, 2 * text_columns // PARTS))] * len(held),
+            [SMEM, ANY, ANY] + [ANY, VMEM, SMEM, SMEM][: len(others)],
+            [ANY] * len(held),
+            scratch_shapes=[pltpu.SemaphoreType.DMA((len(held), 3))],
+        )(place, queries, cotangent, *others)
+        sent_text.update(zip(held, packed))
     held_text = shift_all([sent_text[k] for k in ORDER], "x", ORDER, 1)
     held_vision = shift_all([row_vision] * PARTS, "zl", LATE, 1)
 

time: 107 us -> 106 us (level)
  no operation moved by 1% of the time
where the time goes in v9:
time: 106 us
  starting transfers between devices  51 us (48%)
  blocking collectives  38.5 us (36%)
  Pallas kernels  9.06 us (9%)
  waiting for transfers between devices  3.17 us (3%)
  local copies, waits for them, and re-layouts  2.29 us (2%)
  between operations  1.53 us (1%)
    ppermute x12, starting transfers between devices, shift_all(): lax.ppermute(part, axis, [(i, (i + way * k) % PARTS) for i in range(PARTS)])  46.1 us
    all_to_all x2, blocking collectives, exchange(): return lax.all_to_all(value, axes, 0, 0, tiled=True)  38.5 us
    all_to_all x1, starting transfers between devices, exchange(): return lax.all_to_all(value, axes, 0, 0, tiled=True)  4.84 us
    pallas_call x1, Pallas kernels, attend_call(): kernel(functools.partial(attend_body, heads=heads, head_size=head_size, p...  4.06 us
    ppermute x12, waiting for transfers between devices, shift_all(): lax.ppermute(part, axis, [(i, (i + way * k) % PARTS) for i in range(PARTS)])  3.17 us
    unnamed x16, local copies, waits for them, and re-layouts  2.29 us
  transfers between devices with their start and end apart: 13, of which 1 were waited for; matrix products, arithmetic and copies ran while one was open for 0% of the time, Pallas kernels for 1%

profile of v9, /device:TPU:1, one launch (start us, length us, event | category | flops | bytes accessed | tf_op | source)
XLA Modules:
  0.0 105.6 jit_solution(17524238053483409379)
XLA Ops:
  0.7 1.0 copy-done.3
  1.7 0.7 shard_map.119
  2.4 4.8 %all-to-all-start = ((bf16[4,16,2048]{2,1,0:T(8,128)(2,1)}), bf16[4,16,2048]{2,1,0:T(8,128)(2,1)S(1)}, u32[]{:S(2)}, u32[]{:S(2)}) async-start(bf16[4,16,2048]{2,1,0:T(8,128)(2,1)} %shard_map.119), calls=%async_computation | async-start | bytes 524288 | tf_op jit(solution)/shard_map/all_to_all | solution.py:309
  7.3 1.2 %copy-done.1 = bf16[2,64,4096]{2,1,0:T(8,128)(2,1)S(1)} copy-done((bf16[2,64,4096]{2,1,0:T(8,128)(2,1)S(1)}, bf16[2,64,4096]{2,1,0:T(8,128)(2,1)}, u32[]{:S(2)}) %copy-start.1) | copy-done | bytes 1048600
  8.6 0.6 shard_map.121
  9.2 4.9 %collective-permute-start = (bf16[2,64,2048]{2,1,0:T(8,128)(2,1)S(1)}, bf16[2,64,2048]{2,1,0:T(8,128)(2,1)S(1)}, u32[]{:S(2)}, u32[]{:S(2)}) collective-permute-start(bf16[2,64,2048]{2,1,0:T(8,128)(2,1)S(1)} %shard_map.121), channel_id=1, source_target_pairs={{0,2},{1,3},{2,0},{3,1},{4,6},{5,7},{6,4},{7,5},{8,10},{9,11},{10,... | collective-permute-start | bytes 1572872 | tf_op jit(solution)/shard_map/ppermute | solution.py:288
  14.1 5.8 %collective-permute-start.5 = (bf16[4,16,2048]{2,1,0:T(8,128)(2,1)S(1)}, bf16[4,16,2048]{2,1,0:T(8,128)(2,1)S(1)}, u32[]{:S(2)}, u32[]{:S(2)}) collective-permute-start(bf16[4,16,2048]{2,1,0:T(8,128)(2,1)S(1)} %all-to-all-done.refs_0_.refs_4_), channel_id=1, source_target_pairs={{0,8},{4,12},{8,0},{12,4},{1,9},{5,13},{9,1},{13,5},{2,10},{6,14},... | collective-permute-start | bytes 786440 | tf_op jit(solution)/shard_map/ppermute | solution.py:288
  20.0 0.8 shard_map.120
  20.8 2.2 %collective-permute-start.1 = (bf16[2,64,2048]{2,1,0:T(8,128)(2,1)S(1)}, bf16[2,64,2048]{2,1,0:T(8,128)(2,1)S(1)}, u32[]{:S(2)}, u32[]{:S(2)}) collective-permute-start(bf16[2,64,2048]{2,1,0:T(8,128)(2,1)S(1)} %get-tuple-element.27), channel_id=1, source_target_pairs={{0,1},{1,2},{2,3},{3,0},{4,5},{5,6},{6,7},{7,4},{8,9},{9,10},{10,1... | collective-permute-start | bytes 1572872 | tf_op jit(solution)/shard_map/ppermute | solution.py:288
  23.0 4.3 %collective-permute-start.2 = (bf16[2,64,2048]{2,1,0:T(8,128)(2,1)S(1)}, bf16[2,64,2048]{2,1,0:T(8,128)(2,1)S(1)}, u32[]{:S(2)}, u32[]{:S(2)}) collective-permute-start(bf16[2,64,2048]{2,1,0:T(8,128)(2,1)S(1)} %get-tuple-element.28), channel_id=1, source_target_pairs={{0,3},{1,0},{2,1},{3,2},{4,7},{5,4},{6,5},{7,6},{8,11},{9,8},{10,9... | collective-permute-start | bytes 1572872 | tf_op jit(solution)/shard_map/ppermute | solution.py:288
  27.3 4.0 %collective-permute-start.4 = (bf16[4,16,2048]{2,1,0:T(8,128)(2,1)S(1)}, bf16[4,16,2048]{2,1,0:T(8,128)(2,1)S(1)}, u32[]{:S(2)}, u32[]{:S(2)}) collective-permute-start(bf16[4,16,2048]{2,1,0:T(8,128)(2,1)S(1)} %all-to-all-done.refs_0_.refs_4_), channel_id=1, source_target_pairs={{0,4},{4,8},{8,12},{12,0},{1,5},{5,9},{9,13},{13,1},{2,6},{6,10},{... | collective-permute-start | bytes 786440 | tf_op jit(solution)/shard_map/ppermute | solution.py:288
  31.4 6.1 %collective-permute-start.3 = (bf16[4,16,2048]{2,1,0:T(8,128)(2,1)S(1)}, bf16[4,16,2048]{2,1,0:T(8,128)(2,1)S(1)}, u32[]{:S(2)}, u32[]{:S(2)}) collective-permute-start(bf16[4,16,2048]{2,1,0:T(8,128)(2,1)S(1)} %all-to-all-done.refs_0_.refs_4_), channel_id=1, source_target_pairs={{0,12},{4,0},{8,4},{12,8},{1,13},{5,1},{9,5},{13,9},{2,14},{6,2},{... | collective-permute-start | bytes 786440 | tf_op jit(solution)/shard_map/ppermute | solution.py:288
  38.2 3.1 %collective-permute-done.3.refs_5_ = bf16[4,16,2048]{2,1,0:T(8,128)(2,1)S(1)} collective-permute-done((bf16[4,16,2048]{2,1,0:T(8,128)(2,1)S(1)}, bf16[4,16,2048]{2,1,0:T(8,128)(2,1)S(1)}, u32[]{:S(2)}, u32[]{:S(2)}) %collective-permute-start.3) | collective-permute-done | bytes 262176 | tf_op jit(solution)/shard_map/ppermute | solution.py:288
  41.3 4.1 %shard_map.122 = (bf16[160,1024]{1,0:T(8,128)(2,1)S(1)}, bf16[160,1024]{1,0:T(8,128)(2,1)S(1)}, bf16[160,1024]{1,0:T(8,128)(2,1)S(1)}, bf16[160,1024]{1,0:T(8,12...) custom-call(s32[2]{0:T(128)S(1)} %pad_add_fusion.place, ...), custom_call_target="tpu_custom_call" | custom-call | tf_op jit(solution)/shard_map/pallas_call | solution.py:318
  45.4 5.7 %collective-permute-start.6 = (bf16[4,16,2048]{2,1,0:T(8,128)(2,1)S(1)}, bf16[4,16,2048]{2,1,0:T(8,128)(2,1)S(1)}, u32[]{:S(2)}, u32[]{:S(2)}) collective-permute-start(bf16[4,16,2048]{2,1,0:T(8,128)(2,1)S(1)} %get-tuple-element.31), channel_id=1, source_target_pairs={{0,12},{4,0},{8,4},{12,8},{1,13},{5,1},{9,5},{13,9},{2,14},{6,2},{... | collective-permute-start | bytes 786440 | tf_op jit(solution)/shard_map/ppermute | solution.py:288
  51.1 1.9 %collective-permute-start.7 = (bf16[4,16,2048]{2,1,0:T(8,128)(2,1)S(1)}, bf16[4,16,2048]{2,1,0:T(8,128)(2,1)S(1)}, u32[]{:S(2)}, u32[]{:S(2)}) collective-permute-start(bf16[4,16,2048]{2,1,0:T(8,128)(2,1)S(1)} %get-tuple-element.32), channel_id=1, source_target_pairs={{0,8},{4,12},{8,0},{12,4},{1,9},{5,13},{9,1},{13,5},{2,10},{6,14},... | collective-permute-start | bytes 786440 | tf_op jit(solution)/shard_map/ppermute | solution.py:288
  53.0 2.2 %collective-permute-start.8 = (bf16[4,16,2048]{2,1,0:T(8,128)(2,1)S(1)}, bf16[4,16,2048]{2,1,0:T(8,128)(2,1)S(1)}, u32[]{:S(2)}, u32[]{:S(2)}) collective-permute-start(bf16[4,16,2048]{2,1,0:T(8,128)(2,1)S(1)} %get-tuple-element.33), channel_id=1, source_target_pairs={{0,4},{4,8},{8,12},{12,0},{1,5},{5,9},{9,13},{13,1},{2,6},{6,10},{... | collective-permute-start | bytes 786440 | tf_op jit(solution)/shard_map/ppermute | solution.py:288
  55.2 17.9 %all_to_all.15.after.tiles = f32[32,4,128]{2,1,0:T(4,128)S(1)} all-to-all(f32[32,4,128]{2,1,0:T(4,128)S(1)} %get-tuple-element.29), channel_id=1, replica_groups=mesh['y'=8,'zh'=2,'core'=2,'zl'=4,'x'=4] {'y','x'}, dimensions={0} | all-to-all | bytes 131072 | tf_op jit(solution)/shard_map/all_to_all | solution.py:309
  73.2 1.1 %shard_map.123 = (bf16[160,1024]{1,0:T(8,128)(2,1)S(1)}, bf16[160,1024]{1,0:T(8,128)(2,1)S(1)}, bf16[160,1024]{1,0:T(8,128)(2,1)S(1)}, bf16[160,1024]{1,0:T(8,128)(2,1)S(1)}) custom-call(s32[2]{0:T(128)S(1)} %pad_add_fusion.place, f32[32,4,128]{2,1,0:T(4,128)S(1)} %all_to_all.15.after.tiles, ...), custom_call_target="tpu_custom_call", output_to_operand_aliasing={{0}: (6, {}), {1}: (7, {}), {2}: (8, {}), {3}: (9, {})} | custom-call | tf_op jit(solution)/shard_map/pallas_call | solution.py:378
  74.3 2.9 %collective-permute-start.9 = (bf16[160,1024]{1,0:T(8,128)(2,1)S(1)}, bf16[160,1024]{1,0:T(8,128)(2,1)S(1)}, u32[]{:S(2)}, u32[]{:S(2)}) collective-permute-start(bf16[160,1024]{1,0:T(8,128)(2,1)S(1)} %get-tuple-element.39), channel_id=1, source_target_pairs={{0,2},{1,3},{2,0},{3,1},{4,6},{5,7},{6,4},{7,5},{8,10},{9,11},{10,... | collective-permute-start | bytes 983048 | tf_op jit(solution)/shard_map/ppermute | solution.py:288
  77.2 4.2 %collective-permute-start.10 = (bf16[160,1024]{1,0:T(8,128)(2,1)S(1)}, bf16[160,1024]{1,0:T(8,128)(2,1)S(1)}, u32[]{:S(2)}, u32[]{:S(2)}) collective-permute-start(bf16[160,1024]{1,0:T(8,128)(2,1)S(1)} %get-tuple-element.40), channel_id=1, source_target_pairs={{0,3},{1,0},{2,1},{3,2},{4,7},{5,4},{6,5},{7,6},{8,11},{9,8},{10,9... | collective-permute-start | bytes 983048 | tf_op jit(solution)/shard_map/ppermute | solution.py:288
  81.4 1.9 %collective-permute-start.11 = (bf16[160,1024]{1,0:T(8,128)(2,1)S(1)}, bf16[160,1024]{1,0:T(8,128)(2,1)S(1)}, u32[]{:S(2)}, u32[]{:S(2)}) collective-permute-start(bf16[160,1024]{1,0:T(8,128)(2,1)S(1)} %get-tuple-element.41), channel_id=1, source_target_pairs={{0,1},{1,2},{2,3},{3,0},{4,5},{5,6},{6,7},{7,4},{8,9},{9,10},{10,1... | collective-permute-start | bytes 983048 | tf_op jit(solution)/shard_map/ppermute | solution.py:288
  83.3 20.6 %all_to_all.16.tiles = f32[16,4,128]{2,1,0:T(4,128)S(1)} all-to-all(f32[16,4,128]{2,1,0:T(4,128)S(1)} %shard_map.124), channel_id=1, replica_groups=mesh['y'=8,'zh'=2,'core'=2,'zl'=4,'x'=4] {'zh','core','zl'}, dimensions={0} | all-to-all | bytes 65536 | tf_op jit(solution)/shard_map/all_to_all | solution.py:309
  104.0 1.7 %shard_map.125 = (bf16[128,4096]{1,0:T(8,128)(2,1)}, bf16[16,8192]{1,0:T(8,128)(2,1)}, f32[4,16,128]{2,1,0:T(8,128)}, f32[2,128]{1,0:T(2,128)}, f32[1,1]{1,0:T(1,128)}) custom-call(s32[2]{0:T(128)S(1)} %pad_add_fusion.place, f32[16,4,128]{2,1,0:T(4,128)S(1)} %all_to_all.16.tiles, f32[4,16,128]{2,1,0:T(8,128)S(1)} %copy-done.4, f32[2,128]{1,0:T(2,128)S(1)} %bitcast.17, ...), custom_call_target="tpu_custom_call" | custom-call | tf_op jit(solution)/shard_map/pallas_call | solution.py:394
  (28 shorter events, 0.2 us)
Async XLA Ops:
  0.6 6.7 %copy-start = (bf16[2,64,4096]{2,1,0:T(8,128)(2,1)S(1)}, bf16[2,64,4096]{2,1,0:T(8,128)(2,1)}, u32[]{:S(2)}) copy-start(bf16[2,64,4096]{2,1,0:T(8,128)(2,1)} %queries.3) | copy-start | bytes 3145732
  0.6 1.0 copy-start.3
  2.4 11.7 %all-to-all-start = ((bf16[4,16,2048]{2,1,0:T(8,128)(2,1)}), bf16[4,16,2048]{2,1,0:T(8,128)(2,1)S(1)}, u32[]{:S(2)}, u32[]{:S(2)}) async-start(bf16[4,16,2048]{2,1,0:T(8,128)(2,1)} %shard_map.119), calls=%async_computation | async-start | bytes 524288 | tf_op jit(solution)/shard_map/all_to_all | solution.py:309
  7.3 1.2 %copy-start.1 = (bf16[2,64,4096]{2,1,0:T(8,128)(2,1)S(1)}, bf16[2,64,4096]{2,1,0:T(8,128)(2,1)}, u32[]{:S(2)}) copy-start(bf16[2,64,4096]{2,1,0:T(8,128)(2,1)} %cotangent.3) | copy-start | bytes 3145732
  8.5 11.4 %copy-start.2 = (bf16[2,64,4096]{2,1,0:T(8,128)(2,1)S(1)}, bf16[2,64,4096]{2,1,0:T(8,128)(2,1)}, u32[]{:S(2)}) copy-start(bf16[2,64,4096]{2,1,0:T(8,128)(2,1)} %cotangent.3) | copy-start | bytes 3145732
  8.5 11.4 %copy-start.7 = (s32[2]{0:T(128)S(1)}, s32[2]{0:T(128)}, u32[]{:S(2)}) copy-start(s32[2]{0:T(128)} %counts.1) | copy-start | bytes 28
  9.2 10.8 %copy-start.5 = (f32[256]{0:T(256)S(1)}, f32[256]{0:T(256)}, u32[]{:S(2)}) copy-start(f32[256]{0:T(256)} %param.14) | copy-start | bytes 3076
  9.2 10.8 %copy-start.6 = (s32[1,2]{1,0:T(1,128)S(1)}, s32[1,2]{1,0:T(1,128)}, u32[]{:S(2)}) copy-start(s32[1,2]{1,0:T(1,128)} %assignment.1) | copy-start | bytes 28
  9.2 32.1 %collective-permute-start = (bf16[2,64,2048]{2,1,0:T(8,128)(2,1)S(1)}, bf16[2,64,2048]{2,1,0:T(8,128)(2,1)S(1)}, u32[]{:S(2)}, u32[]{:S(2)}) collective-permute-start(bf16[2,64,2048]{2,1,0:T(8,128)(2,1)S(1)} %shard_map.121), channel_id=1, source_target_pairs={{0,2},{1,3},{2,0},{3,1},{4,6},{5,7},{6,4},{7,5},{8,10},{9,11},{10,... | collective-permute-start | bytes 1572872 | tf_op jit(solution)/shard_map/ppermute | solution.py:288
  14.1 17.2 %collective-permute-start.5 = (bf16[4,16,2048]{2,1,0:T(8,128)(2,1)S(1)}, bf16[4,16,2048]{2,1,0:T(8,128)(2,1)S(1)}, u32[]{:S(2)}, u32[]{:S(2)}) collective-permute-start(bf16[4,16,2048]{2,1,0:T(8,128)(2,1)S(1)} %all-to-all-done.refs_0_.refs_4_), channel_id=1, source_target_pairs={{0,8},{4,12},{8,0},{12,4},{1,9},{5,13},{9,1},{13,5},{2,10},{6,14},... | collective-permute-start | bytes 786440 | tf_op jit(solution)/shard_map/ppermute | solution.py:288
  20.0 21.3 %copy-start.4 = (f32[4,16,128]{2,1,0:T(8,128)S(1)}, f32[4,16,128]{2,1,0:T(8,128)}, u32[]{:S(2)}) copy-start(f32[4,16,128]{2,1,0:T(8,128)} %lambdas.3) | copy-start | bytes 98308
  20.8 20.5 %collective-permute-start.1 = (bf16[2,64,2048]{2,1,0:T(8,128)(2,1)S(1)}, bf16[2,64,2048]{2,1,0:T(8,128)(2,1)S(1)}, u32[]{:S(2)}, u32[]{:S(2)}) collective-permute-start(bf16[2,64,2048]{2,1,0:T(8,128)(2,1)S(1)} %get-tuple-element.27), channel_id=1, source_target_pairs={{0,1},{1,2},{2,3},{3,0},{4,5},{5,6},{6,7},{7,4},{8,9},{9,10},{10,1... | collective-permute-start | bytes 1572872 | tf_op jit(solution)/shard_map/ppermute | solution.py:288
  23.0 18.3 %collective-permute-start.2 = (bf16[2,64,2048]{2,1,0:T(8,128)(2,1)S(1)}, bf16[2,64,2048]{2,1,0:T(8,128)(2,1)S(1)}, u32[]{:S(2)}, u32[]{:S(2)}) collective-permute-start(bf16[2,64,2048]{2,1,0:T(8,128)(2,1)S(1)} %get-tuple-element.28), channel_id=1, source_target_pairs={{0,3},{1,0},{2,1},{3,2},{4,7},{5,4},{6,5},{7,6},{8,11},{9,8},{10,9... | collective-permute-start | bytes 1572872 | tf_op jit(solution)/shard_map/ppermute | solution.py:288
  27.3 10.8 %collective-permute-start.4 = (bf16[4,16,2048]{2,1,0:T(8,128)(2,1)S(1)}, bf16[4,16,2048]{2,1,0:T(8,128)(2,1)S(1)}, u32[]{:S(2)}, u32[]{:S(2)}) collective-permute-start(bf16[4,16,2048]{2,1,0:T(8,128)(2,1)S(1)} %all-to-all-done.refs_0_.refs_4_), channel_id=1, source_target_pairs={{0,4},{4,8},{8,12},{12,0},{1,5},{5,9},{9,13},{13,1},{2,6},{6,10},{... | collective-permute-start | bytes 786440 | tf_op jit(solution)/shard_map/ppermute | solution.py:288
  31.4 9.9 %collective-permute-start.3 = (bf16[4,16,2048]{2,1,0:T(8,128)(2,1)S(1)}, bf16[4,16,2048]{2,1,0:T(8,128)(2,1)S(1)}, u32[]{:S(2)}, u32[]{:S(2)}) collective-permute-start(bf16[4,16,2048]{2,1,0:T(8,128)(2,1)S(1)} %all-to-all-done.refs_0_.refs_4_), channel_id=1, source_target_pairs={{0,12},{4,0},{8,4},{12,8},{1,13},{5,1},{9,5},{13,9},{2,14},{6,2},{... | collective-permute-start | bytes 786440 | tf_op jit(solution)/shard_map/ppermute | solution.py:288
  45.4 27.8 %collective-permute-start.6 = (bf16[4,16,2048]{2,1,0:T(8,128)(2,1)S(1)}, bf16[4,16,2048]{2,1,0:T(8,128)(2,1)S(1)}, u32[]{:S(2)}, u32[]{:S(2)}) collective-permute-start(bf16[4,16,2048]{2,1,0:T(8,128)(2,1)S(1)} %get-tuple-element.31), channel_id=1, source_target_pairs={{0,12},{4,0},{8,4},{12,8},{1,13},{5,1},{9,5},{13,9},{2,14},{6,2},{... | collective-permute-start | bytes 786440 | tf_op jit(solution)/shard_map/ppermute | solution.py:288
  51.1 22.1 %collective-permute-start.7 = (bf16[4,16,2048]{2,1,0:T(8,128)(2,1)S(1)}, bf16[4,16,2048]{2,1,0:T(8,128)(2,1)S(1)}, u32[]{:S(2)}, u32[]{:S(2)}) collective-permute-start(bf16[4,16,2048]{2,1,0:T(8,128)(2,1)S(1)} %get-tuple-element.32), channel_id=1, source_target_pairs={{0,8},{4,12},{8,0},{12,4},{1,9},{5,13},{9,1},{13,5},{2,10},{6,14},... | collective-permute-start | bytes 786440 | tf_op jit(solution)/shard_map/ppermute | solution.py:288
  53.0 20.1 %collective-permute-start.8 = (bf16[4,16,2048]{2,1,0:T(8,128)(2,1)S(1)}, bf16[4,16,2048]{2,1,0:T(8,128)(2,1)S(1)}, u32[]{:S(2)}, u32[]{:S(2)}) collective-permute-start(bf16[4,16,2048]{2,1,0:T(8,128)(2,1)S(1)} %get-tuple-element.33), channel_id=1, source_target_pairs={{0,4},{4,8},{8,12},{12,0},{1,5},{5,9},{9,13},{13,1},{2,6},{6,10},{... | collective-permute-start | bytes 786440 | tf_op jit(solution)/shard_map/ppermute | solution.py:288
  74.3 29.7 %collective-permute-start.9 = (bf16[160,1024]{1,0:T(8,128)(2,1)S(1)}, bf16[160,1024]{1,0:T(8,128)(2,1)S(1)}, u32[]{:S(2)}, u32[]{:S(2)}) collective-permute-start(bf16[160,1024]{1,0:T(8,128)(2,1)S(1)} %get-tuple-element.39), channel_id=1, source_target_pairs={{0,2},{1,3},{2,0},{3,1},{4,6},{5,7},{6,4},{7,5},{8,10},{9,11},{10,... | collective-permute-start | bytes 983048 | tf_op jit(solution)/shard_map/ppermute | solution.py:288
  77.2 26.8 %collective-permute-start.10 = (bf16[160,1024]{1,0:T(8,128)(2,1)S(1)}, bf16[160,1024]{1,0:T(8,128)(2,1)S(1)}, u32[]{:S(2)}, u32[]{:S(2)}) collective-permute-start(bf16[160,1024]{1,0:T(8,128)(2,1)S(1)} %get-tuple-element.40), channel_id=1, source_target_pairs={{0,3},{1,0},{2,1},{3,2},{4,7},{5,4},{6,5},{7,6},{8,11},{9,8},{10,9... | collective-permute-start | bytes 983048 | tf_op jit(solution)/shard_map/ppermute | solution.py:288
  81.4 22.6 %collective-permute-start.11 = (bf16[160,1024]{1,0:T(8,128)(2,1)S(1)}, bf16[160,1024]{1,0:T(8,128)(2,1)S(1)}, u32[]{:S(2)}, u32[]{:S(2)}) collective-permute-start(bf16[160,1024]{1,0:T(8,128)(2,1)S(1)} %get-tuple-element.41), channel_id=1, source_target_pairs={{0,1},{1,2},{2,3},{3,0},{4,5},{5,6},{6,7},{7,4},{8,9},{9,10},{10,1... | collective-permute-start | bytes 983048 | tf_op jit(solution)/shard_map/ppermute | solution.py:288

commit v10 on v9

--- a/solution.py
+++ b/solution.py
@@ -14,7 +14,7 @@
 FIRST, SECOND = 32, 16
 PARTS = 4
 GROUP = 2
-ORDER, LATE = (0, 2, 1, 3), (0, 3, 1, 2)
+ORDER, LATE, BACK = (0, 2, 1, 3), (0, 3, 1, 2), (0, 1, 3, 2)
 VMEM = pl.BlockSpec(memory_space=pltpu.VMEM)
 SMEM = pl.BlockSpec(memory_space=pltpu.SMEM)
 ANY = pl.BlockSpec(memory_space=pl.ANY)
@@ -71,7 +71,7 @@
 def attend_body(
     place, assignment, counts, lambdas, norm_gain, gate, *refs, heads, head_size, patch
 ):
-    text, vision, payload, grad_vision = (refs[i * PARTS : (i + 1) * PARTS] for i in range(4))
+    text, vision, grad_text, grad_vision = (refs[i * PARTS : (i + 1) * PARTS] for i in range(4))
     vision = [vision[LATE.index(k)] for k in range(PARTS)]
     stats, gain, bias, raw_gain = refs[4 * PARTS :]
     zl, x = place[0], place[1]
@@ -185,7 +185,7 @@
             grad_query = dot(grad_scores[h, v, m], key_rows[h, v, m], (0, 0)).astype(bf16)
             own_rows = pl.ds(pl.multiple_of(place_of[v] * toks, toks), toks)
             for i in range(PARTS):
-                payload[i][own_rows, map_columns(h, m)] = grad_query[i * toks : (i + 1) * toks]
+                grad_text[i][own_rows, map_columns(h, m)] = grad_query[i * toks : (i + 1) * toks]
         for h in range(first, first + GROUP):
             for columns, parts in (
                 (map_columns(h, 0), [grad_keys[h, v, 0] for v in range(seqs)]),
@@ -210,29 +210,18 @@
 
 def sum_vision_body(place, after, *refs):
     del after
-    parts, outs, total, sems = (
-        refs[:PARTS],
-        refs[2 * PARTS : 3 * PARTS],
-        refs[3 * PARTS],
-        refs[3 * PARTS + 1],
-    )
-    rows, columns = total.shape[1] // 2, total.shape[2]
-    copies = []
-    for k in range(PARTS):
+    parts, text, outs = (refs[i * PARTS : (i + 1) * PARTS] for i in range(3))
+    for k, out in enumerate(outs):
         x = wrap(place[1] - ORDER[k])
         value = parts[0][x].astype(f32)
         for part in parts[1:]:
             value = value + part[x].astype(f32)
         value = value.astype(bf16)
-        total[k, :rows] = value[:, :columns]
-        total[k, rows:] = value[:, columns:]
-        base = outs[k].shape[0] - 2 * rows
-        copies.append(
-            pltpu.make_async_copy(total.at[k], outs[k].at[pl.ds(base, 2 * rows)], sems.at[k])
-        )
-        copies[k].start()
-    for copy in copies:
-        copy.wait()
+        text_rows, columns = text[k].shape
+        rows = value.shape[0]
+        out[:text_rows] = text[k][...]
+        out[text_rows : text_rows + rows] = value[:, :columns]
+        out[text_rows + rows :] = value[:, columns:]
 
 
 def spread_sum_body(tiles, after, out):
@@ -319,7 +308,7 @@
         functools.partial(
             attend_body, heads=heads, head_size=head_size, patch=rows // seqs
         ),
-        [shaped((seqs * toks + 2 * rows, columns // 2))] * PARTS
+        [shaped((seqs * toks, columns // 2))] * PARTS
         + [shaped(slab)] * PARTS
         + [shaped((FIRST, 4, head_size), f32)],
         [SMEM] * 3 + [VMEM] * (3 + 2 * PARTS),
@@ -371,21 +360,16 @@
         held_text,
         held_vision,
     )
-    payload, grad_vision, stats = grads[:PARTS], grads[PARTS : 2 * PARTS], grads[2 * PARTS]
-
-    back_vision = shift_all(grad_vision, "zl", range(PARTS), -1)
+    grad_text, grad_vision, stats = grads[:PARTS], grads[PARTS : 2 * PARTS], grads[2 * PARTS]
+
+    back_vision = shift_all([grad_vision[k] for k in BACK], "zl", BACK, -1)
     stats = exchange(stats, ("y", "x"))
     payload = kernel(
         sum_vision_body,
-        [shaped(payload[0].shape)] * PARTS,
-        [SMEM, ANY] + [VMEM] * PARTS + [ANY] * PARTS,
-        [ANY] * PARTS,
-        scratch_shapes=[
-            pltpu.VMEM((PARTS, 2 * rows, text_columns // PARTS), bf16),
-            pltpu.SemaphoreType.DMA((PARTS,)),
-        ],
-        input_output_aliases={2 + PARTS + k: k for k in range(PARTS)},
-    )(place, stats, *back_vision, *payload)
+        [shaped((seqs * toks + 2 * rows, text_columns // PARTS))] * PARTS,
+        [SMEM, ANY] + [VMEM] * (2 * PARTS),
+        [VMEM] * PARTS,
+    )(place, stats, *back_vision, *grad_text)
     back = shift_all(payload, "x", ORDER, -1)
     stats = kernel(spread_sum_body, shaped((SECOND, 4, head_size), f32), [VMEM, ANY], VMEM)(
         stats, payload[0]

time: 106 us -> 107 us (level)
  blocking collectives: 38.5 us -> 36.7 us
  starting transfers between devices: 51 us -> 52.4 us
  waiting for transfers between devices: 3.17 us -> 4.52 us
    all_to_all x2, blocking collectives: 38.5 us -> 36.7 us  [exchange(): return lax.all_to_all(value, axes, 0, 0, tiled=True)]
    ppermute x12, starting transfers between devices: 46.1 us -> 47.6 us  [shift_all(): lax.ppermute(part, axis, [(i, (i + way * k) % PARTS) for i in range(PARTS)])]
    ppermute x12, waiting for transfers between devices: 3.17 us -> 4.51 us  [shift_all(): lax.ppermute(part, axis, [(i, (i + way * k) % PARTS) for i in range(PARTS)])]
  transfers between devices with their start and end apart: 13 -> 13, of which waited for: 1 -> 2; matrix products, arithmetic and copies ran while one was open for 0% -> 0% of each run, Pallas kernels for 1% -> 1%
where the time goes in v10:
time: 107 us; the launch traced here: 106 us
  starting transfers between devices  52.4 us (49%)
  blocking collectives  36.7 us (34%)
  Pallas kernels  8.67 us (8%)
  waiting for transfers between devices  4.52 us (4%)
  local copies, waits for them, and re-layouts  2.29 us (2%)
  between operations  1.52 us (1%)
    ppermute x12, starting transfers between devices, shift_all(): lax.ppermute(part, axis, [(i, (i + way * k) % PARTS) for i in range(PARTS)])  47.6 us
    all_to_all x2, blocking collectives, exchange(): return lax.all_to_all(value, axes, 0, 0, tiled=True)  36.7 us
    all_to_all x1, starting transfers between devices, exchange(): return lax.all_to_all(value, axes, 0, 0, tiled=True)  4.84 us
    ppermute x12, waiting for transfers between devices, shift_all(): lax.ppermute(part, axis, [(i, (i + way * k) % PARTS) for i in range(PARTS)])  4.51 us
    pallas_call x1, Pallas kernels, attend_call(): kernel(functools.partial(attend_body, heads=heads, head_size=head_size, p...  4.06 us
    unnamed x16, local copies, waits for them, and re-layouts  2.29 us
  transfers between devices with their start and end apart: 13, of which 2 were waited for; matrix products, arithmetic and copies ran while one was open for 0% of the time, Pallas kernels for 1%

profile of v10, /device:TPU:1, one launch (start us, length us, event | category | flops | bytes accessed | tf_op | source)
XLA Modules:
  0.0 106.1 jit_solution(5115245826821162081)
XLA Ops:
  0.7 1.0 copy-done.3
  1.7 0.7 shard_map.119
  2.4 4.8 %all-to-all-start = ((bf16[4,16,2048]{2,1,0:T(8,128)(2,1)}), bf16[4,16,2048]{2,1,0:T(8,128)(2,1)S(1)}, u32[]{:S(2)}, u32[]{:S(2)}) async-start(bf16[4,16,2048]{2,1,0:T(8,128)(2,1)} %shard_map.119), calls=%async_computation | async-start | bytes 524288 | tf_op jit(solution)/shard_map/all_to_all | solution.py:298
  7.3 1.2 %copy-done.1 = bf16[2,64,4096]{2,1,0:T(8,128)(2,1)S(1)} copy-done((bf16[2,64,4096]{2,1,0:T(8,128)(2,1)S(1)}, bf16[2,64,4096]{2,1,0:T(8,128)(2,1)}, u32[]{:S(2)}) %copy-start.1) | copy-done | bytes 1048600
  9.2 4.9 %collective-permute-start = (bf16[2,64,2048]{2,1,0:T(8,128)(2,1)S(1)}, bf16[2,64,2048]{2,1,0:T(8,128)(2,1)S(1)}, u32[]{:S(2)}, u32[]{:S(2)}) collective-permute-start(bf16[2,64,2048]{2,1,0:T(8,128)(2,1)S(1)} %shard_map.121), channel_id=1, source_target_pairs={{0,2},{1,3},{2,0},{3,1},{4,6},{5,7},{6,4},{7,5},{8,10},{9,11},{10,... | collective-permute-start | bytes 1572872 | tf_op jit(solution)/shard_map/ppermute | solution.py:277
  14.1 5.8 %collective-permute-start.5 = (bf16[4,16,2048]{2,1,0:T(8,128)(2,1)S(1)}, bf16[4,16,2048]{2,1,0:T(8,128)(2,1)S(1)}, u32[]{:S(2)}, u32[]{:S(2)}) collective-permute-start(bf16[4,16,2048]{2,1,0:T(8,128)(2,1)S(1)} %all-to-all-done.refs_0_.refs_4_), channel_id=1, source_target_pairs={{0,8},{4,12},{8,0},{12,4},{1,9},{5,13},{9,1},{13,5},{2,10},{6,14},... | collective-permute-start | bytes 786440 | tf_op jit(solution)/shard_map/ppermute | solution.py:277
  20.0 0.8 shard_map.120
  20.8 2.2 %collective-permute-start.1 = (bf16[2,64,2048]{2,1,0:T(8,128)(2,1)S(1)}, bf16[2,64,2048]{2,1,0:T(8,128)(2,1)S(1)}, u32[]{:S(2)}, u32[]{:S(2)}) collective-permute-start(bf16[2,64,2048]{2,1,0:T(8,128)(2,1)S(1)} %get-tuple-element.27), channel_id=1, source_target_pairs={{0,1},{1,2},{2,3},{3,0},{4,5},{5,6},{6,7},{7,4},{8,9},{9,10},{10,1... | collective-permute-start | bytes 1572872 | tf_op jit(solution)/shard_map/ppermute | solution.py:277
  23.0 4.3 %collective-permute-start.2 = (bf16[2,64,2048]{2,1,0:T(8,128)(2,1)S(1)}, bf16[2,64,2048]{2,1,0:T(8,128)(2,1)S(1)}, u32[]{:S(2)}, u32[]{:S(2)}) collective-permute-start(bf16[2,64,2048]{2,1,0:T(8,128)(2,1)S(1)} %get-tuple-element.28), channel_id=1, source_target_pairs={{0,3},{1,0},{2,1},{3,2},{4,7},{5,4},{6,5},{7,6},{8,11},{9,8},{10,9... | collective-permute-start | bytes 1572872 | tf_op jit(solution)/shard_map/ppermute | solution.py:277
  27.3 4.0 %collective-permute-start.4 = (bf16[4,16,2048]{2,1,0:T(8,128)(2,1)S(1)}, bf16[4,16,2048]{2,1,0:T(8,128)(2,1)S(1)}, u32[]{:S(2)}, u32[]{:S(2)}) collective-permute-start(bf16[4,16,2048]{2,1,0:T(8,128)(2,1)S(1)} %all-to-all-done.refs_0_.refs_4_), channel_id=1, source_target_pairs={{0,4},{4,8},{8,12},{12,0},{1,5},{5,9},{9,13},{13,1},{2,6},{6,10},{... | collective-permute-start | bytes 786440 | tf_op jit(solution)/shard_map/ppermute | solution.py:277
  31.4 6.1 %collective-permute-start.3 = (bf16[4,16,2048]{2,1,0:T(8,128)(2,1)S(1)}, bf16[4,16,2048]{2,1,0:T(8,128)(2,1)S(1)}, u32[]{:S(2)}, u32[]{:S(2)}) collective-permute-start(bf16[4,16,2048]{2,1,0:T(8,128)(2,1)S(1)} %all-to-all-done.refs_0_.refs_4_), channel_id=1, source_target_pairs={{0,12},{4,0},{8,4},{12,8},{1,13},{5,1},{9,5},{13,9},{2,14},{6,2},{... | collective-permute-start | bytes 786440 | tf_op jit(solution)/shard_map/ppermute | solution.py:277
  38.2 3.1 %collective-permute-done.3.refs_5_ = bf16[4,16,2048]{2,1,0:T(8,128)(2,1)S(1)} collective-permute-done((bf16[4,16,2048]{2,1,0:T(8,128)(2,1)S(1)}, bf16[4,16,2048]{2,1,0:T(8,128)(2,1)S(1)}, u32[]{:S(2)}, u32[]{:S(2)}) %collective-permute-start.3) | collective-permute-done | bytes 262176 | tf_op jit(solution)/shard_map/ppermute | solution.py:277
  41.3 4.1 %shard_map.122 = (bf16[128,1024]{1,0:T(8,128)(2,1)S(1)}, bf16[128,1024]{1,0:T(8,128)(2,1)S(1)}, bf16[128,1024]{1,0:T(8,128)(2,1)S(1)}, bf16[128,1024]{1,0:T(8,12...) custom-call(s32[2]{0:T(128)S(1)} %pad_add_fusion.place, ...), custom_call_target="tpu_custom_call" | custom-call | tf_op jit(solution)/shard_map/pallas_call | solution.py:307
  45.4 5.7 %collective-permute-start.6 = (bf16[4,16,2048]{2,1,0:T(8,128)(2,1)S(1)}, bf16[4,16,2048]{2,1,0:T(8,128)(2,1)S(1)}, u32[]{:S(2)}, u32[]{:S(2)}) collective-permute-start(bf16[4,16,2048]{2,1,0:T(8,128)(2,1)S(1)} %get-tuple-element.31), channel_id=1, source_target_pairs={{0,12},{4,0},{8,4},{12,8},{1,13},{5,1},{9,5},{13,9},{2,14},{6,2},{... | collective-permute-start | bytes 786440 | tf_op jit(solution)/shard_map/ppermute | solution.py:277
  51.1 1.9 %collective-permute-start.7 = (bf16[4,16,2048]{2,1,0:T(8,128)(2,1)S(1)}, bf16[4,16,2048]{2,1,0:T(8,128)(2,1)S(1)}, u32[]{:S(2)}, u32[]{:S(2)}) collective-permute-start(bf16[4,16,2048]{2,1,0:T(8,128)(2,1)S(1)} %get-tuple-element.32), channel_id=1, source_target_pairs={{0,4},{4,8},{8,12},{12,0},{1,5},{5,9},{9,13},{13,1},{2,6},{6,10},{... | collective-permute-start | bytes 786440 | tf_op jit(solution)/shard_map/ppermute | solution.py:277
  53.0 2.2 %collective-permute-start.8 = (bf16[4,16,2048]{2,1,0:T(8,128)(2,1)S(1)}, bf16[4,16,2048]{2,1,0:T(8,128)(2,1)S(1)}, u32[]{:S(2)}, u32[]{:S(2)}) collective-permute-start(bf16[4,16,2048]{2,1,0:T(8,128)(2,1)S(1)} %get-tuple-element.33), channel_id=1, source_target_pairs={{0,8},{4,12},{8,0},{12,4},{1,9},{5,13},{9,1},{13,5},{2,10},{6,14},... | collective-permute-start | bytes 786440 | tf_op jit(solution)/shard_map/ppermute | solution.py:277
  55.2 17.9 %all_to_all.15.after.tiles = f32[32,4,128]{2,1,0:T(4,128)S(1)} all-to-all(f32[32,4,128]{2,1,0:T(4,128)S(1)} %get-tuple-element.29), channel_id=1, replica_groups=mesh['y'=8,'zh'=2,'core'=2,'zl'=4,'x'=4] {'y','x'}, dimensions={0} | all-to-all | bytes 131072 | tf_op jit(solution)/shard_map/all_to_all | solution.py:298
  73.2 1.3 %collective-permute-done.8.refs_3_ = bf16[4,16,2048]{2,1,0:T(8,128)(2,1)S(1)} collective-permute-done((bf16[4,16,2048]{2,1,0:T(8,128)(2,1)S(1)}, bf16[4,16,2048]{2,1,0:T(8,128)(2,1)S(1)}, u32[]{:S(2)}, u32[]{:S(2)}) %collective-permute-start.8) | collective-permute-done | bytes 262176 | tf_op jit(solution)/shard_map/ppermute | solution.py:277
  74.5 0.7 shard_map.123
  75.2 3.0 %collective-permute-start.9 = (bf16[160,1024]{1,0:T(8,128)(2,1)S(1)}, bf16[160,1024]{1,0:T(8,128)(2,1)S(1)}, u32[]{:S(2)}, u32[]{:S(2)}) collective-permute-start(bf16[160,1024]{1,0:T(8,128)(2,1)S(1)} %get-tuple-element.39), channel_id=1, source_target_pairs={{0,2},{1,3},{2,0},{3,1},{4,6},{5,7},{6,4},{7,5},{8,10},{9,11},{10,... | collective-permute-start | bytes 983048 | tf_op jit(solution)/shard_map/ppermute | solution.py:277
  78.2 5.5 %collective-permute-start.10 = (bf16[160,1024]{1,0:T(8,128)(2,1)S(1)}, bf16[160,1024]{1,0:T(8,128)(2,1)S(1)}, u32[]{:S(2)}, u32[]{:S(2)}) collective-permute-start(bf16[160,1024]{1,0:T(8,128)(2,1)S(1)} %get-tuple-element.40), channel_id=1, source_target_pairs={{0,3},{1,0},{2,1},{3,2},{4,7},{5,4},{6,5},{7,6},{8,11},{9,8},{10,9... | collective-permute-start | bytes 983048 | tf_op jit(solution)/shard_map/ppermute | solution.py:277
  83.8 1.9 %collective-permute-start.11 = (bf16[160,1024]{1,0:T(8,128)(2,1)S(1)}, bf16[160,1024]{1,0:T(8,128)(2,1)S(1)}, u32[]{:S(2)}, u32[]{:S(2)}) collective-permute-start(bf16[160,1024]{1,0:T(8,128)(2,1)S(1)} %get-tuple-element.41), channel_id=1, source_target_pairs={{0,1},{1,2},{2,3},{3,0},{4,5},{5,6},{6,7},{7,4},{8,9},{9,10},{10,1... | collective-permute-start | bytes 983048 | tf_op jit(solution)/shard_map/ppermute | solution.py:277
  85.7 18.7 %all_to_all.16.tiles = f32[16,4,128]{2,1,0:T(4,128)S(1)} all-to-all(f32[16,4,128]{2,1,0:T(4,128)S(1)} %shard_map.124), channel_id=1, replica_groups=mesh['y'=8,'zh'=2,'core'=2,'zl'=4,'x'=4] {'zh','core','zl'}, dimensions={0} | all-to-all | bytes 65536 | tf_op jit(solution)/shard_map/all_to_all | solution.py:298
  104.5 1.7 %shard_map.125 = (bf16[128,4096]{1,0:T(8,128)(2,1)}, bf16[16,8192]{1,0:T(8,128)(2,1)}, f32[4,16,128]{2,1,0:T(8,128)}, f32[2,128]{1,0:T(2,128)}, f32[1,1]{1,0:T(1,128)}) custom-call(s32[2]{0:T(128)S(1)} %pad_add_fusion.place, f32[16,4,128]{2,1,0:T(4,128)S(1)} %all_to_all.16.tiles, f32[4,16,128]{2,1,0:T(8,128)S(1)} %copy-done.4, f32[2,128]{1,0:T(2,128)S(1)} %bitcast.17, ...), custom_call_target="tpu_custom_call" | custom-call | tf_op jit(solution)/shard_map/pallas_call | solution.py:378
  (28 shorter events, 0.8 us)
Async XLA Ops:
  0.6 6.7 %copy-start = (bf16[2,64,4096]{2,1,0:T(8,128)(2,1)S(1)}, bf16[2,64,4096]{2,1,0:T(8,128)(2,1)}, u32[]{:S(2)}) copy-start(bf16[2,64,4096]{2,1,0:T(8,128)(2,1)} %queries.3) | copy-start | bytes 3145732
  0.6 1.0 copy-start.3
  2.4 11.7 %all-to-all-start = ((bf16[4,16,2048]{2,1,0:T(8,128)(2,1)}), bf16[4,16,2048]{2,1,0:T(8,128)(2,1)S(1)}, u32[]{:S(2)}, u32[]{:S(2)}) async-start(bf16[4,16,2048]{2,1,0:T(8,128)(2,1)} %shard_map.119), calls=%async_computation | async-start | bytes 524288 | tf_op jit(solution)/shard_map/all_to_all | solution.py:298
  7.3 1.2 %copy-start.1 = (bf16[2,64,4096]{2,1,0:T(8,128)(2,1)S(1)}, bf16[2,64,4096]{2,1,0:T(8,128)(2,1)}, u32[]{:S(2)}) copy-start(bf16[2,64,4096]{2,1,0:T(8,128)(2,1)} %cotangent.3) | copy-start | bytes 3145732
  8.5 11.4 %copy-start.2 = (bf16[2,64,4096]{2,1,0:T(8,128)(2,1)S(1)}, bf16[2,64,4096]{2,1,0:T(8,128)(2,1)}, u32[]{:S(2)}) copy-start(bf16[2,64,4096]{2,1,0:T(8,128)(2,1)} %cotangent.3) | copy-start | bytes 3145732
  8.5 11.4 %copy-start.7 = (s32[2]{0:T(128)S(1)}, s32[2]{0:T(128)}, u32[]{:S(2)}) copy-start(s32[2]{0:T(128)} %counts.1) | copy-start | bytes 28
  9.2 10.8 %copy-start.5 = (f32[256]{0:T(256)S(1)}, f32[256]{0:T(256)}, u32[]{:S(2)}) copy-start(f32[256]{0:T(256)} %param.14) | copy-start | bytes 3076
  9.2 10.8 %copy-start.6 = (s32[1,2]{1,0:T(1,128)S(1)}, s32[1,2]{1,0:T(1,128)}, u32[]{:S(2)}) copy-start(s32[1,2]{1,0:T(1,128)} %assignment.1) | copy-start | bytes 28
  9.2 32.1 %collective-permute-start = (bf16[2,64,2048]{2,1,0:T(8,128)(2,1)S(1)}, bf16[2,64,2048]{2,1,0:T(8,128)(2,1)S(1)}, u32[]{:S(2)}, u32[]{:S(2)}) collective-permute-start(bf16[2,64,2048]{2,1,0:T(8,128)(2,1)S(1)} %shard_map.121), channel_id=1, source_target_pairs={{0,2},{1,3},{2,0},{3,1},{4,6},{5,7},{6,4},{7,5},{8,10},{9,11},{10,... | collective-permute-start | bytes 1572872 | tf_op jit(solution)/shard_map/ppermute | solution.py:277
  14.1 17.2 %collective-permute-start.5 = (bf16[4,16,2048]{2,1,0:T(8,128)(2,1)S(1)}, bf16[4,16,2048]{2,1,0:T(8,128)(2,1)S(1)}, u32[]{:S(2)}, u32[]{:S(2)}) collective-permute-start(bf16[4,16,2048]{2,1,0:T(8,128)(2,1)S(1)} %all-to-all-done.refs_0_.refs_4_), channel_id=1, source_target_pairs={{0,8},{4,12},{8,0},{12,4},{1,9},{5,13},{9,1},{13,5},{2,10},{6,14},... | collective-permute-start | bytes 786440 | tf_op jit(solution)/shard_map/ppermute | solution.py:277
  20.0 21.3 %copy-start.4 = (f32[4,16,128]{2,1,0:T(8,128)S(1)}, f32[4,16,128]{2,1,0:T(8,128)}, u32[]{:S(2)}) copy-start(f32[4,16,128]{2,1,0:T(8,128)} %lambdas.3) | copy-start | bytes 98308
  20.8 20.5 %collective-permute-start.1 = (bf16[2,64,2048]{2,1,0:T(8,128)(2,1)S(1)}, bf16[2,64,2048]{2,1,0:T(8,128)(2,1)S(1)}, u32[]{:S(2)}, u32[]{:S(2)}) collective-permute-start(bf16[2,64,2048]{2,1,0:T(8,128)(2,1)S(1)} %get-tuple-element.27), channel_id=1, source_target_pairs={{0,1},{1,2},{2,3},{3,0},{4,5},{5,6},{6,7},{7,4},{8,9},{9,10},{10,1... | collective-permute-start | bytes 1572872 | tf_op jit(solution)/shard_map/ppermute | solution.py:277
  23.0 18.3 %collective-permute-start.2 = (bf16[2,64,2048]{2,1,0:T(8,128)(2,1)S(1)}, bf16[2,64,2048]{2,1,0:T(8,128)(2,1)S(1)}, u32[]{:S(2)}, u32[]{:S(2)}) collective-permute-start(bf16[2,64,2048]{2,1,0:T(8,128)(2,1)S(1)} %get-tuple-element.28), channel_id=1, source_target_pairs={{0,3},{1,0},{2,1},{3,2},{4,7},{5,4},{6,5},{7,6},{8,11},{9,8},{10,9... | collective-permute-start | bytes 1572872 | tf_op jit(solution)/shard_map/ppermute | solution.py:277
  27.3 10.8 %collective-permute-start.4 = (bf16[4,16,2048]{2,1,0:T(8,128)(2,1)S(1)}, bf16[4,16,2048]{2,1,0:T(8,128)(2,1)S(1)}, u32[]{:S(2)}, u32[]{:S(2)}) collective-permute-start(bf16[4,16,2048]{2,1,0:T(8,128)(2,1)S(1)} %all-to-all-done.refs_0_.refs_4_), channel_id=1, source_target_pairs={{0,4},{4,8},{8,12},{12,0},{1,5},{5,9},{9,13},{13,1},{2,6},{6,10},{... | collective-permute-start | bytes 786440 | tf_op jit(solution)/shard_map/ppermute | solution.py:277
  31.4 9.9 %collective-permute-start.3 = (bf16[4,16,2048]{2,1,0:T(8,128)(2,1)S(1)}, bf16[4,16,2048]{2,1,0:T(8,128)(2,1)S(1)}, u32[]{:S(2)}, u32[]{:S(2)}) collective-permute-start(bf16[4,16,2048]{2,1,0:T(8,128)(2,1)S(1)} %all-to-all-done.refs_0_.refs_4_), channel_id=1, source_target_pairs={{0,12},{4,0},{8,4},{12,8},{1,13},{5,1},{9,5},{13,9},{2,14},{6,2},{... | collective-permute-start | bytes 786440 | tf_op jit(solution)/shard_map/ppermute | solution.py:277
  45.4 27.8 %collective-permute-start.6 = (bf16[4,16,2048]{2,1,0:T(8,128)(2,1)S(1)}, bf16[4,16,2048]{2,1,0:T(8,128)(2,1)S(1)}, u32[]{:S(2)}, u32[]{:S(2)}) collective-permute-start(bf16[4,16,2048]{2,1,0:T(8,128)(2,1)S(1)} %get-tuple-element.31), channel_id=1, source_target_pairs={{0,12},{4,0},{8,4},{12,8},{1,13},{5,1},{9,5},{13,9},{2,14},{6,2},{... | collective-permute-start | bytes 786440 | tf_op jit(solution)/shard_map/ppermute | solution.py:277
  51.1 22.1 %collective-permute-start.7 = (bf16[4,16,2048]{2,1,0:T(8,128)(2,1)S(1)}, bf16[4,16,2048]{2,1,0:T(8,128)(2,1)S(1)}, u32[]{:S(2)}, u32[]{:S(2)}) collective-permute-start(bf16[4,16,2048]{2,1,0:T(8,128)(2,1)S(1)} %get-tuple-element.32), channel_id=1, source_target_pairs={{0,4},{4,8},{8,12},{12,0},{1,5},{5,9},{9,13},{13,1},{2,6},{6,10},{... | collective-permute-start | bytes 786440 | tf_op jit(solution)/shard_map/ppermute | solution.py:277
  53.0 21.5 %collective-permute-start.8 = (bf16[4,16,2048]{2,1,0:T(8,128)(2,1)S(1)}, bf16[4,16,2048]{2,1,0:T(8,128)(2,1)S(1)}, u32[]{:S(2)}, u32[]{:S(2)}) collective-permute-start(bf16[4,16,2048]{2,1,0:T(8,128)(2,1)S(1)} %get-tuple-element.33), channel_id=1, source_target_pairs={{0,8},{4,12},{8,0},{12,4},{1,9},{5,13},{9,1},{13,5},{2,10},{6,14},... | collective-permute-start | bytes 786440 | tf_op jit(solution)/shard_map/ppermute | solution.py:277
  75.2 29.2 %collective-permute-start.9 = (bf16[160,1024]{1,0:T(8,128)(2,1)S(1)}, bf16[160,1024]{1,0:T(8,128)(2,1)S(1)}, u32[]{:S(2)}, u32[]{:S(2)}) collective-permute-start(bf16[160,1024]{1,0:T(8,128)(2,1)S(1)} %get-tuple-element.39), channel_id=1, source_target_pairs={{0,2},{1,3},{2,0},{3,1},{4,6},{5,7},{6,4},{7,5},{8,10},{9,11},{10,... | collective-permute-start | bytes 983048 | tf_op jit(solution)/shard_map/ppermute | solution.py:277
  78.2 26.2 %collective-permute-start.10 = (bf16[160,1024]{1,0:T(8,128)(2,1)S(1)}, bf16[160,1024]{1,0:T(8,128)(2,1)S(1)}, u32[]{:S(2)}, u32[]{:S(2)}) collective-permute-start(bf16[160,1024]{1,0:T(8,128)(2,1)S(1)} %get-tuple-element.40), channel_id=1, source_target_pairs={{0,3},{1,0},{2,1},{3,2},{4,7},{5,4},{6,5},{7,6},{8,11},{9,8},{10,9... | collective-permute-start | bytes 983048 | tf_op jit(solution)/shard_map/ppermute | solution.py:277
  83.8 20.7 %collective-permute-start.11 = (bf16[160,1024]{1,0:T(8,128)(2,1)S(1)}, bf16[160,1024]{1,0:T(8,128)(2,1)S(1)}, u32[]{:S(2)}, u32[]{:S(2)}) collective-permute-start(bf16[160,1024]{1,0:T(8,128)(2,1)S(1)} %get-tuple-element.41), channel_id=1, source_target_pairs={{0,1},{1,2},{2,3},{3,0},{4,5},{5,6},{6,7},{7,4},{8,9},{9,10},{10,1... | collective-permute-start | bytes 983048 | tf_op jit(solution)/shard_map/ppermute | solution.py:277

commit v11 on v10

--- a/solution.py
+++ b/solution.py
@@ -14,7 +14,7 @@
 FIRST, SECOND = 32, 16
 PARTS = 4
 GROUP = 2
-ORDER, LATE, BACK = (0, 2, 1, 3), (0, 3, 1, 2), (0, 1, 3, 2)
+ORDER, LATE, BACK = (0, 2, 1, 3), (0, 3, 1, 2), (0, 1, 2, 3)
 VMEM = pl.BlockSpec(memory_space=pltpu.VMEM)
 SMEM = pl.BlockSpec(memory_space=pltpu.SMEM)
 ANY = pl.BlockSpec(memory_space=pl.ANY)

time: 107 us -> 106 us (level)
  blocking collectives: 36.7 us -> 38.5 us
  starting transfers between devices: 52.4 us -> 51 us
  waiting for transfers between devices: 4.52 us -> 3.17 us
    all_to_all x2, blocking collectives: 36.7 us -> 38.5 us  [exchange(): return lax.all_to_all(value, axes, 0, 0, tiled=True)]
    ppermute x12, starting transfers between devices: 47.6 us -> 46.1 us  [shift_all(): lax.ppermute(part, axis, [(i, (i + way * k) % PARTS) for i in range(PARTS)])]
    ppermute x12, waiting for transfers between devices: 4.51 us -> 3.17 us  [shift_all(): lax.ppermute(part, axis, [(i, (i + way * k) % PARTS) for i in range(PARTS)])]
  transfers between devices with their start and end apart: 13 -> 13, of which waited for: 2 -> 1; matrix products, arithmetic and copies ran while one was open for 0% -> 0% of each run, Pallas kernels for 1% -> 1%
where the time goes in v11:
time: 106 us; the launch traced here: 105 us
  starting transfers between devices  51 us (48%)
  blocking collectives  38.5 us (36%)
  Pallas kernels  8.68 us (8%)
  waiting for transfers between devices  3.17 us (3%)
  local copies, waits for them, and re-layouts  2.29 us (2%)
  between operations  1.52 us (1%)
    ppermute x12, starting transfers between devices, shift_all(): lax.ppermute(part, axis, [(i, (i + way * k) % PARTS) for i in range(PARTS)])  46.1 us
    all_to_all x2, blocking collectives, exchange(): return lax.all_to_all(value, axes, 0, 0, tiled=True)  38.5 us
    all_to_all x1, starting transfers between devices, exchange(): return lax.all_to_all(value, axes, 0, 0, tiled=True)  4.84 us
    pallas_call x1, Pallas kernels, attend_call(): kernel(functools.partial(attend_body, heads=heads, head_size=head_size, p...  4.06 us
    ppermute x12, waiting for transfers between devices, shift_all(): lax.ppermute(part, axis, [(i, (i + way * k) % PARTS) for i in range(PARTS)])  3.17 us
    unnamed x16, local copies, waits for them, and re-layouts  2.29 us
  transfers between devices with their start and end apart: 13, of which 1 were waited for; matrix products, arithmetic and copies ran while one was open for 0% of the time, Pallas kernels for 1%

profile of v11, /device:TPU:1, one launch (start us, length us, event | category | flops | bytes accessed | tf_op | source)
XLA Modules:
  0.0 105.2 jit_solution(3771233388337802617)
XLA Ops:
  0.7 1.0 copy-done.3
  1.7 0.7 shard_map.119
  2.4 4.8 %all-to-all-start = ((bf16[4,16,2048]{2,1,0:T(8,128)(2,1)}), bf16[4,16,2048]{2,1,0:T(8,128)(2,1)S(1)}, u32[]{:S(2)}, u32[]{:S(2)}) async-start(bf16[4,16,2048]{2,1,0:T(8,128)(2,1)} %shard_map.119), calls=%async_computation | async-start | bytes 524288 | tf_op jit(solution)/shard_map/all_to_all | solution.py:298
  7.3 1.2 %copy-done.1 = bf16[2,64,4096]{2,1,0:T(8,128)(2,1)S(1)} copy-done((bf16[2,64,4096]{2,1,0:T(8,128)(2,1)S(1)}, bf16[2,64,4096]{2,1,0:T(8,128)(2,1)}, u32[]{:S(2)}) %copy-start.1) | copy-done | bytes 1048600
  8.6 0.6 shard_map.121
  9.2 4.9 %collective-permute-start = (bf16[2,64,2048]{2,1,0:T(8,128)(2,1)S(1)}, bf16[2,64,2048]{2,1,0:T(8,128)(2,1)S(1)}, u32[]{:S(2)}, u32[]{:S(2)}) collective-permute-start(bf16[2,64,2048]{2,1,0:T(8,128)(2,1)S(1)} %shard_map.121), channel_id=1, source_target_pairs={{0,2},{1,3},{2,0},{3,1},{4,6},{5,7},{6,4},{7,5},{8,10},{9,11},{10,... | collective-permute-start | bytes 1572872 | tf_op jit(solution)/shard_map/ppermute | solution.py:277
  14.1 5.8 %collective-permute-start.5 = (bf16[4,16,2048]{2,1,0:T(8,128)(2,1)S(1)}, bf16[4,16,2048]{2,1,0:T(8,128)(2,1)S(1)}, u32[]{:S(2)}, u32[]{:S(2)}) collective-permute-start(bf16[4,16,2048]{2,1,0:T(8,128)(2,1)S(1)} %all-to-all-done.refs_0_.refs_4_), channel_id=1, source_target_pairs={{0,8},{4,12},{8,0},{12,4},{1,9},{5,13},{9,1},{13,5},{2,10},{6,14},... | collective-permute-start | bytes 786440 | tf_op jit(solution)/shard_map/ppermute | solution.py:277
  20.0 0.8 shard_map.120
  20.8 2.2 %collective-permute-start.1 = (bf16[2,64,2048]{2,1,0:T(8,128)(2,1)S(1)}, bf16[2,64,2048]{2,1,0:T(8,128)(2,1)S(1)}, u32[]{:S(2)}, u32[]{:S(2)}) collective-permute-start(bf16[2,64,2048]{2,1,0:T(8,128)(2,1)S(1)} %get-tuple-element.27), channel_id=1, source_target_pairs={{0,1},{1,2},{2,3},{3,0},{4,5},{5,6},{6,7},{7,4},{8,9},{9,10},{10,1... | collective-permute-start | bytes 1572872 | tf_op jit(solution)/shard_map/ppermute | solution.py:277
  23.0 4.3 %collective-permute-start.2 = (bf16[2,64,2048]{2,1,0:T(8,128)(2,1)S(1)}, bf16[2,64,2048]{2,1,0:T(8,128)(2,1)S(1)}, u32[]{:S(2)}, u32[]{:S(2)}) collective-permute-start(bf16[2,64,2048]{2,1,0:T(8,128)(2,1)S(1)} %get-tuple-element.28), channel_id=1, source_target_pairs={{0,3},{1,0},{2,1},{3,2},{4,7},{5,4},{6,5},{7,6},{8,11},{9,8},{10,9... | collective-permute-start | bytes 1572872 | tf_op jit(solution)/shard_map/ppermute | solution.py:277
  27.3 4.0 %collective-permute-start.4 = (bf16[4,16,2048]{2,1,0:T(8,128)(2,1)S(1)}, bf16[4,16,2048]{2,1,0:T(8,128)(2,1)S(1)}, u32[]{:S(2)}, u32[]{:S(2)}) collective-permute-start(bf16[4,16,2048]{2,1,0:T(8,128)(2,1)S(1)} %all-to-all-done.refs_0_.refs_4_), channel_id=1, source_target_pairs={{0,4},{4,8},{8,12},{12,0},{1,5},{5,9},{9,13},{13,1},{2,6},{6,10},{... | collective-permute-start | bytes 786440 | tf_op jit(solution)/shard_map/ppermute | solution.py:277
  31.4 6.1 %collective-permute-start.3 = (bf16[4,16,2048]{2,1,0:T(8,128)(2,1)S(1)}, bf16[4,16,2048]{2,1,0:T(8,128)(2,1)S(1)}, u32[]{:S(2)}, u32[]{:S(2)}) collective-permute-start(bf16[4,16,2048]{2,1,0:T(8,128)(2,1)S(1)} %all-to-all-done.refs_0_.refs_4_), channel_id=1, source_target_pairs={{0,12},{4,0},{8,4},{12,8},{1,13},{5,1},{9,5},{13,9},{2,14},{6,2},{... | collective-permute-start | bytes 786440 | tf_op jit(solution)/shard_map/ppermute | solution.py:277
  38.2 3.1 %collective-permute-done.3.refs_5_ = bf16[4,16,2048]{2,1,0:T(8,128)(2,1)S(1)} collective-permute-done((bf16[4,16,2048]{2,1,0:T(8,128)(2,1)S(1)}, bf16[4,16,2048]{2,1,0:T(8,128)(2,1)S(1)}, u32[]{:S(2)}, u32[]{:S(2)}) %collective-permute-start.3) | collective-permute-done | bytes 262176 | tf_op jit(solution)/shard_map/ppermute | solution.py:277
  41.3 4.1 %shard_map.122 = (bf16[128,1024]{1,0:T(8,128)(2,1)S(1)}, bf16[128,1024]{1,0:T(8,128)(2,1)S(1)}, bf16[128,1024]{1,0:T(8,128)(2,1)S(1)}, bf16[128,1024]{1,0:T(8,12...) custom-call(s32[2]{0:T(128)S(1)} %pad_add_fusion.place, ...), custom_call_target="tpu_custom_call" | custom-call | tf_op jit(solution)/shard_map/pallas_call | solution.py:307
  45.4 5.7 %collective-permute-start.6 = (bf16[4,16,2048]{2,1,0:T(8,128)(2,1)S(1)}, bf16[4,16,2048]{2,1,0:T(8,128)(2,1)S(1)}, u32[]{:S(2)}, u32[]{:S(2)}) collective-permute-start(bf16[4,16,2048]{2,1,0:T(8,128)(2,1)S(1)} %get-tuple-element.31), channel_id=1, source_target_pairs={{0,12},{4,0},{8,4},{12,8},{1,13},{5,1},{9,5},{13,9},{2,14},{6,2},{... | collective-permute-start | bytes 786440 | tf_op jit(solution)/shard_map/ppermute | solution.py:277
  51.1 1.9 %collective-permute-start.7 = (bf16[4,16,2048]{2,1,0:T(8,128)(2,1)S(1)}, bf16[4,16,2048]{2,1,0:T(8,128)(2,1)S(1)}, u32[]{:S(2)}, u32[]{:S(2)}) collective-permute-start(bf16[4,16,2048]{2,1,0:T(8,128)(2,1)S(1)} %get-tuple-element.32), channel_id=1, source_target_pairs={{0,8},{4,12},{8,0},{12,4},{1,9},{5,13},{9,1},{13,5},{2,10},{6,14},... | collective-permute-start | bytes 786440 | tf_op jit(solution)/shard_map/ppermute | solution.py:277
  53.0 2.2 %collective-permute-start.8 = (bf16[4,16,2048]{2,1,0:T(8,128)(2,1)S(1)}, bf16[4,16,2048]{2,1,0:T(8,128)(2,1)S(1)}, u32[]{:S(2)}, u32[]{:S(2)}) collective-permute-start(bf16[4,16,2048]{2,1,0:T(8,128)(2,1)S(1)} %get-tuple-element.33), channel_id=1, source_target_pairs={{0,4},{4,8},{8,12},{12,0},{1,5},{5,9},{9,13},{13,1},{2,6},{6,10},{... | collective-permute-start | bytes 786440 | tf_op jit(solution)/shard_map/ppermute | solution.py:277
  55.2 17.9 %all_to_all.15.after.tiles = f32[32,4,128]{2,1,0:T(4,128)S(1)} all-to-all(f32[32,4,128]{2,1,0:T(4,128)S(1)} %get-tuple-element.29), channel_id=1, replica_groups=mesh['y'=8,'zh'=2,'core'=2,'zl'=4,'x'=4] {'y','x'}, dimensions={0} | all-to-all | bytes 131072 | tf_op jit(solution)/shard_map/all_to_all | solution.py:298
  73.2 0.7 shard_map.123
  73.9 2.9 %collective-permute-start.9 = (bf16[160,1024]{1,0:T(8,128)(2,1)S(1)}, bf16[160,1024]{1,0:T(8,128)(2,1)S(1)}, u32[]{:S(2)}, u32[]{:S(2)}) collective-permute-start(bf16[160,1024]{1,0:T(8,128)(2,1)S(1)} %get-tuple-element.39), channel_id=1, source_target_pairs={{0,2},{1,3},{2,0},{3,1},{4,6},{5,7},{6,4},{7,5},{8,10},{9,11},{10,... | collective-permute-start | bytes 983048 | tf_op jit(solution)/shard_map/ppermute | solution.py:277
  76.8 4.2 %collective-permute-start.10 = (bf16[160,1024]{1,0:T(8,128)(2,1)S(1)}, bf16[160,1024]{1,0:T(8,128)(2,1)S(1)}, u32[]{:S(2)}, u32[]{:S(2)}) collective-permute-start(bf16[160,1024]{1,0:T(8,128)(2,1)S(1)} %get-tuple-element.40), channel_id=1, source_target_pairs={{0,3},{1,0},{2,1},{3,2},{4,7},{5,4},{6,5},{7,6},{8,11},{9,8},{10,9... | collective-permute-start | bytes 983048 | tf_op jit(solution)/shard_map/ppermute | solution.py:277
  81.0 1.9 %collective-permute-start.11 = (bf16[160,1024]{1,0:T(8,128)(2,1)S(1)}, bf16[160,1024]{1,0:T(8,128)(2,1)S(1)}, u32[]{:S(2)}, u32[]{:S(2)}) collective-permute-start(bf16[160,1024]{1,0:T(8,128)(2,1)S(1)} %get-tuple-element.41), channel_id=1, source_target_pairs={{0,1},{1,2},{2,3},{3,0},{4,5},{5,6},{6,7},{7,4},{8,9},{9,10},{10,1... | collective-permute-start | bytes 983048 | tf_op jit(solution)/shard_map/ppermute | solution.py:277
  83.0 20.6 %all_to_all.16.tiles = f32[16,4,128]{2,1,0:T(4,128)S(1)} all-to-all(f32[16,4,128]{2,1,0:T(4,128)S(1)} %shard_map.124), channel_id=1, replica_groups=mesh['y'=8,'zh'=2,'core'=2,'zl'=4,'x'=4] {'zh','core','zl'}, dimensions={0} | all-to-all | bytes 65536 | tf_op jit(solution)/shard_map/all_to_all | solution.py:298
  103.6 1.7 %shard_map.125 = (bf16[128,4096]{1,0:T(8,128)(2,1)}, bf16[16,8192]{1,0:T(8,128)(2,1)}, f32[4,16,128]{2,1,0:T(8,128)}, f32[2,128]{1,0:T(2,128)}, f32[1,1]{1,0:T(1,128)}) custom-call(s32[2]{0:T(128)S(1)} %pad_add_fusion.place, f32[16,4,128]{2,1,0:T(4,128)S(1)} %all_to_all.16.tiles, f32[4,16,128]{2,1,0:T(8,128)S(1)} %copy-done.4, f32[2,128]{1,0:T(2,128)S(1)} %bitcast.17, ...), custom_call_target="tpu_custom_call" | custom-call | tf_op jit(solution)/shard_map/pallas_call | solution.py:378
  (28 shorter events, 0.2 us)
Async XLA Ops:
  0.6 6.7 %copy-start = (bf16[2,64,4096]{2,1,0:T(8,128)(2,1)S(1)}, bf16[2,64,4096]{2,1,0:T(8,128)(2,1)}, u32[]{:S(2)}) copy-start(bf16[2,64,4096]{2,1,0:T(8,128)(2,1)} %queries.3) | copy-start | bytes 3145732
  0.6 1.0 copy-start.3
  2.4 11.7 %all-to-all-start = ((bf16[4,16,2048]{2,1,0:T(8,128)(2,1)}), bf16[4,16,2048]{2,1,0:T(8,128)(2,1)S(1)}, u32[]{:S(2)}, u32[]{:S(2)}) async-start(bf16[4,16,2048]{2,1,0:T(8,128)(2,1)} %shard_map.119), calls=%async_computation | async-start | bytes 524288 | tf_op jit(solution)/shard_map/all_to_all | solution.py:298
  7.3 1.2 %copy-start.1 = (bf16[2,64,4096]{2,1,0:T(8,128)(2,1)S(1)}, bf16[2,64,4096]{2,1,0:T(8,128)(2,1)}, u32[]{:S(2)}) copy-start(bf16[2,64,4096]{2,1,0:T(8,128)(2,1)} %cotangent.3) | copy-start | bytes 3145732
  8.5 11.4 %copy-start.2 = (bf16[2,64,4096]{2,1,0:T(8,128)(2,1)S(1)}, bf16[2,64,4096]{2,1,0:T(8,128)(2,1)}, u32[]{:S(2)}) copy-start(bf16[2,64,4096]{2,1,0:T(8,128)(2,1)} %cotangent.3) | copy-start | bytes 3145732
  8.5 11.4 %copy-start.7 = (s32[2]{0:T(128)S(1)}, s32[2]{0:T(128)}, u32[]{:S(2)}) copy-start(s32[2]{0:T(128)} %counts.1) | copy-start | bytes 28
  9.2 10.8 %copy-start.5 = (f32[256]{0:T(256)S(1)}, f32[256]{0:T(256)}, u32[]{:S(2)}) copy-start(f32[256]{0:T(256)} %param.14) | copy-start | bytes 3076
  9.2 10.8 %copy-start.6 = (s32[1,2]{1,0:T(1,128)S(1)}, s32[1,2]{1,0:T(1,128)}, u32[]{:S(2)}) copy-start(s32[1,2]{1,0:T(1,128)} %assignment.1) | copy-start | bytes 28
  9.2 32.1 %collective-permute-start = (bf16[2,64,2048]{2,1,0:T(8,128)(2,1)S(1)}, bf16[2,64,2048]{2,1,0:T(8,128)(2,1)S(1)}, u32[]{:S(2)}, u32[]{:S(2)}) collective-permute-start(bf16[2,64,2048]{2,1,0:T(8,128)(2,1)S(1)} %shard_map.121), channel_id=1, source_target_pairs={{0,2},{1,3},{2,0},{3,1},{4,6},{5,7},{6,4},{7,5},{8,10},{9,11},{10,... | collective-permute-start | bytes 1572872 | tf_op jit(solution)/shard_map/ppermute | solution.py:277
  14.1 17.2 %collective-permute-start.5 = (bf16[4,16,2048]{2,1,0:T(8,128)(2,1)S(1)}, bf16[4,16,2048]{2,1,0:T(8,128)(2,1)S(1)}, u32[]{:S(2)}, u32[]{:S(2)}) collective-permute-start(bf16[4,16,2048]{2,1,0:T(8,128)(2,1)S(1)} %all-to-all-done.refs_0_.refs_4_), channel_id=1, source_target_pairs={{0,8},{4,12},{8,0},{12,4},{1,9},{5,13},{9,1},{13,5},{2,10},{6,14},... | collective-permute-start | bytes 786440 | tf_op jit(solution)/shard_map/ppermute | solution.py:277
  20.0 21.3 %copy-start.4 = (f32[4,16,128]{2,1,0:T(8,128)S(1)}, f32[4,16,128]{2,1,0:T(8,128)}, u32[]{:S(2)}) copy-start(f32[4,16,128]{2,1,0:T(8,128)} %lambdas.3) | copy-start | bytes 98308
  20.8 20.5 %collective-permute-start.1 = (bf16[2,64,2048]{2,1,0:T(8,128)(2,1)S(1)}, bf16[2,64,2048]{2,1,0:T(8,128)(2,1)S(1)}, u32[]{:S(2)}, u32[]{:S(2)}) collective-permute-start(bf16[2,64,2048]{2,1,0:T(8,128)(2,1)S(1)} %get-tuple-element.27), channel_id=1, source_target_pairs={{0,1},{1,2},{2,3},{3,0},{4,5},{5,6},{6,7},{7,4},{8,9},{9,10},{10,1... | collective-permute-start | bytes 1572872 | tf_op jit(solution)/shard_map/ppermute | solution.py:277
  23.0 18.3 %collective-permute-start.2 = (bf16[2,64,2048]{2,1,0:T(8,128)(2,1)S(1)}, bf16[2,64,2048]{2,1,0:T(8,128)(2,1)S(1)}, u32[]{:S(2)}, u32[]{:S(2)}) collective-permute-start(bf16[2,64,2048]{2,1,0:T(8,128)(2,1)S(1)} %get-tuple-element.28), channel_id=1, source_target_pairs={{0,3},{1,0},{2,1},{3,2},{4,7},{5,4},{6,5},{7,6},{8,11},{9,8},{10,9... | collective-permute-start | bytes 1572872 | tf_op jit(solution)/shard_map/ppermute | solution.py:277
  27.3 10.8 %collective-permute-start.4 = (bf16[4,16,2048]{2,1,0:T(8,128)(2,1)S(1)}, bf16[4,16,2048]{2,1,0:T(8,128)(2,1)S(1)}, u32[]{:S(2)}, u32[]{:S(2)}) collective-permute-start(bf16[4,16,2048]{2,1,0:T(8,128)(2,1)S(1)} %all-to-all-done.refs_0_.refs_4_), channel_id=1, source_target_pairs={{0,4},{4,8},{8,12},{12,0},{1,5},{5,9},{9,13},{13,1},{2,6},{6,10},{... | collective-permute-start | bytes 786440 | tf_op jit(solution)/shard_map/ppermute | solution.py:277
  31.4 9.9 %collective-permute-start.3 = (bf16[4,16,2048]{2,1,0:T(8,128)(2,1)S(1)}, bf16[4,16,2048]{2,1,0:T(8,128)(2,1)S(1)}, u32[]{:S(2)}, u32[]{:S(2)}) collective-permute-start(bf16[4,16,2048]{2,1,0:T(8,128)(2,1)S(1)} %all-to-all-done.refs_0_.refs_4_), channel_id=1, source_target_pairs={{0,12},{4,0},{8,4},{12,8},{1,13},{5,1},{9,5},{13,9},{2,14},{6,2},{... | collective-permute-start | bytes 786440 | tf_op jit(solution)/shard_map/ppermute | solution.py:277
  45.4 27.8 %collective-permute-start.6 = (bf16[4,16,2048]{2,1,0:T(8,128)(2,1)S(1)}, bf16[4,16,2048]{2,1,0:T(8,128)(2,1)S(1)}, u32[]{:S(2)}, u32[]{:S(2)}) collective-permute-start(bf16[4,16,2048]{2,1,0:T(8,128)(2,1)S(1)} %get-tuple-element.31), channel_id=1, source_target_pairs={{0,12},{4,0},{8,4},{12,8},{1,13},{5,1},{9,5},{13,9},{2,14},{6,2},{... | collective-permute-start | bytes 786440 | tf_op jit(solution)/shard_map/ppermute | solution.py:277
  51.1 22.1 %collective-permute-start.7 = (bf16[4,16,2048]{2,1,0:T(8,128)(2,1)S(1)}, bf16[4,16,2048]{2,1,0:T(8,128)(2,1)S(1)}, u32[]{:S(2)}, u32[]{:S(2)}) collective-permute-start(bf16[4,16,2048]{2,1,0:T(8,128)(2,1)S(1)} %get-tuple-element.32), channel_id=1, source_target_pairs={{0,8},{4,12},{8,0},{12,4},{1,9},{5,13},{9,1},{13,5},{2,10},{6,14},... | collective-permute-start | bytes 786440 | tf_op jit(solution)/shard_map/ppermute | solution.py:277
  53.0 20.1 %collective-permute-start.8 = (bf16[4,16,2048]{2,1,0:T(8,128)(2,1)S(1)}, bf16[4,16,2048]{2,1,0:T(8,128)(2,1)S(1)}, u32[]{:S(2)}, u32[]{:S(2)}) collective-permute-start(bf16[4,16,2048]{2,1,0:T(8,128)(2,1)S(1)} %get-tuple-element.33), channel_id=1, source_target_pairs={{0,4},{4,8},{8,12},{12,0},{1,5},{5,9},{9,13},{13,1},{2,6},{6,10},{... | collective-permute-start | bytes 786440 | tf_op jit(solution)/shard_map/ppermute | solution.py:277
  73.9 29.7 %collective-permute-start.9 = (bf16[160,1024]{1,0:T(8,128)(2,1)S(1)}, bf16[160,1024]{1,0:T(8,128)(2,1)S(1)}, u32[]{:S(2)}, u32[]{:S(2)}) collective-permute-start(bf16[160,1024]{1,0:T(8,128)(2,1)S(1)} %get-tuple-element.39), channel_id=1, source_target_pairs={{0,2},{1,3},{2,0},{3,1},{4,6},{5,7},{6,4},{7,5},{8,10},{9,11},{10,... | collective-permute-start | bytes 983048 | tf_op jit(solution)/shard_map/ppermute | solution.py:277
  76.8 26.8 %collective-permute-start.10 = (bf16[160,1024]{1,0:T(8,128)(2,1)S(1)}, bf16[160,1024]{1,0:T(8,128)(2,1)S(1)}, u32[]{:S(2)}, u32[]{:S(2)}) collective-permute-start(bf16[160,1024]{1,0:T(8,128)(2,1)S(1)} %get-tuple-element.40), channel_id=1, source_target_pairs={{0,3},{1,0},{2,1},{3,2},{4,7},{5,4},{6,5},{7,6},{8,11},{9,8},{10,9... | collective-permute-start | bytes 983048 | tf_op jit(solution)/shard_map/ppermute | solution.py:277
  81.0 22.6 %collective-permute-start.11 = (bf16[160,1024]{1,0:T(8,128)(2,1)S(1)}, bf16[160,1024]{1,0:T(8,128)(2,1)S(1)}, u32[]{:S(2)}, u32[]{:S(2)}) collective-permute-start(bf16[160,1024]{1,0:T(8,128)(2,1)S(1)} %get-tuple-element.41), channel_id=1, source_target_pairs={{0,1},{1,2},{2,3},{3,0},{4,5},{5,6},{6,7},{7,4},{8,9},{9,10},{10,1... | collective-permute-start | bytes 983048 | tf_op jit(solution)/shard_map/ppermute | solution.py:277
